TPU v7x, 32 devices: a whole 2x2x4 slice. The times are simulated.
32 devices in a mesh: parts: 2 (over x), blk: 2 (over core), rows: 8 (over z, y).
Axes of the slice: x: 2, y: 2, z: 4, core: 2. Of those that a mesh axis runs over, the one named last changes fastest.
Arguments:
- wave: bfloat16 [2, 1024, 128, 128], P('blk', ('parts', 'rows')), parts along dimension 1, may hold values from -6 to 6
- left_env: bfloat16 [256, 10, 128, 128], P(('parts', 'rows'), 'blk'), parts along dimension 0, may hold values from -0.5 to 0.5
- right_env: bfloat16 [256, 10, 128, 128], P(('parts', 'rows'), 'blk'), parts along dimension 0, may hold values from -0.25 to 0.25
- right_slot: int32 [1024], P('parts'), parts along dimension 0, may hold values from 0 to 511, as said below
- term_mask: int32 [256, 10], P(('parts', 'rows')), parts along dimension 0, may hold values from 0 to 1, as said below
Outputs:
- applied: bfloat16 [2, 1024, 128, 128], P('blk', ('parts', 'rows')), parts along dimension 1
There are 2 independent parts, one for each index of `parts`. A program takes and returns all parts, laid end to end along the dimension named above; each array names one. Nothing has to cross between parts.
Inputs may be any that keep to these rules, and one draw needn't show every extreme that they name: right_slot is a permutation of the blocks; block b lies on index b // 64 of rows and goes to index right_slot[b] // 64; every index of rows receives 4 * 16 blocks, sends at most 8 of them to any one index, and sends exactly 8 to some. `term_mask`: every row holds exactly 5 ones.
All inputs are finite; a program needn't handle non-finite values.
Results may differ from a plain program's by a relative error of at most 0.0049.
Values may be sent and summed in bfloat16 or wider, within the bound.
No kernel may reach another device: no remote copies, remote signals or barrier semaphores. Data moves between devices by JAX's collectives and lax.ppermute only.
A program may use at most 192 MiB of HBM per device.

v0:
```python
import jax
import jax.numpy as jnp
from jax import lax
from jax.sharding import PartitionSpec as P

WACT = 5


def body(wave, left_env, right_env, right_slot, term_mask):
    blocks = wave.shape[1]
    state_width = wave.shape[3]
    sectors = left_env.shape[0]
    fan_out = blocks // sectors
    devices = lax.axis_size("rows")
    capacity = (blocks + devices - 1) // devices
    slot_count = devices * capacity
    grouped = wave[0].reshape(sectors, fan_out, state_width, state_width)
    terms = jnp.einsum(
        "skab,stbc->stkac",
        lax.all_gather(left_env, "blk", axis=1, tiled=True),
        grouped,
        preferred_element_type=jnp.float32,
    )
    product = terms.astype(jnp.bfloat16)
    components = product.shape[2]
    product = product.reshape(blocks, components, state_width, state_width)
    my_slots = lax.dynamic_slice_in_dim(right_slot, lax.axis_index("rows") * blocks, blocks)
    target = my_slots // blocks
    local_tag = my_slots % blocks
    block_order = jnp.arange(blocks, dtype=jnp.int32)
    earlier = (target[None, :] == target[:, None]) & (block_order[None, :] < block_order[:, None])
    send_rank = jnp.sum(earlier.astype(jnp.int32), axis=1)
    position = target * capacity + send_rank
    matches = position[None, :] == jnp.arange(slot_count, dtype=jnp.int32)[:, None]
    filled = jnp.any(matches, axis=1)
    source = jnp.argmax(matches, axis=1)
    send_tags = jnp.where(filled, local_tag[source], -1)
    running = jnp.cumsum(term_mask, axis=1) - 1
    chosen = (term_mask[:, :, None] == 1) & (
        running[:, :, None] == jnp.arange(WACT, dtype=jnp.int32)[None, None, :]
    )
    picked = jnp.sum(
        chosen.astype(jnp.int32) * jnp.arange(components, dtype=jnp.int32)[None, :, None], axis=1
    )
    comp_labels = jnp.repeat(picked, fan_out, axis=0)
    payload = jnp.take_along_axis(product, comp_labels[:, :, None, None], axis=1)
    weights = jnp.ones_like(comp_labels)
    send_data = jnp.where(filled[:, None, None, None], payload[source], jnp.zeros((), jnp.bfloat16))
    send_labels = comp_labels[source]
    send_weights = jnp.where(filled[:, None], weights[source], 0)
    received = (
        lax.all_to_all(send_data, "rows", split_axis=0, concat_axis=0, tiled=True),
        lax.all_to_all(send_labels, "rows", split_axis=0, concat_axis=0, tiled=True),
        lax.all_to_all(send_weights, "rows", split_axis=0, concat_axis=0, tiled=True),
        lax.all_to_all(send_tags, "rows", split_axis=0, concat_axis=0, tiled=True),
    )
    recv_data, recv_labels, recv_weights, recv_tags = received
    wanted = recv_tags[None, :] == block_order[:, None]
    pick_index = jnp.argmax(wanted, axis=1)
    ordered = recv_data[pick_index]
    selector = (
        recv_labels[pick_index][:, :, None]
        == jnp.arange(components, dtype=jnp.int32)[None, None, :]
    )
    selector = (selector.astype(jnp.int32) * recv_weights[pick_index][:, :, None]).astype(
        jnp.bfloat16
    )
    spread = jnp.einsum(
        "bmk,bmac->bkac", selector, ordered, preferred_element_type=jnp.float32
    ).astype(jnp.bfloat16)
    spread = spread.reshape(sectors, fan_out, components, state_width, state_width)
    right_full = lax.all_gather(right_env, "blk", axis=1, tiled=True)
    applied = jnp.einsum("stkac,skdc->stad", spread, right_full, preferred_element_type=jnp.float32)
    applied = applied.reshape(blocks, state_width, state_width).astype(jnp.bfloat16)
    valid = recv_tags >= 0
    back_rows = jnp.where(
        valid[:, None, None], applied[jnp.maximum(recv_tags, 0)], jnp.zeros((), jnp.bfloat16)
    )
    returned = lax.all_to_all(back_rows, "rows", split_axis=0, concat_axis=0, tiled=True)
    return returned[position][None]


def solution(mesh):
    in_specs = (
        P("blk", ("parts", "rows"), None, None),
        P(("parts", "rows"), "blk", None, None),
        P(("parts", "rows"), "blk", None, None),
        P("parts"),
        P(("parts", "rows"), None),
    )
    out_specs = P("blk", ("parts", "rows"), None, None)
    return jax.shard_map(body, mesh=mesh, in_specs=in_specs, out_specs=out_specs, check_vma=False)
```

profile of v0, /device:TPU:0, one launch (start us, length us, event | category | flops | bytes accessed | tf_op | source)
XLA Modules:
  0.0 469.1 jit_solution(4067337263441447913)
XLA Ops:
  7.3 0.8 and_select_fusion
  9.6 0.8 gather_fusion
  11.2 7.3 %all-to-all-start = ((s32[8,8,1]{1,2,0:T(1,128)}), s32[8,8,1]{1,2,0:T(1,128)S(1)}, u32[]{:S(2)}, u32[]{:S(2)}) async-start(s32[8,8,1]{1,2,0:T(1,128)} %bitcast), calls=%async_computation | async-start | bytes 8192 | tf_op jit(solution)/shard_map/all_to_all | solution.py:55
  18.6 0.9 reduce_window_sum.11
  21.2 1.2 gather_fusion.1
  23.1 3.8 all-gather.3.cloned.1.call-done
  26.9 12.5 %convolution_convert_fusion.1 = bf16[16,4,128,10,128]{4,2,3,1,0:T(8,128)(2,1)} fusion(bf16[16,4,128,128,1]{3,2,4,1,0:T(8,128)(2,1)S(1)} %bitcast.44, bf16[16,10,128,128]{3,2,1,0:T(8,128)(2,1)} %all-gather.3.cloned.1.call-done), kind=kOutput, calls=%fused_computation.14 | convolution fusion | flops 2694840320 | bytes 28311552 | tf_op jit(solution)/shard_map/skab,stbc->stkac/dot_general | solution.py:18
  39.4 22.8 %gather_fusion.9 = bf16[320,128,128]{1,2,0:T(8,128)(2,1)} fusion(bf16[64,10,128,128]{2,3,1,0:T(8,128)(2,1)} %bitcast.45, s32[320]{0:T(512)S(1)} %reshape.217), kind=kCustom, calls=%fused_computation.9 | custom fusion | bytes 20974080 | tf_op jit(solution)/shard_map/jit(take_along_axis)/gather | solution.py:46
  62.1 14.4 %copy.23 = bf16[320,128,128]{2,1,0:T(8,128)(2,1)} copy(bf16[320,128,128]{1,2,0:T(8,128)(2,1)} %gather_fusion.9) | data formatting | bytes 20971520 | tf_op jit(solution)/shard_map/jit(take_along_axis)/gather | solution.py:46
  76.5 5.8 %all-to-all-start.2 = ((s32[8,8,5]{2,1,0:T(8,128)}), s32[8,8,5]{2,1,0:T(8,128)S(1)}, u32[]{:S(2)}, u32[]{:S(2)}) async-start(s32[8,8,5]{2,1,0:T(8,128)} %bitcast_select_fusion), calls=%async_computation.2 | async-start | bytes 65536 | tf_op jit(solution)/shard_map/all_to_all | solution.py:54
  82.3 10.1 %broadcast_select_fusion.1 = bf16[64,5,128,128]{3,2,1,0:T(8,128)(2,1)} fusion(bf16[64,5,128,128]{3,2,1,0:T(8,128)(2,1)} %bitcast.47, pred[64,5]{1,0:T(8,128)(4,1)S(1)} %compare_and_fusion), kind=kLoop, calls=%fused_computation.16 | loop fusion | flops 5242880 | bytes 20971840 | tf_op jit(solution)/shard_map/jit(take_along_axis)/select_n | solution.py:46
  92.4 10.5 %gather_fusion.5 = bf16[64,5,128,128]{3,2,1,0:T(8,128)(2,1)} fusion(bf16[64,5,128,128]{3,2,1,0:T(8,128)(2,1)} %broadcast_select_fusion.1, s32[1024]{0:T(1024)S(1)} %pad_clamp_fusion.3), kind=kCustom, calls=%fused_computation.5 | custom fusion | bytes 20971776 | tf_op jit(solution)/shard_map/gather | solution.py:48
  102.9 6.0 %all-to-all-start.1 = ((s32[8,8,5]{2,1,0:T(8,128)}), s32[8,8,5]{2,1,0:T(8,128)S(1)}, u32[]{:S(2)}, u32[]{:S(2)}) async-start(s32[8,8,5]{2,1,0:T(8,128)} %bitcast.2), calls=%async_computation.1 | async-start | bytes 65536 | tf_op jit(solution)/shard_map/all_to_all | solution.py:53
  108.9 9.9 %broadcast_select_fusion = bf16[64,5,128,128]{3,2,1,0:T(8,128)(2,1)} fusion(bf16[64,5,128,128]{3,2,1,0:T(8,128)(2,1)} %gather_fusion.5, pred[64]{0:T(512)(128)(4,1)S(1)} %fusion.18), kind=kLoop, calls=%fused_computation.15 | loop fusion | flops 5242880 | bytes 20971584 | tf_op jit(solution)/shard_map/jit(_where)/select_n | solution.py:48
  118.8 6.0 %all-to-all-start.3 = ((bf16[64,5,128,128]{3,2,1,0:T(8,128)(2,1)}), bf16[64,5,128,128]{3,2,1,0:T(8,128)(2,1)}, u32[]{:S(2)}, u32[]{:S(2)}) async-start(bf16[64,5,128,128]{3,2,1,0:T(8,128)(2,1)} %broadcast_select_fusion), calls=%async_computation.3 | async-start | bytes 20971520 | tf_op jit(solution)/shard_map/all_to_all | solution.py:52
  128.8 223.5 %all-to-all-done.3 = bf16[64,5,128,128]{3,2,1,0:T(8,128)(2,1)} async-done(((bf16[64,5,128,128]{3,2,1,0:T(8,128)(2,1)}), bf16[64,5,128,128]{3,2,1,0:T(8,128)(2,1)}, u32[]{:S(2)}, u32[]{:S(2)}) %all-to-all-start.3) | async-done | bytes 10485792 | tf_op jit(solution)/shard_map/all_to_all | solution.py:52
  352.2 10.5 %gather_fusion.6 = bf16[64,5,128,128]{3,2,1,0:T(8,128)(2,1)} fusion(bf16[64,5,128,128]{3,2,1,0:T(8,128)(2,1)} %all-to-all-done.3, s32[1024]{0:T(1024)S(1)} %pad_clamp_fusion.2), kind=kCustom, calls=%fused_computation.6 | custom fusion | bytes 20971776 | tf_op jit(solution)/shard_map/gather | solution.py:60
  362.8 19.0 %convolution_convert_fusion = bf16[64,10,128,128]{3,1,2,0:T(8,128)(2,1)} fusion(bf16[64,5,128,128]{3,2,1,0:T(8,128)(2,1)} %gather_fusion.6, s32[64,5]{1,0:T(8,128)S(1)} %gather_fusion.4, s32[64,5]{1,0:T(8,128)S(1)} %gather_fusion.2), kind=kOutput, calls=%fused_computation.12 | convolution fusion | flops 115352960 | bytes 31459840 | tf_op jit(solution)/shard_map/bmk,bmac->bkac/dot_general | solution.py:68
  381.7 17.8 %bitcast_convert_fusion = bf16[16,4,128,128]{3,2,1,0:T(8,128)(2,1)} fusion(bf16[16,10,128,128]{3,2,1,0:T(8,128)(2,1)} %all-gather.5.cloned.1.call-done, bf16[16,4,10,128,128]{4,2,3,1,0:T(8,128)(2,1)} %bitcast.46), kind=kOutput, calls=%fused_computation.19 | convolution fusion | flops 2685403136 | bytes 28311552 | tf_op jit(solution)/shard_map/stkac,skdc->stad/dot_general | solution.py:73
  399.5 3.8 gather_fusion.7
  403.2 3.1 broadcast_select_fusion.2
  406.4 4.3 all-to-all-start.4
  410.7 47.8 %all-to-all-done.4 = bf16[64,128,128]{2,1,0:T(8,128)(2,1)} async-done(((bf16[64,128,128]{2,1,0:T(8,128)(2,1)}), bf16[64,128,128]{2,1,0:T(8,128)(2,1)}, u32[]{:S(2)}, u32[]{:S(2)}) %all-to-all-start.4) | async-done | bytes 2097184 | tf_op jit(solution)/shard_map/all_to_all | solution.py:79
  458.5 3.7 gather_fusion.8
  (45 shorter events, 9.6 us)
Async XLA Ops:
  6.5 20.3 %copy-start = (bf16[1,64,128,128]{3,2,1,0:T(8,128)(2,1)S(1)}, bf16[1,64,128,128]{3,2,1,0:T(8,128)(2,1)}, u32[]{:S(2)}) copy-start(bf16[1,64,128,128]{3,2,1,0:T(8,128)(2,1)} %param.5) | copy-start | bytes 6291460
  6.5 20.3 %all-gather.3.cloned.1.call-start = ((), (), s32[]{:S(2)}) async-start(), calls=%async_computation.5 | async-start | bytes 7864320 | tf_op jit(solution)/shard_map/all_gather | solution.py:20
  11.2 65.3 %all-to-all-start = ((s32[8,8,1]{1,2,0:T(1,128)}), s32[8,8,1]{1,2,0:T(1,128)S(1)}, u32[]{:S(2)}, u32[]{:S(2)}) async-start(s32[8,8,1]{1,2,0:T(1,128)} %bitcast), calls=%async_computation | async-start | bytes 8192 | tf_op jit(solution)/shard_map/all_to_all | solution.py:55
  76.5 26.4 %all-to-all-start.2 = ((s32[8,8,5]{2,1,0:T(8,128)}), s32[8,8,5]{2,1,0:T(8,128)S(1)}, u32[]{:S(2)}, u32[]{:S(2)}) async-start(s32[8,8,5]{2,1,0:T(8,128)} %bitcast_select_fusion), calls=%async_computation.2 | async-start | bytes 65536 | tf_op jit(solution)/shard_map/all_to_all | solution.py:54
  102.9 15.9 %all-to-all-start.1 = ((s32[8,8,5]{2,1,0:T(8,128)}), s32[8,8,5]{2,1,0:T(8,128)S(1)}, u32[]{:S(2)}, u32[]{:S(2)}) async-start(s32[8,8,5]{2,1,0:T(8,128)} %bitcast.2), calls=%async_computation.1 | async-start | bytes 65536 | tf_op jit(solution)/shard_map/all_to_all | solution.py:53
  118.8 233.4 %all-to-all-start.3 = ((bf16[64,5,128,128]{3,2,1,0:T(8,128)(2,1)}), bf16[64,5,128,128]{3,2,1,0:T(8,128)(2,1)}, u32[]{:S(2)}, u32[]{:S(2)}) async-start(bf16[64,5,128,128]{3,2,1,0:T(8,128)(2,1)} %broadcast_select_fusion), calls=%async_computation.3 | async-start | bytes 20971520 | tf_op jit(solution)/shard_map/all_to_all | solution.py:52
  124.8 256.9 %all-gather.5.cloned.1.call-start = ((), (), s32[]{:S(2)}) async-start(), calls=%async_computation.6 | async-start | bytes 7864320 | tf_op jit(solution)/shard_map/all_gather | solution.py:72
  381.7 80.5 %copy-start.1 = (bf16[1,64,128,128]{3,2,1,0:T(8,128)(2,1)S(1)}, bf16[1,64,128,128]{3,2,1,0:T(8,128)(2,1)}, u32[]{:S(2)}) copy-start(bf16[1,64,128,128]{3,2,1,0:T(8,128)(2,1)} %param.5) | copy-start | bytes 6291460
  406.4 52.2 %all-to-all-start.4 = ((bf16[64,128,128]{2,1,0:T(8,128)(2,1)}), bf16[64,128,128]{2,1,0:T(8,128)(2,1)}, u32[]{:S(2)}, u32[]{:S(2)}) async-start(bf16[64,128,128]{2,1,0:T(8,128)(2,1)} %broadcast_select_fusion.2), calls=%async_computation.4 | async-start | bytes 4194304 | tf_op jit(solution)/shard_map/all_to_all | solution.py:79
Sparse Core Ops, SparseCore 0:
  8.9 17.9 all-gather.2
  127.2 16.5 all-gather.4
where the time goes:
time: 470 us; the launch traced here: 469 us
  waiting for transfers between devices  276 us (59%)
  local copies, waits for them, and re-layouts  71 us (15%)
  matrix products  49.2 us (10%)
  starting transfers between devices  29.6 us (6%)
  other arithmetic  29.4 us (6%)
  between operations  13.5 us (3%)
    all_to_all x1, waiting for transfers between devices, body(): lax.all_to_all(send_data, 'rows', split_axis=0, concat_axis=0, tiled=True)  223 us
    all_to_all x1, waiting for transfers between devices, body(): lax.all_to_all(back_rows, 'rows', split_axis=0, concat_axis=0, tiled=True)  47.8 us
    gather x3, local copies, waits for them, and re-layouts, body(): jnp.take_along_axis(product, comp_labels[:, :, None, None], axis=1)  37.3 us
    dot_general x1, matrix products, body(): jnp.einsum('bmk,bmac->bkac', selector, ordered, preferred_element_type=jn...  19 us
    dot_general x1, matrix products, body(): jnp.einsum('stkac,skdc->stad', spread, right_full, preferred_element_type...  17.8 us
    dot_general x1, matrix products, body(): jnp.einsum('skab,stbc->stkac', lax.all_gather(left_env, 'blk', axis=1, ti...  12.5 us
    gather x1, local copies, waits for them, and re-layouts, body(): payload[source]  10.5 us
    gather x1, local copies, waits for them, and re-layouts, body(): ordered = recv_data[pick_index]  10.5 us
  transfers between devices with their start and end apart: 7, of which 3 were waited for; matrix products, arithmetic and copies ran while one was open for 26% of the time, Pallas kernels for 0%

commit v1 on v0

v1 whole, which is shorter than its diff:
```python
import functools

import jax
import jax.numpy as jnp
from jax import lax
from jax.experimental import pallas as pl
from jax.experimental.pallas import tpu as pltpu
from jax.sharding import PartitionSpec as P

WACT = 5
VMEM = 48 * 1024 * 1024


def smem():
    return pl.BlockSpec(memory_space=pltpu.SMEM)


def hbm():
    return pl.BlockSpec(memory_space=pl.ANY)


class Plan:
    def __init__(self, wave, left_env, devices, cores):
        self.blocks, self.width = wave.shape[1], wave.shape[3]
        self.sectors, self.half = left_env.shape[0], left_env.shape[1]
        self.fan = self.blocks // self.sectors
        self.devices = devices
        self.cap = self.blocks // devices
        self.split = cores == 2 and self.cap % 2 == 0
        self.capc = self.cap // 2 if self.split else self.cap
        self.vectors = 2 if self.split else 1
        self.by_pairs = devices == 8
        if self.by_pairs:
            self.groups = [(4,), (5,), (6,), (7,), (2,), (3,), (1,), (0,)]
        else:
            self.groups = [tuple(range(devices))]

    def partner(self, p):
        return jnp.bitwise_xor(lax.axis_index("rows"), p) if self.by_pairs else jnp.int32(p)

    def rank0(self, core):
        return core * self.capc if self.split else 0


def lists(plan, right_slot):
    devices, blocks, cap, fan, sectors = plan.devices, plan.blocks, plan.cap, plan.fan, plan.sectors
    me = lax.axis_index("rows")
    slots = right_slot.reshape(devices, blocks)
    target = slots // blocks
    index = jnp.arange(blocks, dtype=jnp.int32)
    earlier = (target[:, None, :] == target[:, :, None]) & (index[None, None, :] < index[None, :, None])
    rank = jnp.sum(earlier.astype(jnp.int32), axis=2)
    ranks = jnp.arange(cap, dtype=jnp.int32)
    device = jnp.arange(devices, dtype=jnp.int32)
    value = (device[:, None] * sectors + index[None, :] // fan) * sectors + (slots % blocks) // fan
    hit = (target[:, None, :] == me) & (rank[:, None, :] == ranks[None, :, None])
    code = jnp.sum(jnp.where(hit, value[:, None, :], 0), axis=2)
    my_target = lax.dynamic_slice_in_dim(target, me, 1, axis=0)
    my_rank = lax.dynamic_slice_in_dim(rank, me, 1, axis=0)
    mine = (my_target[:, None, :] == device[:, None, None]) & (my_rank[:, None, :] == ranks[None, :, None])
    order = jnp.sum(jnp.where(mine, index[None, None, :], 0), axis=2)
    return order.astype(jnp.int32).reshape(-1), code.astype(jnp.int32).reshape(-1)


def active(term_mask):
    comps = term_mask.shape[1]
    k = jnp.arange(comps, dtype=jnp.int32)
    on = term_mask == 1
    before = jnp.sum((on[:, None, :] & (k[None, None, :] < k[None, :, None])).astype(jnp.int32), axis=2)
    j = jnp.arange(WACT, dtype=jnp.int32)
    chosen = on[:, None, :] & (before[:, None, :] == j[None, :, None])
    return jnp.sum(jnp.where(chosen, k[None, None, :], 0), axis=2).astype(jnp.int32)


def send_kernel(plan, groups, code_ref, comps_ref, own_ref, other_ref, *rest):
    outs, sem = rest[: len(groups)], rest[len(groups)]
    core = lax.axis_index("blk")
    for n, group in enumerate(groups):
        out = outs[n]

        @pl.loop(0, len(group) * plan.capc)
        def _(s):
            p = group[0] if len(group) == 1 else s // plan.capc
            q = s if len(group) == 1 else lax.rem(s, plan.capc)
            code = code_ref[plan.partner(p) * plan.cap + plan.rank0(core) + q]
            sector = lax.rem(code, plan.sectors)
            row = lax.div(code, plan.sectors)
            for j in range(WACT):
                k = comps_ref[row * WACT + j]
                side = lax.div(k, plan.half)
                at = lax.rem(k, plan.half)
                dst = out.at[s, j]

                @pl.when(side == core)
                def _():
                    pltpu.make_async_copy(own_ref.at[sector, at], dst, sem.at[n]).start()

                @pl.when(side != core)
                def _():
                    pltpu.make_async_copy(other_ref.at[sector, at], dst, sem.at[n]).start()

    for n in range(len(groups)):
        pltpu.make_async_copy(outs[n], outs[n], sem.at[n]).wait()


def send(plan, groups, code, comps, own, other):
    w = plan.width
    return pl.pallas_call(
        functools.partial(send_kernel, plan, groups),
        out_shape=[jax.ShapeDtypeStruct((len(g) * plan.capc, WACT, w, w), own.dtype) for g in groups],
        in_specs=[smem(), smem(), hbm(), hbm()],
        out_specs=[hbm() for _ in groups],
        scratch_shapes=[pltpu.SemaphoreType.DMA((len(groups),))],
        cost_estimate=pl.CostEstimate(flops=0, bytes_accessed=2 * len(groups) * len(groups[0]) * plan.capc * WACT * w * w * 2, transcendentals=0),
    )(code, comps, own, other)


def product_kernel(plan, order_ref, comps_ref, own_l, other_l, *rest):
    waves, (out_ref, left, psi, sem) = rest[: plan.vectors], rest[plan.vectors :]
    core = lax.axis_index("blk")
    s = pl.program_id(0)
    w = plan.width

    @pl.when(s == 0)
    def _():
        copies = [
            pltpu.make_async_copy(own_l, left.at[:, pl.ds(core * plan.half, plan.half)], sem.at[0]),
            pltpu.make_async_copy(other_l, left.at[:, pl.ds((1 - core) * plan.half, plan.half)], sem.at[1]),
        ]
        for v in range(plan.vectors):
            copies.append(pltpu.make_async_copy(waves[v], psi.at[v], sem.at[2 + v]))
        for c in copies:
            c.start()
        for c in copies:
            c.wait()

    p, q = lax.div(s, plan.capc), lax.rem(s, plan.capc)
    b = order_ref[plan.partner(p) * plan.cap + plan.rank0(core) + q]
    sector = lax.div(b, plan.fan)
    lhs = jnp.concatenate([left[sector, comps_ref[sector * WACT + j]] for j in range(WACT)], axis=0)
    rhs = jnp.concatenate([psi[v, b] for v in range(plan.vectors)], axis=1)
    terms = jnp.dot(lhs, rhs, preferred_element_type=jnp.float32).astype(jnp.bfloat16)
    for j in range(WACT):
        for v in range(plan.vectors):
            out_ref[0, pl.ds(v * w, w), pl.ds(j * w, w)] = terms[j * w : (j + 1) * w, v * w : (v + 1) * w]


def products(plan, order, comps, own_l, other_l, waves):
    w, slots = plan.width, plan.devices * plan.capc
    return pl.pallas_call(
        functools.partial(product_kernel, plan),
        grid=(slots,),
        out_shape=jax.ShapeDtypeStruct((slots, plan.vectors * w, WACT * w), jnp.bfloat16),
        in_specs=[smem(), smem(), hbm(), hbm()] + [hbm() for _ in waves],
        out_specs=pl.BlockSpec((1, plan.vectors * w, WACT * w), lambda s: (s, 0, 0)),
        scratch_shapes=[
            pltpu.VMEM((plan.sectors, 2 * plan.half, w, w), jnp.bfloat16),
            pltpu.VMEM((plan.vectors, plan.blocks, w, w), jnp.bfloat16),
            pltpu.SemaphoreType.DMA((2 + plan.vectors,)),
        ],
        compiler_params=pltpu.CompilerParams(vmem_limit_bytes=VMEM),
        cost_estimate=pl.CostEstimate(
            flops=2 * slots * plan.vectors * WACT * w**3,
            bytes_accessed=slots * plan.vectors * WACT * w * w * 2 + 9_000_000,
            transcendentals=0,
        ),
    )(order, comps, own_l, other_l, *waves)


def contract_kernel(plan, terms_ref, right_ref, *outs):
    w = plan.width
    right = jnp.concatenate([right_ref[0, j] for j in range(WACT)], axis=1)
    done = lax.dot_general(
        terms_ref[0], right, (((1,), (1,)), ((), ())), preferred_element_type=jnp.float32
    ).astype(jnp.bfloat16)
    for v in range(plan.vectors):
        outs[v][0] = done[v * w : (v + 1) * w]


def contract(plan, group, terms, right):
    w, count = plan.width, len(group) * plan.capc
    first = group[0] * plan.capc
    return pl.pallas_call(
        functools.partial(contract_kernel, plan),
        grid=(count,),
        out_shape=[jax.ShapeDtypeStruct((count, w, w), jnp.bfloat16) for _ in range(plan.vectors)],
        in_specs=[
            pl.BlockSpec((1, plan.vectors * w, WACT * w), lambda s: (first + s, 0, 0)),
            pl.BlockSpec((1, WACT, w, w), lambda s: (s, 0, 0, 0)),
        ],
        out_specs=[pl.BlockSpec((1, w, w), lambda s: (s, 0, 0)) for _ in range(plan.vectors)],
        compiler_params=pltpu.CompilerParams(vmem_limit_bytes=VMEM),
        cost_estimate=pl.CostEstimate(
            flops=2 * count * plan.vectors * WACT * w**3,
            bytes_accessed=count * (plan.vectors + 1) * (WACT + 1) * w * w * 2,
            transcendentals=0,
        ),
    )(terms, right)


def place_kernel(plan, order_ref, *rest):
    n = len(plan.groups)
    parts, out_ref, sem = rest[: n * plan.vectors], rest[n * plan.vectors], rest[n * plan.vectors + 1]
    core = lax.axis_index("blk")
    for v in range(plan.vectors):
        whose = core if v == 0 else 1 - core
        for g, group in enumerate(plan.groups):
            part = parts[v * n + g]

            @pl.loop(0, len(group) * plan.capc)
            def _(s):
                p = group[0] if len(group) == 1 else s // plan.capc
                q = s if len(group) == 1 else lax.rem(s, plan.capc)
                b = order_ref[plan.partner(p) * plan.cap + plan.rank0(whose) + q]
                pltpu.make_async_copy(part.at[s], out_ref.at[b], sem).start()

    pltpu.make_async_copy(out_ref, out_ref, sem).wait()


def place(plan, order, parts):
    w = plan.width
    return pl.pallas_call(
        functools.partial(place_kernel, plan),
        out_shape=jax.ShapeDtypeStruct((plan.blocks, w, w), jnp.bfloat16),
        in_specs=[smem()] + [hbm() for _ in parts],
        out_specs=hbm(),
        scratch_shapes=[pltpu.SemaphoreType.DMA],
        cost_estimate=pl.CostEstimate(flops=0, bytes_accessed=2 * plan.blocks * w * w * 2, transcendentals=0),
    )(order, *parts)


def body(wave, left_env, right_env, right_slot, term_mask):
    devices = lax.axis_size("rows")
    plan = Plan(wave, left_env, devices, lax.axis_size("blk"))
    swap = functools.partial(lax.ppermute, axis_name="blk", perm=[(0, 1), (1, 0)])

    other_r = swap(right_env)
    comps = active(term_mask).reshape(-1)
    asked = lax.all_to_all(
        jnp.broadcast_to(comps[None], (devices, comps.shape[0])), "rows", split_axis=0, concat_axis=0, tiled=True
    ).reshape(-1)
    order, code = lists(plan, right_slot)

    groups = plan.groups
    sent = []
    for some in (groups[:2], groups[2:]):
        if some:
            sent += send(plan, some, code, asked, right_env, other_r)
    if plan.by_pairs:
        right = [
            x if g == (0,) else lax.ppermute(x, "rows", [(i, i ^ g[0]) for i in range(devices)])
            for g, x in zip(groups, sent)
        ]
    else:
        right = [lax.all_to_all(sent[0], "rows", split_axis=0, concat_axis=0, tiled=True)]

    other_l = swap(left_env)
    waves = [wave[0]] + ([swap(wave[0])] if plan.split else [])
    terms = products(plan, order, comps, left_env, other_l, waves)
    done = [contract(plan, g, terms, r) for g, r in zip(groups, right)]
    parts = [d[0] for d in done]
    if plan.split:
        parts += [swap(d[1]) for d in done]
    return place(plan, order, parts)[None]


def solution(mesh):
    in_specs = (
        P("blk", ("parts", "rows"), None, None),
        P(("parts", "rows"), "blk", None, None),
        P(("parts", "rows"), "blk", None, None),
        P("parts"),
        P(("parts", "rows"), None),
    )
    out_specs = P("blk", ("parts", "rows"), None, None)
    return jax.shard_map(body, mesh=mesh, in_specs=in_specs, out_specs=out_specs, check_vma=False)
```

time: 470 us -> 341 us (0.73)
  the two profiles are of different devices: /device:TPU:0 before, /device:TPU:9 now
where the time goes in v1:
time: 341 us; the launch traced here: 340 us
  Pallas kernels  271 us (79%)
  waiting for transfers between devices  28.2 us (8%)
  starting transfers between devices  26.5 us (8%)
  local copies, waits for them, and re-layouts  11.7 us (3%)
    pallas_call x2, Pallas kernels, send(): pl.pallas_call(functools.partial(send_kernel, plan, groups), out_shape=[j...  163 us
    pallas_call x1, Pallas kernels, place(): pl.pallas_call(functools.partial(place_kernel, plan), out_shape=jax.Shape...  65.3 us
    ppermute x7, waiting for transfers between devices, body(): lax.ppermute(x, 'rows', [(i, i ^ g[0]) for i in range(devices)])  25.2 us
    pallas_call x8, Pallas kernels, contract(): pl.pallas_call(functools.partial(contract_kernel, plan), grid=(count,), o...  22.6 us
    pallas_call x1, Pallas kernels, products(): pl.pallas_call(functools.partial(product_kernel, plan), grid=(slots,), ou...  19.9 us
    ppermute x8, starting transfers between devices, body(): parts += [swap(d[1]) for d in done]  10.4 us
    ppermute x7, starting transfers between devices, body(): lax.ppermute(x, 'rows', [(i, i ^ g[0]) for i in range(devices)])  9.12 us
    unnamed x44, local copies, waits for them, and re-layouts  8.14 us
  transfers between devices with their start and end apart: 19, of which 6 were waited for; matrix products, arithmetic and copies ran while one was open for 2% of the time, Pallas kernels for 60%

profile of v1, /device:TPU:9, one launch (start us, length us, event | category | flops | bytes accessed | tf_op | source)
XLA Modules:
  0.0 339.9 jit_solution(13908032750455447745)
XLA Ops:
  3.2 5.7 %all-to-all-start = ((s32[8,1,80]{2,1,0:T(1,128)}), s32[8,1,80]{2,1,0:T(1,128)S(1)}, u32[]{:S(2)}, u32[]{:S(2)}) async-start(s32[8,1,80]{2,1,0:T(1,128)} %broadcast_in_dim.39), calls=%async_computation | async-start | bytes 8192 | tf_op jit(solution)/shard_map/all_to_all | solution.py:239
  11.0 2.0 all-to-all-done
  14.8 1.5 copy-done.13
  16.3 41.6 %shard_map.56 = (bf16[4,5,128,128]{3,2,1,0:T(8,128)(2,1)}, bf16[4,5,128,128]{3,2,1,0:T(8,128)(2,1)}) custom-call(s32[64]{0:T(128)} %reshape.280.code_ref, s32[640]{0:T(1024)} %reshape.281.comps_ref, bf16[16,5,128,128]{3,2,1,0:T(8,128)(2,1)} %own_ref.3, bf16[16,5,128,128]{3,2,1,0:T(8,128)(2,1)} %copy-done.13), custom_call_target="tpu_custom_call" | custom-call | bytes 2621440 | tf_op jit(solution)/shard_map/pallas_call | solution.py:108
  58.2 2.1 collective-permute-start.4
  60.3 121.1 %shard_map.59 = (bf16[4,5,128,128]{3,2,1,0:T(8,128)(2,1)}, bf16[4,5,128,128]{3,2,1,0:T(8,128)(2,1)}, bf16[4,5,128,128]{3,2,1,0:T(8,128)(2,1)}, bf16[4,5,128,128]...) custom-call(s32[64]{0:T(128)} %reshape.280.code_ref, s32[640]{0:T(1024)} %reshape.281.comps_ref, ...), custom_call_target="tpu_custom_call" | custom-call | bytes 7864320 | tf_op jit(solution)/shard_map/pallas_call | solution.py:108
  181.8 2.1 collective-permute-start.6
  183.9 3.0 collective-permute-start.7
  187.0 0.8 copy-done.1
  187.8 1.2 collective-permute-start.9
  189.3 19.9 %shard_map.55.terms_ref = bf16[32,256,640]{2,1,0:T(8,128)(2,1)} custom-call(s32[64]{0:T(128)S(1)} %reshape.278.order_ref, s32[80]{0:T(128)S(1)} %reshape.279.comps_ref, bf16[16,5,128,128]{3,2,1,0:T(8,128)(2,1)} %own_l.1, bf16[16,5,128,128]{3,2,1,0:T(8,128)(2,1)} %collective-permute-done.other_l, bf16[64,128,128]{2,1,0:T(8,128)(2,1)S(1)} %bitcast.7, ...), custom_call_target="tpu_custom_call" | custom-call | flops 1342177280 | bytes 19485760 | tf_op jit(solution)/shard_map/pallas_call | solution.py:150
  209.3 2.8 shard_map.65
  212.7 2.8 shard_map.57
  216.2 2.8 shard_map.58
  219.7 5.1 %collective-permute-done.5.right_ref = bf16[4,5,128,128]{3,2,1,0:T(8,128)(2,1)} collective-permute-done((bf16[4,5,128,128]{3,2,1,0:T(8,128)(2,1)}, bf16[4,5,128,128]{3,2,1,0:T(8,128)(2,1)}, u32[]{:S(2)}, u32[]{:S(2)}) %collective-permute-start.5) | collective-permute-done | bytes 655392 | tf_op jit(solution)/shard_map/ppermute | solution.py:251
  224.8 4.3 %collective-permute-start.17 = (bf16[4,128,128]{2,1,0:T(8,128)(2,1)S(1)}, bf16[4,128,128]{2,1,0:T(8,128)(2,1)S(1)}, u32[]{:S(2)}, u32[]{:S(2)}) collective-permute-start(bf16[4,128,128]{2,1,0:T(8,128)(2,1)S(1)} %get-tuple-element.52), channel_id=1, source_target_pairs={{0,8},{8,0},{1,9},{9,1},{2,10},{10,2},{3,11},{11,3},{4,12},{12,4},... | collective-permute-start | bytes 393224 | tf_op jit(solution)/shard_map/ppermute | solution.py:263
  229.0 20.1 %collective-permute-done.6.right_ref = bf16[4,5,128,128]{3,2,1,0:T(8,128)(2,1)} collective-permute-done((bf16[4,5,128,128]{3,2,1,0:T(8,128)(2,1)}, bf16[4,5,128,128]{3,2,1,0:T(8,128)(2,1)}, u32[]{:S(2)}, u32[]{:S(2)}) %collective-permute-start.6) | collective-permute-done | bytes 655392 | tf_op jit(solution)/shard_map/ppermute | solution.py:251
  249.1 4.6 %collective-permute-start.10 = (bf16[4,128,128]{2,1,0:T(8,128)(2,1)S(1)}, bf16[4,128,128]{2,1,0:T(8,128)(2,1)S(1)}, u32[]{:S(2)}, u32[]{:S(2)}) collective-permute-start(bf16[4,128,128]{2,1,0:T(8,128)(2,1)S(1)} %get-tuple-element.45), channel_id=1, source_target_pairs={{0,8},{8,0},{1,9},{9,1},{2,10},{10,2},{3,11},{11,3},{4,12},{12,4},... | collective-permute-start | bytes 393224 | tf_op jit(solution)/shard_map/ppermute | solution.py:263
  253.8 2.9 shard_map.60
  257.3 2.9 shard_map.61
  260.9 2.9 shard_map.62
  264.9 2.9 shard_map.63
  268.4 2.8 shard_map.64
  274.6 65.3 %shard_map.66 = bf16[64,128,128]{2,1,0:T(8,128)(2,1)} custom-call(s32[64]{0:T(128)} %copy-done.12, bf16[4,128,128]{2,1,0:T(8,128)(2,1)} %copy-done.5, bf16[4,128,128]{2,1,0:T(8,128)(2,1)} %copy-done.6, bf16[4,128,128]{2,1,0:T(8,128)(2,1)} %copy-done.7, bf16[4,128,128]{2,1,0:T(8,128)(2,1)} %copy-done.8, bf16[4,128,128]{2,1,0:T(8,128)(2,1)} %copy-done.9, ...), custom_call_target="tpu_custom_call" | custom-call | bytes 4194304 | tf_op jit(solution)/shard_map/pallas_call | solution.py:222
  (95 shorter events, 16.5 us)
Async XLA Ops:
  0.0 14.8 %collective-permute-start.2 = (bf16[16,5,128,128]{3,2,1,0:T(8,128)(2,1)}, bf16[16,5,128,128]{3,2,1,0:T(8,128)(2,1)S(1)}, u32[]{:S(2)}, u32[]{:S(2)}) collective-permute-start(bf16[16,5,128,128]{3,2,1,0:T(8,128)(2,1)} %own_ref.3), channel_id=1, source_target_pairs={{0,8},{8,0},{1,9},{9,1},{2,10},{10,2},{3,11},{11,3},{4,12},{12,4},... | collective-permute-start | bytes 7864328 | tf_op jit(solution)/shard_map/ppermute | solution.py:237
  0.7 183.2 %collective-permute-start = (bf16[16,5,128,128]{3,2,1,0:T(8,128)(2,1)}, bf16[16,5,128,128]{3,2,1,0:T(8,128)(2,1)}, u32[]{:S(2)}, u32[]{:S(2)}) collective-permute-start(bf16[16,5,128,128]{3,2,1,0:T(8,128)(2,1)} %own_l.1), channel_id=1, source_target_pairs={{0,8},{8,0},{1,9},{9,1},{2,10},{10,2},{3,11},{11,3},{4,12},{12,4},... | collective-permute-start | bytes 7864328 | tf_op jit(solution)/shard_map/ppermute | solution.py:257
  0.7 181.1 %collective-permute-start.1 = (bf16[64,128,128]{2,1,0:T(8,128)(2,1)}, bf16[64,128,128]{2,1,0:T(8,128)(2,1)}, u32[]{:S(2)}, u32[]{:S(2)}) collective-permute-start(bf16[64,128,128]{2,1,0:T(8,128)(2,1)} %bitcast.6), channel_id=1, source_target_pairs={{0,8},{8,0},{1,9},{9,1},{2,10},{10,2},{3,11},{11,3},{4,12},{12,4},... | collective-permute-start | bytes 6291464 | tf_op jit(solution)/shard_map/ppermute | solution.py:258
  3.2 9.8 %all-to-all-start = ((s32[8,1,80]{2,1,0:T(1,128)}), s32[8,1,80]{2,1,0:T(1,128)S(1)}, u32[]{:S(2)}, u32[]{:S(2)}) async-start(s32[8,1,80]{2,1,0:T(1,128)} %broadcast_in_dim.39), calls=%async_computation | async-start | bytes 8192 | tf_op jit(solution)/shard_map/all_to_all | solution.py:239
  57.9 129.0 %collective-permute-start.3 = (bf16[4,5,128,128]{3,2,1,0:T(8,128)(2,1)}, bf16[4,5,128,128]{3,2,1,0:T(8,128)(2,1)S(1)}, u32[]{:S(2)}, u32[]{:S(2)}) collective-permute-start(bf16[4,5,128,128]{3,2,1,0:T(8,128)(2,1)} %get-tuple-element.29), channel_id=1, source_target_pairs={{0,4},{1,5},{2,6},{3,7},{4,0},{5,1},{6,2},{7,3},{8,12},{9,13},{10,... | collective-permute-start | bytes 1966088 | tf_op jit(solution)/shard_map/ppermute | solution.py:251
  58.2 128.7 %collective-permute-start.4 = (bf16[4,5,128,128]{3,2,1,0:T(8,128)(2,1)}, bf16[4,5,128,128]{3,2,1,0:T(8,128)(2,1)S(1)}, u32[]{:S(2)}, u32[]{:S(2)}) collective-permute-start(bf16[4,5,128,128]{3,2,1,0:T(8,128)(2,1)} %get-tuple-element.31), channel_id=1, source_target_pairs={{0,5},{1,4},{2,7},{3,6},{4,1},{5,0},{6,3},{7,2},{8,13},{9,12},{10,... | collective-permute-start | bytes 1966088 | tf_op jit(solution)/shard_map/ppermute | solution.py:251
  60.3 129.0 %copy-start = (bf16[1,64,128,128]{3,2,1,0:T(8,128)(2,1)S(1)}, bf16[1,64,128,128]{3,2,1,0:T(8,128)(2,1)}, u32[]{:S(2)}) copy-start(bf16[1,64,128,128]{3,2,1,0:T(8,128)(2,1)} %param.5) | copy-start | bytes 6291460
  181.5 43.3 %collective-permute-start.5 = (bf16[4,5,128,128]{3,2,1,0:T(8,128)(2,1)}, bf16[4,5,128,128]{3,2,1,0:T(8,128)(2,1)}, u32[]{:S(2)}, u32[]{:S(2)}) collective-permute-start(bf16[4,5,128,128]{3,2,1,0:T(8,128)(2,1)} %get-tuple-element.33), channel_id=1, source_target_pairs={{0,6},{1,7},{2,4},{3,5},{4,2},{5,3},{6,0},{7,1},{8,14},{9,15},{10,... | collective-permute-start | bytes 1966088 | tf_op jit(solution)/shard_map/ppermute | solution.py:251
  181.8 67.3 %collective-permute-start.6 = (bf16[4,5,128,128]{3,2,1,0:T(8,128)(2,1)}, bf16[4,5,128,128]{3,2,1,0:T(8,128)(2,1)}, u32[]{:S(2)}, u32[]{:S(2)}) collective-permute-start(bf16[4,5,128,128]{3,2,1,0:T(8,128)(2,1)} %get-tuple-element.35), channel_id=1, source_target_pairs={{0,7},{1,6},{2,5},{3,4},{4,3},{5,2},{6,1},{7,0},{8,15},{9,14},{10,... | collective-permute-start | bytes 1966088 | tf_op jit(solution)/shard_map/ppermute | solution.py:251
  183.9 69.9 %collective-permute-start.7 = (bf16[4,5,128,128]{3,2,1,0:T(8,128)(2,1)}, bf16[4,5,128,128]{3,2,1,0:T(8,128)(2,1)}, u32[]{:S(2)}, u32[]{:S(2)}) collective-permute-start(bf16[4,5,128,128]{3,2,1,0:T(8,128)(2,1)} %get-tuple-element.37), channel_id=1, source_target_pairs={{0,2},{1,3},{2,0},{3,1},{4,6},{5,7},{6,4},{7,5},{8,10},{9,11},{10,... | collective-permute-start | bytes 1966088 | tf_op jit(solution)/shard_map/ppermute | solution.py:251
  186.9 77.5 %collective-permute-start.8 = (bf16[4,5,128,128]{3,2,1,0:T(8,128)(2,1)}, bf16[4,5,128,128]{3,2,1,0:T(8,128)(2,1)}, u32[]{:S(2)}, u32[]{:S(2)}) collective-permute-start(bf16[4,5,128,128]{3,2,1,0:T(8,128)(2,1)} %get-tuple-element.39), channel_id=1, source_target_pairs={{0,3},{1,2},{2,1},{3,0},{4,7},{5,6},{6,5},{7,4},{8,11},{9,10},{10,... | collective-permute-start | bytes 1966088 | tf_op jit(solution)/shard_map/ppermute | solution.py:251
  187.8 80.6 %collective-permute-start.9 = (bf16[4,5,128,128]{3,2,1,0:T(8,128)(2,1)}, bf16[4,5,128,128]{3,2,1,0:T(8,128)(2,1)S(1)}, u32[]{:S(2)}, u32[]{:S(2)}) collective-permute-start(bf16[4,5,128,128]{3,2,1,0:T(8,128)(2,1)} %get-tuple-element.41), channel_id=1, source_target_pairs={{0,1},{1,0},{2,3},{3,2},{4,5},{5,4},{6,7},{7,6},{8,9},{9,8},{10,11... | collective-permute-start | bytes 1966088 | tf_op jit(solution)/shard_map/ppermute | solution.py:251
  189.3 20.0 %copy-start.12 = (s32[64]{0:T(128)}, s32[64]{0:T(128)S(1)}, u32[]{:S(2)}) copy-start(s32[64]{0:T(128)S(1)} %reshape.278.order_ref) | copy-start | bytes 772
  189.3 20.0 %copy-start.3 = (bf16[4,5,128,128]{3,2,1,0:T(8,128)(2,1)S(1)}, bf16[4,5,128,128]{3,2,1,0:T(8,128)(2,1)}, u32[]{:S(2)}) copy-start(bf16[4,5,128,128]{3,2,1,0:T(8,128)(2,1)} %get-tuple-element.43.right_ref) | copy-start | bytes 1966084
  212.7 3.5 %copy-start.2 = (bf16[4,5,128,128]{3,2,1,0:T(8,128)(2,1)S(1)}, bf16[4,5,128,128]{3,2,1,0:T(8,128)(2,1)}, u32[]{:S(2)}) copy-start(bf16[4,5,128,128]{3,2,1,0:T(8,128)(2,1)} %copy-done.1) | copy-start | bytes 1966084
  224.8 47.1 %collective-permute-start.17 = (bf16[4,128,128]{2,1,0:T(8,128)(2,1)S(1)}, bf16[4,128,128]{2,1,0:T(8,128)(2,1)S(1)}, u32[]{:S(2)}, u32[]{:S(2)}) collective-permute-start(bf16[4,128,128]{2,1,0:T(8,128)(2,1)S(1)} %get-tuple-element.52), channel_id=1, source_target_pairs={{0,8},{8,0},{1,9},{9,1},{2,10},{10,2},{3,11},{11,3},{4,12},{12,4},... | collective-permute-start | bytes 393224 | tf_op jit(solution)/shard_map/ppermute | solution.py:263
  249.1 23.2 %collective-permute-start.10 = (bf16[4,128,128]{2,1,0:T(8,128)(2,1)S(1)}, bf16[4,128,128]{2,1,0:T(8,128)(2,1)S(1)}, u32[]{:S(2)}, u32[]{:S(2)}) collective-permute-start(bf16[4,128,128]{2,1,0:T(8,128)(2,1)S(1)} %get-tuple-element.45), channel_id=1, source_target_pairs={{0,8},{8,0},{1,9},{9,1},{2,10},{10,2},{3,11},{11,3},{4,12},{12,4},... | collective-permute-start | bytes 393224 | tf_op jit(solution)/shard_map/ppermute | solution.py:263
  253.8 18.7 %collective-permute-start.11 = (bf16[4,128,128]{2,1,0:T(8,128)(2,1)S(1)}, bf16[4,128,128]{2,1,0:T(8,128)(2,1)S(1)}, u32[]{:S(2)}, u32[]{:S(2)}) collective-permute-start(bf16[4,128,128]{2,1,0:T(8,128)(2,1)S(1)} %get-tuple-element.46), channel_id=1, source_target_pairs={{0,8},{8,0},{1,9},{9,1},{2,10},{10,2},{3,11},{11,3},{4,12},{12,4},... | collective-permute-start | bytes 393224 | tf_op jit(solution)/shard_map/ppermute | solution.py:263
  264.4 8.5 %collective-permute-start.12 = (bf16[4,128,128]{2,1,0:T(8,128)(2,1)S(1)}, bf16[4,128,128]{2,1,0:T(8,128)(2,1)S(1)}, u32[]{:S(2)}, u32[]{:S(2)}) collective-permute-start(bf16[4,128,128]{2,1,0:T(8,128)(2,1)S(1)} %get-tuple-element.47), channel_id=1, source_target_pairs={{0,8},{8,0},{1,9},{9,1},{2,10},{10,2},{3,11},{11,3},{4,12},{12,4},... | collective-permute-start | bytes 393224 | tf_op jit(solution)/shard_map/ppermute | solution.py:263
  268.4 4.5 %collective-permute-start.13 = (bf16[4,128,128]{2,1,0:T(8,128)(2,1)S(1)}, bf16[4,128,128]{2,1,0:T(8,128)(2,1)S(1)}, u32[]{:S(2)}, u32[]{:S(2)}) collective-permute-start(bf16[4,128,128]{2,1,0:T(8,128)(2,1)S(1)} %get-tuple-element.48), channel_id=1, source_target_pairs={{0,8},{8,0},{1,9},{9,1},{2,10},{10,2},{3,11},{11,3},{4,12},{12,4},... | collective-permute-start | bytes 393224 | tf_op jit(solution)/shard_map/ppermute | solution.py:263
  271.9 2.0 copy-start.14
  271.9 1.5 collective-permute-start.14
  272.4 1.3 collective-permute-start.15
  272.5 1.4 collective-permute-start.16
  (17 other events, 14.6 us)

commit v2 on v1

--- a/solution.py
+++ b/solution.py
@@ -13,6 +13,10 @@
 
 def smem():
     return pl.BlockSpec(memory_space=pltpu.SMEM)
+
+
+def vmem():
+    return pl.BlockSpec(memory_space=pltpu.VMEM)
 
 
 def hbm():
@@ -72,47 +76,52 @@
     return jnp.sum(jnp.where(chosen, k[None, None, :], 0), axis=2).astype(jnp.int32)
 
 
-def send_kernel(plan, groups, code_ref, comps_ref, own_ref, other_ref, *rest):
-    outs, sem = rest[: len(groups)], rest[len(groups)]
+def each(count, step):
+    if count <= 8:
+        for s in range(count):
+            step(s)
+    else:
+        pl.loop(0, count)(step)
+
+
+def slot(plan, group, s):
+    if len(group) == 1:
+        return group[0], s
+    return lax.div(s, plan.capc), lax.rem(s, plan.capc)
+
+
+def send_kernel(plan, groups, code_ref, *rest):
+    n = len(groups)
+    asked, (own_ref, other_ref), outs = rest[:n], rest[n : n + 2], rest[n + 2 :]
     core = lax.axis_index("blk")
-    for n, group in enumerate(groups):
-        out = outs[n]
-
-        @pl.loop(0, len(group) * plan.capc)
-        def _(s):
-            p = group[0] if len(group) == 1 else s // plan.capc
-            q = s if len(group) == 1 else lax.rem(s, plan.capc)
+    for group, comps_ref, out in zip(groups, asked, outs):
+
+        def step(s):
+            p, q = slot(plan, group, s)
             code = code_ref[plan.partner(p) * plan.cap + plan.rank0(core) + q]
             sector = lax.rem(code, plan.sectors)
             row = lax.div(code, plan.sectors)
+            if len(group) == 1:
+                row = lax.rem(row, plan.sectors)
             for j in range(WACT):
                 k = comps_ref[row * WACT + j]
-                side = lax.div(k, plan.half)
+                mine = lax.div(k, plan.half) == core
                 at = lax.rem(k, plan.half)
-                dst = out.at[s, j]
-
-                @pl.when(side == core)
-                def _():
-                    pltpu.make_async_copy(own_ref.at[sector, at], dst, sem.at[n]).start()
-
-                @pl.when(side != core)
-                def _():
-                    pltpu.make_async_copy(other_ref.at[sector, at], dst, sem.at[n]).start()
-
-    for n in range(len(groups)):
-        pltpu.make_async_copy(outs[n], outs[n], sem.at[n]).wait()
-
-
-def send(plan, groups, code, comps, own, other):
+                out[s, j] = jnp.where(mine, own_ref[sector, at], other_ref[sector, at])
+
+        each(len(group) * plan.capc, step)
+
+
+def send(plan, groups, code, asked, own, other):
     w = plan.width
     return pl.pallas_call(
         functools.partial(send_kernel, plan, groups),
         out_shape=[jax.ShapeDtypeStruct((len(g) * plan.capc, WACT, w, w), own.dtype) for g in groups],
-        in_specs=[smem(), smem(), hbm(), hbm()],
-        out_specs=[hbm() for _ in groups],
-        scratch_shapes=[pltpu.SemaphoreType.DMA((len(groups),))],
-        cost_estimate=pl.CostEstimate(flops=0, bytes_accessed=2 * len(groups) * len(groups[0]) * plan.capc * WACT * w * w * 2, transcendentals=0),
-    )(code, comps, own, other)
+        in_specs=[smem()] + [smem() for _ in groups] + [vmem(), vmem()],
+        out_specs=[vmem() for _ in groups],
+        compiler_params=pltpu.CompilerParams(vmem_limit_bytes=VMEM),
+        cost_estimate=pl.CostEstimate(flops=0, bytes_accessed=8_000_000, transcendentals=0),
+    )(code, *asked, own, other)
 
 
 def product_kernel(plan, order_ref, comps_ref, own_l, other_l, *rest):
@@ -200,21 +209,19 @@
 
 def place_kernel(plan, order_ref, *rest):
     n = len(plan.groups)
-    parts, out_ref, sem = rest[: n * plan.vectors], rest[n * plan.vectors], rest[n * plan.vectors + 1]
+    parts, out_ref = rest[:-1], rest[-1]
     core = lax.axis_index("blk")
     for v in range(plan.vectors):
         whose = core if v == 0 else 1 - core
         for g, group in enumerate(plan.groups):
             part = parts[v * n + g]
 
-            @pl.loop(0, len(group) * plan.capc)
-            def _(s):
-                p = group[0] if len(group) == 1 else s // plan.capc
-                q = s if len(group) == 1 else lax.rem(s, plan.capc)
+            def step(s):
+                p, q = slot(plan, group, s)
                 b = order_ref[plan.partner(p) * plan.cap + plan.rank0(whose) + q]
-                pltpu.make_async_copy(part.at[s], out_ref.at[b], sem).start()
-
-    pltpu.make_async_copy(out_ref, out_ref, sem).wait()
+                out_ref[b] = part[s]
+
+            each(len(group) * plan.capc, step)
 
 
 def place(plan, order, parts):
@@ -222,9 +229,9 @@
     return pl.pallas_call(
         functools.partial(place_kernel, plan),
         out_shape=jax.ShapeDtypeStruct((plan.blocks, w, w), jnp.bfloat16),
-        in_specs=[smem()] + [hbm() for _ in parts],
-        out_specs=hbm(),
-        scratch_shapes=[pltpu.SemaphoreType.DMA],
+        in_specs=[smem()] + [vmem() for _ in parts],
+        out_specs=vmem(),
+        compiler_params=pltpu.CompilerParams(vmem_limit_bytes=VMEM),
         cost_estimate=pl.CostEstimate(flops=0, bytes_accessed=2 * plan.blocks * w * w * 2, transcendentals=0),
     )(order, *parts)
 
@@ -236,23 +243,24 @@
 
     other_r = swap(right_env)
     comps = active(term_mask).reshape(-1)
-    asked = lax.all_to_all(
-        jnp.broadcast_to(comps[None], (devices, comps.shape[0])), "rows", split_axis=0, concat_axis=0, tiled=True
-    ).reshape(-1)
     order, code = lists(plan, right_slot)
-
     groups = plan.groups
-    sent = []
-    for some in (groups[:2], groups[2:]):
-        if some:
-            sent += send(plan, some, code, asked, right_env, other_r)
+
+    def meet(x, group):
+        if group == (0,):
+            return x
+        return lax.ppermute(x, "rows", [(i, i ^ group[0]) for i in range(devices)])
+
     if plan.by_pairs:
-        right = [
-            x if g == (0,) else lax.ppermute(x, "rows", [(i, i ^ g[0]) for i in range(devices)])
-            for g, x in zip(groups, sent)
-        ]
+        asked = [meet(comps, g) for g in groups]
+        sent = send(plan, groups[:2], code, asked[:2], right_env, other_r)
+        sent += send(plan, groups[2:], code, asked[2:], right_env, other_r)
+        right = [meet(x, g) for g, x in zip(groups, sent)]
     else:
-        right = [lax.all_to_all(sent[0], "rows", split_axis=0, concat_axis=0, tiled=True)]
+        everyone = functools.partial(lax.all_to_all, axis_name="rows", split_axis=0, concat_axis=0, tiled=True)
+        asked = everyone(jnp.broadcast_to(comps[None], (devices, comps.shape[0]))).reshape(-1)
+        sent = send(plan, groups, code, [asked], right_env, other_r)
+        right = [everyone(sent[0])]
 
     other_l = swap(left_env)
     waves = [wave[0]] + ([swap(wave[0])] if plan.split else [])

time: 341 us -> 185 us (0.54)
  Pallas kernels: 271 us -> 53.4 us
  waiting for transfers between devices: 28.2 us -> 99.8 us
  local copies, waits for them, and re-layouts: 11.7 us -> 5.32 us
    pallas_call x2, Pallas kernels: 163 us -> 8.8 us  [send(): pl.pallas_call(functools.partial(send_kernel, plan, groups), out_shape=[j...]
    ppermute x7 -> x14, waiting for transfers between devices: 25.2 us -> 98.8 us  [meet(): return lax.ppermute(x, 'rows', [(i, i ^ group[0]) for i in range(devices)])]
    pallas_call x1, Pallas kernels: 65.3 us -> 2.01 us  [place(): pl.pallas_call(functools.partial(place_kernel, plan), out_shape=jax.Shape...]
    ppermute x7 -> x14, starting transfers between devices: 9.12 us -> 17.3 us  [meet(): return lax.ppermute(x, 'rows', [(i, i ^ group[0]) for i in range(devices)])]
    all_to_all x1 -> x0, starting transfers between devices: 5.72 us -> none  [body(): lax.all_to_all(jnp.broadcast_to(comps[None], (devices, comps.shape[0])),...]
    ppermute x8, starting transfers between devices: 10.4 us -> 4.97 us  [body(): parts += [swap(d[1]) for d in done]]
    unnamed x44 -> x10, local copies, waits for them, and re-layouts: 8.14 us -> 4.15 us
  transfers between devices with their start and end apart: 19 -> 25, of which waited for: 6 -> 11; matrix products, arithmetic and copies ran while one was open for 2% -> 2% of each run, Pallas kernels for 60% -> 28%
where the time goes in v2:
time: 185 us; the launch traced here: 184 us
  waiting for transfers between devices  99.8 us (54%)
  Pallas kernels  53.4 us (29%)
  starting transfers between devices  23.4 us (13%)
  local copies, waits for them, and re-layouts  5.32 us (3%)
  other arithmetic  2.01 us (1%)
    ppermute x14, waiting for transfers between devices, meet(): return lax.ppermute(x, 'rows', [(i, i ^ group[0]) for i in range(devices)])  98.8 us
    pallas_call x8, Pallas kernels, contract(): pl.pallas_call(functools.partial(contract_kernel, plan), grid=(count,), o...  22.7 us
    pallas_call x1, Pallas kernels, products(): pl.pallas_call(functools.partial(product_kernel, plan), grid=(slots,), ou...  19.9 us
    ppermute x14, starting transfers between devices, meet(): return lax.ppermute(x, 'rows', [(i, i ^ group[0]) for i in range(devices)])  17.3 us
    pallas_call x2, Pallas kernels, send(): pl.pallas_call(functools.partial(send_kernel, plan, groups), out_shape=[j...  8.8 us
    ppermute x8, starting transfers between devices, body(): parts += [swap(d[1]) for d in done]  4.97 us
    unnamed x10, local copies, waits for them, and re-layouts  4.15 us
  transfers between devices with their start and end apart: 25, of which 11 were waited for; matrix products, arithmetic and copies ran while one was open for 2% of the time, Pallas kernels for 28%

profile of v2, /device:TPU:9, one launch (start us, length us, event | category | flops | bytes accessed | tf_op | source)
XLA Modules:
  0.0 184.2 jit_solution(9181356277596014803)
XLA Ops:
  2.6 2.4 %collective-permute-start.2 = (s32[80]{0:T(128)S(1)}, s32[80]{0:T(128)S(1)}, u32[]{:S(2)}, u32[]{:S(2)}) collective-permute-start(s32[80]{0:T(128)S(1)} %reshape.267.comps_ref.rest_5_), channel_id=1, source_target_pairs={{0,4},{1,5},{2,6},{3,7},{4,0},{5,1},{6,2},{7,3},{8,12},{9,13},{10,... | collective-permute-start | bytes 968 | tf_op jit(solution)/shard_map/ppermute | solution.py:252
  7.5 1.7 collective-permute-done.3.rest_1_
  10.7 1.7 copy-done
  12.4 3.3 %shard_map.56 = (bf16[4,5,128,128]{3,2,1,0:T(8,128)(2,1)}, bf16[4,5,128,128]{3,2,1,0:T(8,128)(2,1)}) custom-call(s32[64]{0:T(128)S(1)} %reshape.268.code_ref, s32[80]{0:T(128)S(1)} %collective-permute-done.2.rest_0_, s32[80]{0:T(128)S(1)} %collective-permute-done.3.rest_1_, bf16[16,5,128,128]{3,2,1,0:T(8,128)(2,1)S(1)} %copy-done, ...), custom_call_target="tpu_custom_call" | custom-call | bytes 8000000 | tf_op jit(solution)/shard_map/pallas_call | solution.py:117
  15.7 2.3 %collective-permute-start.5 = (bf16[4,5,128,128]{3,2,1,0:T(8,128)(2,1)}, bf16[4,5,128,128]{3,2,1,0:T(8,128)(2,1)S(1)}, u32[]{:S(2)}, u32[]{:S(2)}) collective-permute-start(bf16[4,5,128,128]{3,2,1,0:T(8,128)(2,1)} %get-tuple-element.29), channel_id=1, source_target_pairs={{0,4},{1,5},{2,6},{3,7},{4,0},{5,1},{6,2},{7,3},{8,12},{9,13},{10,... | collective-permute-start | bytes 1966088 | tf_op jit(solution)/shard_map/ppermute | solution.py:252
  20.3 54.5 %collective-permute-done.7.rest_0_ = s32[80]{0:T(128)S(1)} collective-permute-done((s32[80]{0:T(128)S(1)}, s32[80]{0:T(128)S(1)}, u32[]{:S(2)}, u32[]{:S(2)}) %collective-permute-start.7) | collective-permute-done | bytes 352 | tf_op jit(solution)/shard_map/ppermute | solution.py:252
  74.8 2.7 %collective-permute-start.8 = (s32[80]{0:T(128)S(1)}, s32[80]{0:T(128)S(1)}, u32[]{:S(2)}, u32[]{:S(2)}) collective-permute-start(s32[80]{0:T(128)S(1)} %reshape.267.comps_ref.rest_5_), channel_id=1, source_target_pairs={{0,7},{1,6},{2,5},{3,4},{4,3},{5,2},{6,1},{7,0},{8,15},{9,14},{10,... | collective-permute-start | bytes 968 | tf_op jit(solution)/shard_map/ppermute | solution.py:252
  78.5 2.4 %collective-permute-done.9.rest_2_ = s32[80]{0:T(128)S(1)} collective-permute-done((s32[80]{0:T(128)S(1)}, s32[80]{0:T(128)S(1)}, u32[]{:S(2)}, u32[]{:S(2)}) %collective-permute-start.9) | collective-permute-done | bytes 352 | tf_op jit(solution)/shard_map/ppermute | solution.py:252
  81.5 2.7 %collective-permute-done.10.rest_3_ = s32[80]{0:T(128)S(1)} collective-permute-done((s32[80]{0:T(128)S(1)}, s32[80]{0:T(128)S(1)}, u32[]{:S(2)}, u32[]{:S(2)}) %collective-permute-start.10) | collective-permute-done | bytes 352 | tf_op jit(solution)/shard_map/ppermute | solution.py:252
  85.0 1.5 collective-permute-done.11.rest_4_
  86.6 5.5 %shard_map.59 = (bf16[4,5,128,128]{3,2,1,0:T(8,128)(2,1)}, bf16[4,5,128,128]{3,2,1,0:T(8,128)(2,1)}, bf16[4,5,128,128]{3,2,1,0:T(8,128)(2,1)}, bf16[4,5,128,128]...) custom-call(s32[64]{0:T(128)S(1)} %reshape.268.code_ref, ...), custom_call_target="tpu_custom_call" | custom-call | bytes 8000000 | tf_op jit(solution)/shard_map/pallas_call | solution.py:117
  98.4 19.9 %shard_map.55.terms_ref = bf16[32,256,640]{2,1,0:T(8,128)(2,1)} custom-call(s32[64]{0:T(128)S(1)} %reshape.266.order_ref, s32[80]{0:T(128)S(1)} %reshape.267.comps_ref.rest_5_, bf16[16,5,128,128]{3,2,1,0:T(8,128)(2,1)} %own_l.1, bf16[16,5,128,128]{3,2,1,0:T(8,128)(2,1)} %collective-permute-done.other_l, bf16[64,128,128]{2,1,0:T(8,128)(2,1)S(1)} %bitcast.7, ...), custom_call_target="tpu_custom_call" | custom-call | flops 1342177280 | bytes 19485760 | tf_op jit(solution)/shard_map/pallas_call | solution.py:159
  118.3 2.8 %shard_map.65 = (bf16[4,128,128]{2,1,0:T(8,128)(2,1)S(1)}, bf16[4,128,128]{2,1,0:T(8,128)(2,1)S(1)}) custom-call(bf16[32,256,640]{2,1,0:T(8,128)(2,1)} %shard_map.55.terms_ref, bf16[4,5,128,128]{3,2,1,0:T(8,128)(2,1)S(1)} %copy-done.3), custom_call_target="tpu_custom_call" | custom-call | flops 167772160 | bytes 2359296 | tf_op jit(solution)/shard_map/pallas_call | solution.py:192
  121.1 2.8 %shard_map.57 = (bf16[4,128,128]{2,1,0:T(8,128)(2,1)S(1)}, bf16[4,128,128]{2,1,0:T(8,128)(2,1)S(1)}) custom-call(bf16[32,256,640]{2,1,0:T(8,128)(2,1)} %shard_map.55.terms_ref, bf16[4,5,128,128]{3,2,1,0:T(8,128)(2,1)S(1)} %collective-permute-done.5.right_ref), custom_call_target="tpu_custom_call" | custom-call | flops 167772160 | bytes 2359296 | tf_op jit(solution)/shard_map/pallas_call | solution.py:192
  123.9 2.8 %shard_map.58 = (bf16[4,128,128]{2,1,0:T(8,128)(2,1)S(1)}, bf16[4,128,128]{2,1,0:T(8,128)(2,1)S(1)}) custom-call(bf16[32,256,640]{2,1,0:T(8,128)(2,1)} %shard_map.55.terms_ref, bf16[4,5,128,128]{3,2,1,0:T(8,128)(2,1)S(1)} %collective-permute-done.6.right_ref), custom_call_target="tpu_custom_call" | custom-call | flops 167772160 | bytes 2359296 | tf_op jit(solution)/shard_map/pallas_call | solution.py:192
  126.7 10.6 %collective-permute-done.12.right_ref = bf16[4,5,128,128]{3,2,1,0:T(8,128)(2,1)} collective-permute-done((bf16[4,5,128,128]{3,2,1,0:T(8,128)(2,1)}, bf16[4,5,128,128]{3,2,1,0:T(8,128)(2,1)}, u32[]{:S(2)}, u32[]{:S(2)}) %collective-permute-start.12) | collective-permute-done | bytes 655392 | tf_op jit(solution)/shard_map/ppermute | solution.py:252
  137.3 2.0 %collective-permute-start.24 = (bf16[4,128,128]{2,1,0:T(8,128)(2,1)S(1)}, bf16[4,128,128]{2,1,0:T(8,128)(2,1)S(1)}, u32[]{:S(2)}, u32[]{:S(2)}) collective-permute-start(bf16[4,128,128]{2,1,0:T(8,128)(2,1)S(1)} %get-tuple-element.52), channel_id=1, source_target_pairs={{0,8},{8,0},{1,9},{9,1},{2,10},{10,2},{3,11},{11,3},{4,12},{12,4},... | collective-permute-start | bytes 393224 | tf_op jit(solution)/shard_map/ppermute | solution.py:271
  139.3 24.5 %collective-permute-done.13.right_ref = bf16[4,5,128,128]{3,2,1,0:T(8,128)(2,1)} collective-permute-done((bf16[4,5,128,128]{3,2,1,0:T(8,128)(2,1)}, bf16[4,5,128,128]{3,2,1,0:T(8,128)(2,1)}, u32[]{:S(2)}, u32[]{:S(2)}) %collective-permute-start.13) | collective-permute-done | bytes 655392 | tf_op jit(solution)/shard_map/ppermute | solution.py:252
  165.0 2.9 %shard_map.60 = (bf16[4,128,128]{2,1,0:T(8,128)(2,1)S(1)}, bf16[4,128,128]{2,1,0:T(8,128)(2,1)S(1)}) custom-call(bf16[32,256,640]{2,1,0:T(8,128)(2,1)} %shard_map.55.terms_ref, bf16[4,5,128,128]{3,2,1,0:T(8,128)(2,1)} %collective-permute-done.12.right_ref), custom_call_target="tpu_custom_call" | custom-call | flops 167772160 | bytes 2359296 | tf_op jit(solution)/shard_map/pallas_call | solution.py:192
  167.9 2.9 %shard_map.61 = (bf16[4,128,128]{2,1,0:T(8,128)(2,1)S(1)}, bf16[4,128,128]{2,1,0:T(8,128)(2,1)S(1)}) custom-call(bf16[32,256,640]{2,1,0:T(8,128)(2,1)} %shard_map.55.terms_ref, bf16[4,5,128,128]{3,2,1,0:T(8,128)(2,1)} %collective-permute-done.13.right_ref), custom_call_target="tpu_custom_call" | custom-call | flops 167772160 | bytes 2359296 | tf_op jit(solution)/shard_map/pallas_call | solution.py:192
  170.8 2.9 %shard_map.62 = (bf16[4,128,128]{2,1,0:T(8,128)(2,1)S(1)}, bf16[4,128,128]{2,1,0:T(8,128)(2,1)S(1)}) custom-call(bf16[32,256,640]{2,1,0:T(8,128)(2,1)} %shard_map.55.terms_ref, bf16[4,5,128,128]{3,2,1,0:T(8,128)(2,1)} %collective-permute-done.14.right_ref), custom_call_target="tpu_custom_call" | custom-call | flops 167772160 | bytes 2359296 | tf_op jit(solution)/shard_map/pallas_call | solution.py:192
  174.3 2.9 %shard_map.63 = (bf16[4,128,128]{2,1,0:T(8,128)(2,1)S(1)}, bf16[4,128,128]{2,1,0:T(8,128)(2,1)S(1)}) custom-call(bf16[32,256,640]{2,1,0:T(8,128)(2,1)} %shard_map.55.terms_ref, bf16[4,5,128,128]{3,2,1,0:T(8,128)(2,1)} %collective-permute-done.15.right_ref), custom_call_target="tpu_custom_call" | custom-call | flops 167772160 | bytes 2359296 | tf_op jit(solution)/shard_map/pallas_call | solution.py:192
  177.2 2.9 %shard_map.64 = (bf16[4,128,128]{2,1,0:T(8,128)(2,1)S(1)}, bf16[4,128,128]{2,1,0:T(8,128)(2,1)S(1)}) custom-call(bf16[32,256,640]{2,1,0:T(8,128)(2,1)} %shard_map.55.terms_ref, bf16[4,5,128,128]{3,2,1,0:T(8,128)(2,1)} %collective-permute-done.16.right_ref), custom_call_target="tpu_custom_call" | custom-call | flops 167772160 | bytes 2359296 | tf_op jit(solution)/shard_map/pallas_call | solution.py:192
  182.2 2.0 %shard_map.66 = bf16[64,128,128]{2,1,0:T(8,128)(2,1)} custom-call(s32[64]{0:T(128)S(1)} %reshape.266.order_ref, bf16[4,128,128]{2,1,0:T(8,128)(2,1)S(1)} %get-tuple-element.30.rest_0_, bf16[4,128,128]{2,1,0:T(8,128)(2,1)S(1)} %get-tuple-element.32.rest_1_, bf16[4,128,128]{2,1,0:T(8,128)(2,1)S(1)} %get-tuple-element.34.rest_2_, ...), custom_call_target="tpu_custom_call" | custom-call | bytes 4194304 | tf_op jit(solution)/shard_map/pallas_call | solution.py:229
  (69 shorter events, 21.6 us)
Async XLA Ops:
  0.0 9.2 %collective-permute-start.4 = (bf16[16,5,128,128]{3,2,1,0:T(8,128)(2,1)}, bf16[16,5,128,128]{3,2,1,0:T(8,128)(2,1)S(1)}, u32[]{:S(2)}, u32[]{:S(2)}) collective-permute-start(bf16[16,5,128,128]{3,2,1,0:T(8,128)(2,1)} %rest_6_.1), channel_id=1, source_target_pairs={{0,8},{8,0},{1,9},{9,1},{2,10},{10,2},{3,11},{11,3},{4,12},{12,4},... | collective-permute-start | bytes 7864328 | tf_op jit(solution)/shard_map/ppermute | solution.py:244
  0.7 94.7 %collective-permute-start = (bf16[16,5,128,128]{3,2,1,0:T(8,128)(2,1)}, bf16[16,5,128,128]{3,2,1,0:T(8,128)(2,1)}, u32[]{:S(2)}, u32[]{:S(2)}) collective-permute-start(bf16[16,5,128,128]{3,2,1,0:T(8,128)(2,1)} %own_l.1), channel_id=1, source_target_pairs={{0,8},{8,0},{1,9},{9,1},{2,10},{10,2},{3,11},{11,3},{4,12},{12,4},... | collective-permute-start | bytes 7864328 | tf_op jit(solution)/shard_map/ppermute | solution.py:265
  0.7 93.7 %collective-permute-start.1 = (bf16[64,128,128]{2,1,0:T(8,128)(2,1)}, bf16[64,128,128]{2,1,0:T(8,128)(2,1)}, u32[]{:S(2)}, u32[]{:S(2)}) collective-permute-start(bf16[64,128,128]{2,1,0:T(8,128)(2,1)} %bitcast.6), channel_id=1, source_target_pairs={{0,8},{8,0},{1,9},{9,1},{2,10},{10,2},{3,11},{11,3},{4,12},{12,4},... | collective-permute-start | bytes 6291464 | tf_op jit(solution)/shard_map/ppermute | solution.py:266
  2.6 4.9 %collective-permute-start.2 = (s32[80]{0:T(128)S(1)}, s32[80]{0:T(128)S(1)}, u32[]{:S(2)}, u32[]{:S(2)}) collective-permute-start(s32[80]{0:T(128)S(1)} %reshape.267.comps_ref.rest_5_), channel_id=1, source_target_pairs={{0,4},{1,5},{2,6},{3,7},{4,0},{5,1},{6,2},{7,3},{8,12},{9,13},{10,... | collective-permute-start | bytes 968 | tf_op jit(solution)/shard_map/ppermute | solution.py:252
  5.0 4.2 %collective-permute-start.3 = (s32[80]{0:T(128)S(1)}, s32[80]{0:T(128)S(1)}, u32[]{:S(2)}, u32[]{:S(2)}) collective-permute-start(s32[80]{0:T(128)S(1)} %reshape.267.comps_ref.rest_5_), channel_id=1, source_target_pairs={{0,5},{1,4},{2,7},{3,6},{4,1},{5,0},{6,3},{7,2},{8,13},{9,12},{10,... | collective-permute-start | bytes 968 | tf_op jit(solution)/shard_map/ppermute | solution.py:252
  15.7 81.1 %collective-permute-start.5 = (bf16[4,5,128,128]{3,2,1,0:T(8,128)(2,1)}, bf16[4,5,128,128]{3,2,1,0:T(8,128)(2,1)S(1)}, u32[]{:S(2)}, u32[]{:S(2)}) collective-permute-start(bf16[4,5,128,128]{3,2,1,0:T(8,128)(2,1)} %get-tuple-element.29), channel_id=1, source_target_pairs={{0,4},{1,5},{2,6},{3,7},{4,0},{5,1},{6,2},{7,3},{8,12},{9,13},{10,... | collective-permute-start | bytes 1966088 | tf_op jit(solution)/shard_map/ppermute | solution.py:252
  18.0 79.2 %collective-permute-start.6 = (bf16[4,5,128,128]{3,2,1,0:T(8,128)(2,1)}, bf16[4,5,128,128]{3,2,1,0:T(8,128)(2,1)S(1)}, u32[]{:S(2)}, u32[]{:S(2)}) collective-permute-start(bf16[4,5,128,128]{3,2,1,0:T(8,128)(2,1)} %get-tuple-element.31), channel_id=1, source_target_pairs={{0,5},{1,4},{2,7},{3,6},{4,1},{5,0},{6,3},{7,2},{8,13},{9,12},{10,... | collective-permute-start | bytes 1966088 | tf_op jit(solution)/shard_map/ppermute | solution.py:252
  19.0 55.8 %collective-permute-start.7 = (s32[80]{0:T(128)S(1)}, s32[80]{0:T(128)S(1)}, u32[]{:S(2)}, u32[]{:S(2)}) collective-permute-start(s32[80]{0:T(128)S(1)} %reshape.267.comps_ref.rest_5_), channel_id=1, source_target_pairs={{0,6},{1,7},{2,4},{3,5},{4,2},{5,3},{6,0},{7,1},{8,14},{9,15},{10,... | collective-permute-start | bytes 968 | tf_op jit(solution)/shard_map/ppermute | solution.py:252
  74.8 3.7 %collective-permute-start.8 = (s32[80]{0:T(128)S(1)}, s32[80]{0:T(128)S(1)}, u32[]{:S(2)}, u32[]{:S(2)}) collective-permute-start(s32[80]{0:T(128)S(1)} %reshape.267.comps_ref.rest_5_), channel_id=1, source_target_pairs={{0,7},{1,6},{2,5},{3,4},{4,3},{5,2},{6,1},{7,0},{8,15},{9,14},{10,... | collective-permute-start | bytes 968 | tf_op jit(solution)/shard_map/ppermute | solution.py:252
  78.5 2.4 %collective-permute-start.9 = (s32[80]{0:T(128)S(1)}, s32[80]{0:T(128)S(1)}, u32[]{:S(2)}, u32[]{:S(2)}) collective-permute-start(s32[80]{0:T(128)S(1)} %reshape.267.comps_ref.rest_5_), channel_id=1, source_target_pairs={{0,2},{1,3},{2,0},{3,1},{4,6},{5,7},{6,4},{7,5},{8,10},{9,11},{10,... | collective-permute-start | bytes 968 | tf_op jit(solution)/shard_map/ppermute | solution.py:252
  80.9 3.3 %collective-permute-start.10 = (s32[80]{0:T(128)S(1)}, s32[80]{0:T(128)S(1)}, u32[]{:S(2)}, u32[]{:S(2)}) collective-permute-start(s32[80]{0:T(128)S(1)} %reshape.267.comps_ref.rest_5_), channel_id=1, source_target_pairs={{0,3},{1,2},{2,1},{3,0},{4,7},{5,6},{6,5},{7,4},{8,11},{9,10},{10,... | collective-permute-start | bytes 968 | tf_op jit(solution)/shard_map/ppermute | solution.py:252
  84.2 2.4 %collective-permute-start.11 = (s32[80]{0:T(128)S(1)}, s32[80]{0:T(128)S(1)}, u32[]{:S(2)}, u32[]{:S(2)}) collective-permute-start(s32[80]{0:T(128)S(1)} %reshape.267.comps_ref.rest_5_), channel_id=1, source_target_pairs={{0,1},{1,0},{2,3},{3,2},{4,5},{5,4},{6,7},{7,6},{8,9},{9,8},{10,11... | collective-permute-start | bytes 968 | tf_op jit(solution)/shard_map/ppermute | solution.py:252
  93.0 44.3 %collective-permute-start.12 = (bf16[4,5,128,128]{3,2,1,0:T(8,128)(2,1)}, bf16[4,5,128,128]{3,2,1,0:T(8,128)(2,1)}, u32[]{:S(2)}, u32[]{:S(2)}) collective-permute-start(bf16[4,5,128,128]{3,2,1,0:T(8,128)(2,1)} %get-tuple-element.33), channel_id=1, source_target_pairs={{0,6},{1,7},{2,4},{3,5},{4,2},{5,3},{6,0},{7,1},{8,14},{9,15},{10,... | collective-permute-start | bytes 1966088 | tf_op jit(solution)/shard_map/ppermute | solution.py:252
  94.4 69.4 %collective-permute-start.13 = (bf16[4,5,128,128]{3,2,1,0:T(8,128)(2,1)}, bf16[4,5,128,128]{3,2,1,0:T(8,128)(2,1)}, u32[]{:S(2)}, u32[]{:S(2)}) collective-permute-start(bf16[4,5,128,128]{3,2,1,0:T(8,128)(2,1)} %get-tuple-element.35), channel_id=1, source_target_pairs={{0,7},{1,6},{2,5},{3,4},{4,3},{5,2},{6,1},{7,0},{8,15},{9,14},{10,... | collective-permute-start | bytes 1966088 | tf_op jit(solution)/shard_map/ppermute | solution.py:252
  95.3 69.7 %collective-permute-start.14 = (bf16[4,5,128,128]{3,2,1,0:T(8,128)(2,1)}, bf16[4,5,128,128]{3,2,1,0:T(8,128)(2,1)}, u32[]{:S(2)}, u32[]{:S(2)}) collective-permute-start(bf16[4,5,128,128]{3,2,1,0:T(8,128)(2,1)} %get-tuple-element.37), channel_id=1, source_target_pairs={{0,2},{1,3},{2,0},{3,1},{4,6},{5,7},{6,4},{7,5},{8,10},{9,11},{10,... | collective-permute-start | bytes 1966088 | tf_op jit(solution)/shard_map/ppermute | solution.py:252
  96.8 76.9 %collective-permute-start.15 = (bf16[4,5,128,128]{3,2,1,0:T(8,128)(2,1)}, bf16[4,5,128,128]{3,2,1,0:T(8,128)(2,1)}, u32[]{:S(2)}, u32[]{:S(2)}) collective-permute-start(bf16[4,5,128,128]{3,2,1,0:T(8,128)(2,1)} %get-tuple-element.39), channel_id=1, source_target_pairs={{0,3},{1,2},{2,1},{3,0},{4,7},{5,6},{6,5},{7,4},{8,11},{9,10},{10,... | collective-permute-start | bytes 1966088 | tf_op jit(solution)/shard_map/ppermute | solution.py:252
  97.2 79.9 %collective-permute-start.16 = (bf16[4,5,128,128]{3,2,1,0:T(8,128)(2,1)}, bf16[4,5,128,128]{3,2,1,0:T(8,128)(2,1)}, u32[]{:S(2)}, u32[]{:S(2)}) collective-permute-start(bf16[4,5,128,128]{3,2,1,0:T(8,128)(2,1)} %get-tuple-element.41), channel_id=1, source_target_pairs={{0,1},{1,0},{2,3},{3,2},{4,5},{5,4},{6,7},{7,6},{8,9},{9,8},{10,11... | collective-permute-start | bytes 1966088 | tf_op jit(solution)/shard_map/ppermute | solution.py:252
  137.3 42.8 %collective-permute-start.24 = (bf16[4,128,128]{2,1,0:T(8,128)(2,1)S(1)}, bf16[4,128,128]{2,1,0:T(8,128)(2,1)S(1)}, u32[]{:S(2)}, u32[]{:S(2)}) collective-permute-start(bf16[4,128,128]{2,1,0:T(8,128)(2,1)S(1)} %get-tuple-element.52), channel_id=1, source_target_pairs={{0,8},{8,0},{1,9},{9,1},{2,10},{10,2},{3,11},{11,3},{4,12},{12,4},... | collective-permute-start | bytes 393224 | tf_op jit(solution)/shard_map/ppermute | solution.py:271
  163.8 16.9 %collective-permute-start.17 = (bf16[4,128,128]{2,1,0:T(8,128)(2,1)S(1)}, bf16[4,128,128]{2,1,0:T(8,128)(2,1)S(1)}, u32[]{:S(2)}, u32[]{:S(2)}) collective-permute-start(bf16[4,128,128]{2,1,0:T(8,128)(2,1)S(1)} %get-tuple-element.45), channel_id=1, source_target_pairs={{0,8},{8,0},{1,9},{9,1},{2,10},{10,2},{3,11},{11,3},{4,12},{12,4},... | collective-permute-start | bytes 393224 | tf_op jit(solution)/shard_map/ppermute | solution.py:271
  165.0 15.8 %collective-permute-start.18 = (bf16[4,128,128]{2,1,0:T(8,128)(2,1)S(1)}, bf16[4,128,128]{2,1,0:T(8,128)(2,1)S(1)}, u32[]{:S(2)}, u32[]{:S(2)}) collective-permute-start(bf16[4,128,128]{2,1,0:T(8,128)(2,1)S(1)} %get-tuple-element.46), channel_id=1, source_target_pairs={{0,8},{8,0},{1,9},{9,1},{2,10},{10,2},{3,11},{11,3},{4,12},{12,4},... | collective-permute-start | bytes 393224 | tf_op jit(solution)/shard_map/ppermute | solution.py:271
  173.7 7.5 %collective-permute-start.19 = (bf16[4,128,128]{2,1,0:T(8,128)(2,1)S(1)}, bf16[4,128,128]{2,1,0:T(8,128)(2,1)S(1)}, u32[]{:S(2)}, u32[]{:S(2)}) collective-permute-start(bf16[4,128,128]{2,1,0:T(8,128)(2,1)S(1)} %get-tuple-element.47), channel_id=1, source_target_pairs={{0,8},{8,0},{1,9},{9,1},{2,10},{10,2},{3,11},{11,3},{4,12},{12,4},... | collective-permute-start | bytes 393224 | tf_op jit(solution)/shard_map/ppermute | solution.py:271
  177.1 4.1 %collective-permute-start.20 = (bf16[4,128,128]{2,1,0:T(8,128)(2,1)S(1)}, bf16[4,128,128]{2,1,0:T(8,128)(2,1)S(1)}, u32[]{:S(2)}, u32[]{:S(2)}) collective-permute-start(bf16[4,128,128]{2,1,0:T(8,128)(2,1)S(1)} %get-tuple-element.48), channel_id=1, source_target_pairs={{0,8},{8,0},{1,9},{9,1},{2,10},{10,2},{3,11},{11,3},{4,12},{12,4},... | collective-permute-start | bytes 393224 | tf_op jit(solution)/shard_map/ppermute | solution.py:271
  180.1 1.5 collective-permute-start.21
  180.8 1.4 collective-permute-start.23
  (6 other events, 38.8 us)

commit v3 on v2

v3 whole, which is shorter than its diff:
```python
import functools

import jax
import jax.numpy as jnp
from jax import lax
from jax.experimental import pallas as pl
from jax.experimental.pallas import tpu as pltpu
from jax.sharding import PartitionSpec as P

WACT = 5
MIB = 1024 * 1024
COST = 1000


def smem():
    return pl.BlockSpec(memory_space=pltpu.SMEM)


def vmem():
    return pl.BlockSpec(memory_space=pltpu.VMEM)


def hbm():
    return pl.BlockSpec(memory_space=pltpu.HBM)


class Plan:
    def __init__(self, wave, left_env, devices, cores):
        self.blocks, self.width = wave.shape[1], wave.shape[3]
        self.sectors, self.half = left_env.shape[0], left_env.shape[1]
        self.fan = self.blocks // self.sectors
        self.devices = devices
        self.cap = self.blocks // devices
        self.split = cores == 2 and self.cap % 2 == 0
        self.capc = self.cap // 2 if self.split else self.cap
        self.vectors = 2 if self.split else 1
        self.by_pairs = devices == 8
        if self.by_pairs:
            self.groups = [(0,), (6,), (7,), (1,), (2,), (4,), (3,), (5,)]
        else:
            self.groups = [tuple(range(devices))]

    def partner(self, p):
        return jnp.bitwise_xor(lax.axis_index("rows"), p) if self.by_pairs else jnp.int32(p)

    def rank0(self, core):
        return core * self.capc if self.split else 0


def lists(plan, right_slot):
    devices, blocks, cap, fan, sectors = plan.devices, plan.blocks, plan.cap, plan.fan, plan.sectors
    me = lax.axis_index("rows")
    slots = right_slot.reshape(devices, blocks)
    target = slots // blocks
    index = jnp.arange(blocks, dtype=jnp.int32)
    earlier = (target[:, None, :] == target[:, :, None]) & (index[None, None, :] < index[None, :, None])
    rank = jnp.sum(earlier.astype(jnp.int32), axis=2)
    ranks = jnp.arange(cap, dtype=jnp.int32)
    device = jnp.arange(devices, dtype=jnp.int32)
    value = (device[:, None] * sectors + index[None, :] // fan) * sectors + (slots % blocks) // fan
    hit = (target[:, None, :] == me) & (rank[:, None, :] == ranks[None, :, None])
    code = jnp.sum(jnp.where(hit, value[:, None, :], 0), axis=2)
    my_target = lax.dynamic_slice_in_dim(target, me, 1, axis=0)
    my_rank = lax.dynamic_slice_in_dim(rank, me, 1, axis=0)
    mine = (my_target[:, None, :] == device[:, None, None]) & (my_rank[:, None, :] == ranks[None, :, None])
    order = jnp.sum(jnp.where(mine, index[None, None, :], 0), axis=2)
    return order.astype(jnp.int32).reshape(-1), code.astype(jnp.int32).reshape(-1)


def decode(mask_ref, row, comps, found_ref):
    at = jnp.int32(0)
    for k in range(comps):
        found_ref[at] = jnp.int32(k)
        at = at + mask_ref[row, k]
    return [found_ref[j] for j in range(WACT)]


def each(count, step):
    if count <= 8:
        for s in range(count):
            step(s)
    else:
        pl.loop(0, count)(step)


def slot(plan, group, s):
    if len(group) == 1:
        return group[0], s
    return lax.div(s, plan.capc), lax.rem(s, plan.capc)


def send_kernel(plan, groups, where, masks, code_ref, *rest):
    mask_refs, (own_ref, other_ref) = rest[:masks], rest[masks : masks + 2]
    outs, (found, sem) = rest[masks + 2 : -2], rest[-2:]
    core = lax.axis_index("blk")
    for n, (group, (held, first), out) in enumerate(zip(groups, where, outs)):
        mask_ref = mask_refs[held]

        def step(s):
            p, q = slot(plan, group, s)
            code = code_ref[plan.partner(p) * plan.cap + plan.rank0(core) + q]
            sector = lax.rem(code, plan.sectors)
            row = lax.div(code, plan.sectors)
            if len(group) == 1:
                row = first * plan.sectors + lax.rem(row, plan.sectors)
            for j, k in enumerate(decode(mask_ref, row, 2 * plan.half, found)):
                mine = lax.div(k, plan.half) == core
                at = lax.rem(k, plan.half)

                @pl.when(mine)
                def _():
                    pltpu.make_async_copy(own_ref.at[sector, at], out.at[s, j], sem.at[n]).start()

                @pl.when(jnp.logical_not(mine))
                def _():
                    pltpu.make_async_copy(other_ref.at[sector, at], out.at[s, j], sem.at[n]).start()

        each(len(group) * plan.capc, step)
    for n, out in enumerate(outs):
        pltpu.make_async_copy(out, out, sem.at[n]).wait()


def send(plan, groups, where, code, masks, own, other):
    w, left_comps = plan.width, 2 * plan.half
    return pl.pallas_call(
        functools.partial(send_kernel, plan, groups, where, len(masks)),
        out_shape=[jax.ShapeDtypeStruct((len(g) * plan.capc, WACT, w, w), own.dtype) for g in groups],
        in_specs=[smem()] + [smem() for _ in masks] + [hbm(), hbm()],
        out_specs=[vmem() for _ in groups],
        scratch_shapes=[pltpu.SMEM((left_comps + 1,), jnp.int32), pltpu.SemaphoreType.DMA((len(groups),))],
        compiler_params=pltpu.CompilerParams(vmem_limit_bytes=58 * MIB),
        cost_estimate=pl.CostEstimate(flops=0, bytes_accessed=8_000_000, transcendentals=0),
    )(code, *masks, own, other)


def product_kernel(plan, late, order_ref, mask_ref, own_l, other_l, *rest):
    waves, outs, (left, psi, sem, found) = rest[: plan.vectors], rest[plan.vectors : -4], rest[-4:]
    core = lax.axis_index("blk")
    s = pl.program_id(0)
    w = plan.width

    @pl.when(s == 0)
    def _():
        copies = [
            pltpu.make_async_copy(own_l, left.at[:, pl.ds(core * plan.half, plan.half)], sem.at[0]),
            pltpu.make_async_copy(other_l, left.at[:, pl.ds((1 - core) * plan.half, plan.half)], sem.at[1]),
        ]
        for v in range(plan.vectors):
            copies.append(pltpu.make_async_copy(waves[v], psi.at[v], sem.at[2 + v]))
        for c in copies:
            c.start()
        for c in copies:
            c.wait()

    p, q = lax.div(s, plan.capc), lax.rem(s, plan.capc)
    b = order_ref[plan.partner(p) * plan.cap + plan.rank0(core) + q]
    sector = lax.div(b, plan.fan)
    lhs = jnp.concatenate([left[sector, k] for k in decode(mask_ref, sector, 2 * plan.half, found)], axis=0)
    rhs = jnp.concatenate([psi[v, b] for v in range(plan.vectors)], axis=1)
    terms = jnp.dot(lhs, rhs, preferred_element_type=jnp.float32).astype(jnp.bfloat16)

    def store(out_ref, at):
        for j in range(WACT):
            for v in range(plan.vectors):
                out_ref[at, pl.ds(v * w, w), pl.ds(j * w, w)] = terms[j * w : (j + 1) * w, v * w : (v + 1) * w]

    store(outs[0], 0)
    if late is not None:
        pl.when(p == late)(lambda: store(outs[1], q))


def products(plan, late, order, term_mask, own_l, other_l, waves):
    w, slots = plan.width, plan.devices * plan.capc
    tall, wide = plan.vectors * w, WACT * w
    shapes = [jax.ShapeDtypeStruct((slots, tall, wide), jnp.bfloat16)]
    specs = [pl.BlockSpec((1, tall, wide), lambda s: (s, 0, 0))]
    if late is not None:
        shapes.append(jax.ShapeDtypeStruct((plan.capc, tall, wide), jnp.bfloat16))
        specs.append(pl.BlockSpec((plan.capc, tall, wide), lambda s: (0, 0, 0)))
    return pl.pallas_call(
        functools.partial(product_kernel, plan, late),
        grid=(slots,),
        out_shape=shapes,
        in_specs=[smem(), smem(), hbm(), hbm()] + [hbm() for _ in waves],
        out_specs=specs,
        scratch_shapes=[
            pltpu.VMEM((plan.sectors, 2 * plan.half, w, w), jnp.bfloat16),
            pltpu.VMEM((plan.vectors, plan.blocks, w, w), jnp.bfloat16),
            pltpu.SemaphoreType.DMA((2 + plan.vectors,)),
            pltpu.SMEM((2 * plan.half + 1,), jnp.int32),
        ],
        compiler_params=pltpu.CompilerParams(vmem_limit_bytes=20 * MIB),
        cost_estimate=pl.CostEstimate(flops=COST, bytes_accessed=COST, transcendentals=0),
    )(order, term_mask, own_l, other_l, *waves)


def contract_kernel(plan, terms_ref, right_ref, *outs):
    w = plan.width

    def step(s):
        right = jnp.concatenate([right_ref[s, j] for j in range(WACT)], axis=1)
        done = lax.dot_general(
            terms_ref[s], right, (((1,), (1,)), ((), ())), preferred_element_type=jnp.float32
        ).astype(jnp.bfloat16)
        for v in range(plan.vectors):
            outs[v][s] = done[v * w : (v + 1) * w]

    each(terms_ref.shape[0], step)


def contract(plan, group, terms, right):
    w, count = plan.width, len(group) * plan.capc
    block = min(count, 4)
    first = 0 if terms.shape[0] == count else group[0] * plan.capc // block
    return pl.pallas_call(
        functools.partial(contract_kernel, plan),
        grid=(count // block,),
        out_shape=[jax.ShapeDtypeStruct((count, w, w), jnp.bfloat16) for _ in range(plan.vectors)],
        in_specs=[
            pl.BlockSpec((block, plan.vectors * w, WACT * w), lambda s: (first + s, 0, 0)),
            pl.BlockSpec((block, WACT, w, w), lambda s: (s, 0, 0, 0)),
        ],
        out_specs=[pl.BlockSpec((block, w, w), lambda s: (s, 0, 0)) for _ in range(plan.vectors)],
        compiler_params=pltpu.CompilerParams(vmem_limit_bytes=8 * MIB),
        cost_estimate=pl.CostEstimate(flops=COST, bytes_accessed=COST, transcendentals=0),
    )(terms, right)


def place_kernel(plan, groups, order_ref, *rest):
    n = len(groups)
    parts, out_ref = rest[:-1], rest[-1]
    core = lax.axis_index("blk")
    for v in range(plan.vectors):
        whose = core if v == 0 else 1 - core
        for g, group in enumerate(groups):
            part = parts[v * n + g]

            def step(s):
                p, q = slot(plan, group, s)
                b = order_ref[plan.partner(p) * plan.cap + plan.rank0(whose) + q]
                out_ref[b] = part[s]

            each(len(group) * plan.capc, step)


def place(plan, groups, order, parts):
    w = plan.width
    return pl.pallas_call(
        functools.partial(place_kernel, plan, groups),
        out_shape=jax.ShapeDtypeStruct((plan.blocks, w, w), jnp.bfloat16),
        in_specs=[smem()] + [vmem() for _ in parts],
        out_specs=vmem(),
        compiler_params=pltpu.CompilerParams(vmem_limit_bytes=16 * MIB),
        cost_estimate=pl.CostEstimate(flops=COST, bytes_accessed=COST, transcendentals=0),
    )(order, *parts)


def place_last_kernel(plan, group, order_ref, *rest):
    parts, out_ref, sem = rest[: plan.vectors], rest[-2], rest[-1]
    core = lax.axis_index("blk")
    for wait in (False, True):
        for v in range(plan.vectors):
            whose = core if v == 0 else 1 - core
            for s in range(plan.capc):
                b = order_ref[plan.partner(group[0]) * plan.cap + plan.rank0(whose) + s]
                copy = pltpu.make_async_copy(parts[v].at[s], out_ref.at[b], sem.at[v * plan.capc + s])
                if wait:
                    copy.wait()
                else:
                    copy.start()


def place_last(plan, group, order, parts, result):
    return pl.pallas_call(
        functools.partial(place_last_kernel, plan, group),
        out_shape=jax.ShapeDtypeStruct(result.shape, result.dtype),
        in_specs=[smem()] + [vmem() for _ in parts] + [hbm()],
        out_specs=hbm(),
        scratch_shapes=[pltpu.SemaphoreType.DMA((plan.vectors * plan.capc,))],
        input_output_aliases={1 + plan.vectors: 0},
        compiler_params=pltpu.CompilerParams(vmem_limit_bytes=4 * MIB),
        cost_estimate=pl.CostEstimate(flops=0, bytes_accessed=1_000_000, transcendentals=0),
    )(order, *parts, result)


def body(wave, left_env, right_env, right_slot, term_mask):
    devices = lax.axis_size("rows")
    plan = Plan(wave, left_env, devices, lax.axis_size("blk"))
    swap = functools.partial(lax.ppermute, axis_name="blk", perm=[(0, 1), (1, 0)])

    other_r = swap(right_env)
    order, code = lists(plan, right_slot)
    groups = plan.groups

    def meet(x, group):
        if group == (0,):
            return x
        return lax.ppermute(x, "rows", [(i, i ^ group[0]) for i in range(devices)])

    everyone = functools.partial(lax.all_to_all, axis_name="rows", split_axis=0, concat_axis=0, tiled=True)
    rows, comps = term_mask.shape
    if plan.by_pairs:
        pair = jnp.concatenate([term_mask, meet(term_mask, (1,))])
        quad = jnp.concatenate([pair, meet(pair, (6,))])
        near = meet(quad, (2,))
        urgent = [(6,), (7,)]
        made = dict(zip(urgent, send(plan, urgent, [(0, 2), (0, 3)], code, [quad], right_env, other_r)))
        code, made[(6,)] = lax.optimization_barrier((code, made[(6,)]))
        others = [(1,), (2,), (4,), (3,), (5,), (0,)]
        where = [(0, 1), (1, 0), (1, 2), (1, 1), (1, 3), (0, 0)]
        made.update(zip(others, send(plan, others, where, code, [quad, near], right_env, other_r)))
        after = {(5,): (6,)}
        arrived = {}
        for g in groups:
            x = made[g]
            if g in after:
                x, arrived[after[g]] = lax.optimization_barrier((x, arrived[after[g]]))
            arrived[g] = meet(x, g)
        right = [arrived[g] for g in groups]
    else:
        wide = jnp.broadcast_to(term_mask[None], (devices, rows, comps)).reshape(-1, comps)
        sent = send(plan, groups, [(0, 0)], code, [everyone(wide)], right_env, other_r)
        right = [everyone(sent[0])]

    other_l = swap(left_env)
    waves = [wave[0]] + ([swap(wave[0])] if plan.split else [])
    last = groups[-1]
    terms = products(plan, last[0] if plan.by_pairs else None, order, term_mask, left_env, other_l, waves)

    def finish(n):
        mine = terms[1] if plan.by_pairs and n == len(groups) - 1 else terms[0]
        part = list(contract(plan, groups[n], mine, right[n]))
        return [part[0], swap(part[1])] if plan.split else part

    if not plan.by_pairs:
        return place(plan, groups, order, finish(0))[None]
    parts = [finish(n) for n in range(len(groups) - 1)]
    result = place(plan, groups[:-1], order, [part[v] for v in range(plan.vectors) for part in parts])
    result, right[-1] = lax.optimization_barrier((result, right[-1]))
    return place_last(plan, last, order, finish(len(groups) - 1), result)[None]


def solution(mesh):
    in_specs = (
        P("blk", ("parts", "rows"), None, None),
        P(("parts", "rows"), "blk", None, None),
        P(("parts", "rows"), "blk", None, None),
        P("parts"),
        P(("parts", "rows"), None),
    )
    out_specs = P("blk", ("parts", "rows"), None, None)
    return jax.shard_map(body, mesh=mesh, in_specs=in_specs, out_specs=out_specs, check_vma=False)
```

time: 185 us -> 137 us (0.74)
  the two profiles are of different devices: /device:TPU:9 before, /device:TPU:0 now
where the time goes in v3:
time: 137 us; the launch traced here: 136 us
  starting transfers between devices  49.3 us (36%)
  waiting for transfers between devices  42.4 us (31%)
  Pallas kernels  34.7 us (25%)
  local copies, waits for them, and re-layouts  8 us (6%)
  other arithmetic  1.57 us (1%)
    ppermute x10, starting transfers between devices, meet(): return lax.ppermute(x, 'rows', [(i, i ^ group[0]) for i in range(devices)])  46.4 us
    ppermute x10, waiting for transfers between devices, meet(): return lax.ppermute(x, 'rows', [(i, i ^ group[0]) for i in range(devices)])  39.8 us
    pallas_call x1, Pallas kernels, products(): pl.pallas_call(functools.partial(product_kernel, plan, late), grid=(slots...  12.1 us
    pallas_call x2, Pallas kernels, send(): pl.pallas_call(functools.partial(send_kernel, plan, groups, where, len(ma...  9.83 us
    pallas_call x8, Pallas kernels, contract(): pl.pallas_call(functools.partial(contract_kernel, plan), grid=(count // b...  9.5 us
    unnamed x20, local copies, waits for them, and re-layouts  6.5 us
  transfers between devices with their start and end apart: 21, of which 7 were waited for; matrix products, arithmetic and copies ran while one was open for 3% of the time, Pallas kernels for 24%

profile of v3, /device:TPU:0, one launch (start us, length us, event | category | flops | bytes accessed | tf_op | source)
XLA Modules:
  0.0 136.2 jit_solution(14908612306133192496)
XLA Ops:
  1.0 2.5 %collective-permute-start.2 = (s32[16,10]{1,0:T(8,128)}, s32[16,10]{1,0:T(8,128)S(1)}, u32[]{:S(2)}, u32[]{:S(2)}) collective-permute-start(s32[16,10]{1,0:T(8,128)} %mask_ref.1), channel_id=1, source_target_pairs={{0,1},{1,0},{2,3},{3,2},{4,5},{5,4},{6,7},{7,6},{8,9},{9,8},{10,11... | collective-permute-start | bytes 1928 | tf_op jit(solution)/shard_map/ppermute | solution.py:298
  3.5 0.8 reshape.245
  7.0 3.6 %collective-permute-start.3 = (s32[32,10]{1,0:T(8,128)S(1)}, s32[32,10]{1,0:T(8,128)S(1)}, u32[]{:S(2)}, u32[]{:S(2)}) collective-permute-start(s32[32,10]{1,0:T(8,128)S(1)} %pad_add_fusion), channel_id=1, source_target_pairs={{0,6},{1,7},{2,4},{3,5},{4,2},{5,3},{6,0},{7,1},{8,14},{9,15},{10,... | collective-permute-start | bytes 3848 | tf_op jit(solution)/shard_map/ppermute | solution.py:298
  10.6 1.9 %collective-permute-done.3 = s32[32,10]{1,0:T(8,128)S(1)} collective-permute-done((s32[32,10]{1,0:T(8,128)S(1)}, s32[32,10]{1,0:T(8,128)S(1)}, u32[]{:S(2)}, u32[]{:S(2)}) %collective-permute-start.3) | collective-permute-done | bytes 1312 | tf_op jit(solution)/shard_map/ppermute | solution.py:298
  13.1 1.5 %copy-done.6 = bf16[16,5,128,128]{3,2,1,0:T(8,128)(2,1)} copy-done((bf16[16,5,128,128]{3,2,1,0:T(8,128)(2,1)}, bf16[16,5,128,128]{3,2,1,0:T(8,128)(2,1)S(1)}, u32[]{:S(2)}) %copy-start.6) | copy-done | bytes 2621464
  14.7 3.7 %shard_map.56 = (bf16[4,5,128,128]{3,2,1,0:T(8,128)(2,1)}, bf16[4,5,128,128]{3,2,1,0:T(8,128)(2,1)}) custom-call(s32[64]{0:T(128)} %reshape.247.code_ref, s32[64,10]{1,0:T(8,128)} %copy-done.7, bf16[16,5,128,128]{3,2,1,0:T(8,128)(2,1)} %rest_2_.1, bf16[16,5,128,128]{3,2,1,0:T(8,128)(2,1)} %copy-done.6), custom_call_target="tpu_custom_call" | custom-call | bytes 8000000 | tf_op jit(solution)/shard_map/pallas_call | solution.py:125
  18.4 3.7 %collective-permute-start.6 = (bf16[4,5,128,128]{3,2,1,0:T(8,128)(2,1)}, bf16[4,5,128,128]{3,2,1,0:T(8,128)(2,1)S(1)}, u32[]{:S(2)}, u32[]{:S(2)}) collective-permute-start(bf16[4,5,128,128]{3,2,1,0:T(8,128)(2,1)} %get-tuple-element.44), channel_id=1, source_target_pairs={{0,6},{1,7},{2,4},{3,5},{4,2},{5,3},{6,0},{7,1},{8,14},{9,15},{10,... | collective-permute-start | bytes 1966088 | tf_op jit(solution)/shard_map/ppermute | solution.py:298
  22.8 28.4 %collective-permute-done.5.rest_1_ = s32[64,10]{1,0:T(8,128)S(1)} collective-permute-done((s32[64,10]{1,0:T(8,128)}, s32[64,10]{1,0:T(8,128)S(1)}, u32[]{:S(2)}, u32[]{:S(2)}) %collective-permute-start.5) | collective-permute-done | bytes 2592 | tf_op jit(solution)/shard_map/ppermute | solution.py:298
  51.8 6.1 %shard_map.57 = (bf16[4,5,128,128]{3,2,1,0:T(8,128)(2,1)}, bf16[4,5,128,128]{3,2,1,0:T(8,128)(2,1)}, bf16[4,5,128,128]{3,2,1,0:T(8,128)(2,1)}, bf16[4,5,128,128]...) custom-call(s32[64]{0:T(128)} %reshape.247.code_ref, s32[64,10]{1,0:T(8,128)} %copy-done.7, ...), custom_call_target="tpu_custom_call" | custom-call | bytes 8000000 | tf_op jit(solution)/shard_map/pallas_call | solution.py:125
  58.4 1.7 %collective-permute-start.9 = (bf16[4,5,128,128]{3,2,1,0:T(8,128)(2,1)}, bf16[4,5,128,128]{3,2,1,0:T(8,128)(2,1)}, u32[]{:S(2)}, u32[]{:S(2)}) collective-permute-start(bf16[4,5,128,128]{3,2,1,0:T(8,128)(2,1)} %get-tuple-element.51), channel_id=1, source_target_pairs={{0,2},{1,3},{2,0},{3,1},{4,6},{5,7},{6,4},{7,5},{8,10},{9,11},{10,... | collective-permute-start | bytes 1966088 | tf_op jit(solution)/shard_map/ppermute | solution.py:298
  60.1 0.9 copy-done.2
  61.0 5.1 %collective-permute-start.10 = (bf16[4,5,128,128]{3,2,1,0:T(8,128)(2,1)}, bf16[4,5,128,128]{3,2,1,0:T(8,128)(2,1)}, u32[]{:S(2)}, u32[]{:S(2)}) collective-permute-start(bf16[4,5,128,128]{3,2,1,0:T(8,128)(2,1)} %get-tuple-element.53), channel_id=1, source_target_pairs={{0,4},{1,5},{2,6},{3,7},{4,0},{5,1},{6,2},{7,3},{8,12},{9,13},{10,... | collective-permute-start | bytes 1966088 | tf_op jit(solution)/shard_map/ppermute | solution.py:298
  66.2 28.5 %collective-permute-start.19 = (bf16[4,5,128,128]{3,2,1,0:T(8,128)(2,1)}, bf16[4,5,128,128]{3,2,1,0:T(8,128)(2,1)S(1)}, u32[]{:S(2)}, u32[]{:S(2)}) collective-permute-start(bf16[4,5,128,128]{3,2,1,0:T(8,128)(2,1)} %get-tuple-element.64), channel_id=1, source_target_pairs={{0,5},{1,4},{2,7},{3,6},{4,1},{5,0},{6,3},{7,2},{8,13},{9,12},{10,... | collective-permute-start | bytes 1966088 | tf_op jit(solution)/shard_map/ppermute | solution.py:298
  95.0 1.6 %copy-done.1 = bf16[1,64,128,128]{3,2,1,0:T(8,128)(2,1)S(1)} copy-done((bf16[1,64,128,128]{3,2,1,0:T(8,128)(2,1)S(1)}, bf16[1,64,128,128]{3,2,1,0:T(8,128)(2,1)}, u32[]{:S(2)}) %copy-start.1) | copy-done | bytes 2097176
  96.6 12.1 %shard_map.55 = (bf16[32,256,640]{2,1,0:T(8,128)(2,1)S(1)}, bf16[4,256,640]{2,1,0:T(8,128)(2,1)S(1)}) custom-call(s32[64]{0:T(128)S(1)} %reshape.246.order_ref, s32[16,10]{1,0:T(8,128)S(1)} %copy-done.5, bf16[16,5,128,128]{3,2,1,0:T(8,128)(2,1)S(1)} %copy-done, bf16[16,5,128,128]{3,2,1,0:T(8,128)(2,1)} %collective-permute-done.other_l, ...), custom_call_target="tpu_custom_call" | custom-call | flops 1000 | bytes 1000 | tf_op jit(solution)/shard_map/pallas_call | solution.py:180
  110.3 1.6 %shard_map.60 = (bf16[4,128,128]{2,1,0:T(8,128)(2,1)S(1)}, bf16[4,128,128]{2,1,0:T(8,128)(2,1)S(1)}) custom-call(bf16[32,256,640]{2,1,0:T(8,128)(2,1)S(1)} %get-tuple-element.38.terms_ref, bf16[4,5,128,128]{3,2,1,0:T(8,128)(2,1)} %collective-permute-done.7.right_ref), custom_call_target="tpu_custom_call" | custom-call | flops 1000 | bytes 1000 | tf_op jit(solution)/shard_map/pallas_call | solution.py:215
  112.6 1.6 %shard_map.61 = (bf16[4,128,128]{2,1,0:T(8,128)(2,1)S(1)}, bf16[4,128,128]{2,1,0:T(8,128)(2,1)S(1)}) custom-call(bf16[32,256,640]{2,1,0:T(8,128)(2,1)S(1)} %get-tuple-element.38.terms_ref, bf16[4,5,128,128]{3,2,1,0:T(8,128)(2,1)} %collective-permute-done.8.right_ref), custom_call_target="tpu_custom_call" | custom-call | flops 1000 | bytes 1000 | tf_op jit(solution)/shard_map/pallas_call | solution.py:215
  114.2 1.6 %shard_map.62 = (bf16[4,128,128]{2,1,0:T(8,128)(2,1)S(1)}, bf16[4,128,128]{2,1,0:T(8,128)(2,1)S(1)}) custom-call(bf16[32,256,640]{2,1,0:T(8,128)(2,1)S(1)} %get-tuple-element.38.terms_ref, bf16[4,5,128,128]{3,2,1,0:T(8,128)(2,1)} %collective-permute-done.9.right_ref), custom_call_target="tpu_custom_call" | custom-call | flops 1000 | bytes 1000 | tf_op jit(solution)/shard_map/pallas_call | solution.py:215
  115.8 1.6 %shard_map.63 = (bf16[4,128,128]{2,1,0:T(8,128)(2,1)S(1)}, bf16[4,128,128]{2,1,0:T(8,128)(2,1)S(1)}) custom-call(bf16[32,256,640]{2,1,0:T(8,128)(2,1)S(1)} %get-tuple-element.38.terms_ref, bf16[4,5,128,128]{3,2,1,0:T(8,128)(2,1)} %collective-permute-done.10.right_ref), custom_call_target="tpu_custom_call" | custom-call | flops 1000 | bytes 1000 | tf_op jit(solution)/shard_map/pallas_call | solution.py:215
  117.9 1.6 %shard_map.64 = (bf16[4,128,128]{2,1,0:T(8,128)(2,1)S(1)}, bf16[4,128,128]{2,1,0:T(8,128)(2,1)S(1)}) custom-call(bf16[32,256,640]{2,1,0:T(8,128)(2,1)S(1)} %get-tuple-element.38.terms_ref, bf16[4,5,128,128]{3,2,1,0:T(8,128)(2,1)} %collective-permute-done.11.right_ref), custom_call_target="tpu_custom_call" | custom-call | flops 1000 | bytes 1000 | tf_op jit(solution)/shard_map/pallas_call | solution.py:215
  121.5 2.0 %shard_map.65.rest_2_ = bf16[64,128,128]{2,1,0:T(8,128)(2,1)} custom-call(s32[64]{0:T(128)S(1)} %reshape.246.order_ref, bf16[4,128,128]{2,1,0:T(8,128)(2,1)S(1)} %get-tuple-element.42.rest_0_, bf16[4,128,128]{2,1,0:T(8,128)(2,1)S(1)} %get-tuple-element.46.rest_1_, bf16[4,128,128]{2,1,0:T(8,128)(2,1)S(1)} %get-tuple-element.48.rest_2_, ...), custom_call_target="tpu_custom_call" | custom-call | flops 1000 | bytes 1000 | tf_op jit(solution)/shard_map/pallas_call | solution.py:248
  123.4 9.5 %collective-permute-done.19.right_ref = bf16[4,5,128,128]{3,2,1,0:T(8,128)(2,1)S(1)} collective-permute-done((bf16[4,5,128,128]{3,2,1,0:T(8,128)(2,1)}, bf16[4,5,128,128]{3,2,1,0:T(8,128)(2,1)S(1)}, u32[]{:S(2)}, u32[]{:S(2)}) %collective-permute-start.19) | collective-permute-done | bytes 655392 | tf_op jit(solution)/shard_map/ppermute | solution.py:298
  133.5 1.3 collective-permute-done.20.rest_1_
  134.9 1.3 shard_map.67
  (67 shorter events, 11.8 us)
Async XLA Ops:
  0.0 12.5 %collective-permute-start.4 = (bf16[16,5,128,128]{3,2,1,0:T(8,128)(2,1)}, bf16[16,5,128,128]{3,2,1,0:T(8,128)(2,1)S(1)}, u32[]{:S(2)}, u32[]{:S(2)}) collective-permute-start(bf16[16,5,128,128]{3,2,1,0:T(8,128)(2,1)} %rest_2_.1), channel_id=1, source_target_pairs={{0,8},{8,0},{1,9},{9,1},{2,10},{10,2},{3,11},{11,3},{4,12},{12,4},... | collective-permute-start | bytes 7864328 | tf_op jit(solution)/shard_map/ppermute | solution.py:291
  0.5 65.6 %collective-permute-start = (bf16[16,5,128,128]{3,2,1,0:T(8,128)(2,1)}, bf16[16,5,128,128]{3,2,1,0:T(8,128)(2,1)}, u32[]{:S(2)}, u32[]{:S(2)}) collective-permute-start(bf16[16,5,128,128]{3,2,1,0:T(8,128)(2,1)} %own_l.1), channel_id=1, source_target_pairs={{0,8},{8,0},{1,9},{9,1},{2,10},{10,2},{3,11},{11,3},{4,12},{12,4},... | collective-permute-start | bytes 7864328 | tf_op jit(solution)/shard_map/ppermute | solution.py:325
  0.5 57.9 %collective-permute-start.1 = (bf16[64,128,128]{2,1,0:T(8,128)(2,1)}, bf16[64,128,128]{2,1,0:T(8,128)(2,1)}, u32[]{:S(2)}, u32[]{:S(2)}) collective-permute-start(bf16[64,128,128]{2,1,0:T(8,128)(2,1)} %bitcast.6), channel_id=1, source_target_pairs={{0,8},{8,0},{1,9},{9,1},{2,10},{10,2},{3,11},{11,3},{4,12},{12,4},... | collective-permute-start | bytes 6291464 | tf_op jit(solution)/shard_map/ppermute | solution.py:326
  1.0 5.3 %collective-permute-start.2 = (s32[16,10]{1,0:T(8,128)}, s32[16,10]{1,0:T(8,128)S(1)}, u32[]{:S(2)}, u32[]{:S(2)}) collective-permute-start(s32[16,10]{1,0:T(8,128)} %mask_ref.1), channel_id=1, source_target_pairs={{0,1},{1,0},{2,3},{3,2},{4,5},{5,4},{6,7},{7,6},{8,9},{9,8},{10,11... | collective-permute-start | bytes 1928 | tf_op jit(solution)/shard_map/ppermute | solution.py:298
  7.0 5.5 %collective-permute-start.3 = (s32[32,10]{1,0:T(8,128)S(1)}, s32[32,10]{1,0:T(8,128)S(1)}, u32[]{:S(2)}, u32[]{:S(2)}) collective-permute-start(s32[32,10]{1,0:T(8,128)S(1)} %pad_add_fusion), channel_id=1, source_target_pairs={{0,6},{1,7},{2,4},{3,5},{4,2},{5,3},{6,0},{7,1},{8,14},{9,15},{10,... | collective-permute-start | bytes 3848 | tf_op jit(solution)/shard_map/ppermute | solution.py:298
  18.4 41.7 %collective-permute-start.6 = (bf16[4,5,128,128]{3,2,1,0:T(8,128)(2,1)}, bf16[4,5,128,128]{3,2,1,0:T(8,128)(2,1)S(1)}, u32[]{:S(2)}, u32[]{:S(2)}) collective-permute-start(bf16[4,5,128,128]{3,2,1,0:T(8,128)(2,1)} %get-tuple-element.44), channel_id=1, source_target_pairs={{0,6},{1,7},{2,4},{3,5},{4,2},{5,3},{6,0},{7,1},{8,14},{9,15},{10,... | collective-permute-start | bytes 1966088 | tf_op jit(solution)/shard_map/ppermute | solution.py:298
  22.1 44.1 %collective-permute-start.7 = (bf16[4,5,128,128]{3,2,1,0:T(8,128)(2,1)}, bf16[4,5,128,128]{3,2,1,0:T(8,128)(2,1)}, u32[]{:S(2)}, u32[]{:S(2)}) collective-permute-start(bf16[4,5,128,128]{3,2,1,0:T(8,128)(2,1)} %get-tuple-element.47), channel_id=1, source_target_pairs={{0,7},{1,6},{2,5},{3,4},{4,3},{5,2},{6,1},{7,0},{8,15},{9,14},{10,... | collective-permute-start | bytes 1966088 | tf_op jit(solution)/shard_map/ppermute | solution.py:298
  22.8 28.4 %collective-permute-start.5 = (s32[64,10]{1,0:T(8,128)}, s32[64,10]{1,0:T(8,128)S(1)}, u32[]{:S(2)}, u32[]{:S(2)}) collective-permute-start(s32[64,10]{1,0:T(8,128)} %copy-done.7), channel_id=1, source_target_pairs={{0,2},{1,3},{2,0},{3,1},{4,6},{5,7},{6,4},{7,5},{8,10},{9,11},{10,... | collective-permute-start | bytes 7688 | tf_op jit(solution)/shard_map/ppermute | solution.py:298
  22.8 72.2 %copy-start = (bf16[16,5,128,128]{3,2,1,0:T(8,128)(2,1)S(1)}, bf16[16,5,128,128]{3,2,1,0:T(8,128)(2,1)}, u32[]{:S(2)}) copy-start(bf16[16,5,128,128]{3,2,1,0:T(8,128)(2,1)} %own_l.1) | copy-start | bytes 7864324
  22.8 72.2 %copy-start.5 = (s32[16,10]{1,0:T(8,128)S(1)}, s32[16,10]{1,0:T(8,128)}, u32[]{:S(2)}) copy-start(s32[16,10]{1,0:T(8,128)} %mask_ref.1) | copy-start | bytes 1924
  57.9 54.0 %collective-permute-start.8 = (bf16[4,5,128,128]{3,2,1,0:T(8,128)(2,1)}, bf16[4,5,128,128]{3,2,1,0:T(8,128)(2,1)}, u32[]{:S(2)}, u32[]{:S(2)}) collective-permute-start(bf16[4,5,128,128]{3,2,1,0:T(8,128)(2,1)} %get-tuple-element.49), channel_id=1, source_target_pairs={{0,1},{1,0},{2,3},{3,2},{4,5},{5,4},{6,7},{7,6},{8,9},{9,8},{10,11... | collective-permute-start | bytes 1966088 | tf_op jit(solution)/shard_map/ppermute | solution.py:298
  58.4 53.6 %collective-permute-start.9 = (bf16[4,5,128,128]{3,2,1,0:T(8,128)(2,1)}, bf16[4,5,128,128]{3,2,1,0:T(8,128)(2,1)}, u32[]{:S(2)}, u32[]{:S(2)}) collective-permute-start(bf16[4,5,128,128]{3,2,1,0:T(8,128)(2,1)} %get-tuple-element.51), channel_id=1, source_target_pairs={{0,2},{1,3},{2,0},{3,1},{4,6},{5,7},{6,4},{7,5},{8,10},{9,11},{10,... | collective-permute-start | bytes 1966088 | tf_op jit(solution)/shard_map/ppermute | solution.py:298
  61.0 51.5 %collective-permute-start.10 = (bf16[4,5,128,128]{3,2,1,0:T(8,128)(2,1)}, bf16[4,5,128,128]{3,2,1,0:T(8,128)(2,1)}, u32[]{:S(2)}, u32[]{:S(2)}) collective-permute-start(bf16[4,5,128,128]{3,2,1,0:T(8,128)(2,1)} %get-tuple-element.53), channel_id=1, source_target_pairs={{0,4},{1,5},{2,6},{3,7},{4,0},{5,1},{6,2},{7,3},{8,12},{9,13},{10,... | collective-permute-start | bytes 1966088 | tf_op jit(solution)/shard_map/ppermute | solution.py:298
  66.1 51.3 %collective-permute-start.11 = (bf16[4,5,128,128]{3,2,1,0:T(8,128)(2,1)}, bf16[4,5,128,128]{3,2,1,0:T(8,128)(2,1)}, u32[]{:S(2)}, u32[]{:S(2)}) collective-permute-start(bf16[4,5,128,128]{3,2,1,0:T(8,128)(2,1)} %get-tuple-element.55), channel_id=1, source_target_pairs={{0,3},{1,2},{2,1},{3,0},{4,7},{5,6},{6,5},{7,4},{8,11},{9,10},{10,... | collective-permute-start | bytes 1966088 | tf_op jit(solution)/shard_map/ppermute | solution.py:298
  66.2 66.7 %collective-permute-start.19 = (bf16[4,5,128,128]{3,2,1,0:T(8,128)(2,1)}, bf16[4,5,128,128]{3,2,1,0:T(8,128)(2,1)S(1)}, u32[]{:S(2)}, u32[]{:S(2)}) collective-permute-start(bf16[4,5,128,128]{3,2,1,0:T(8,128)(2,1)} %get-tuple-element.64), channel_id=1, source_target_pairs={{0,5},{1,4},{2,7},{3,6},{4,1},{5,0},{6,3},{7,2},{8,13},{9,12},{10,... | collective-permute-start | bytes 1966088 | tf_op jit(solution)/shard_map/ppermute | solution.py:298
  96.6 12.1 %copy-start.4 = (bf16[4,5,128,128]{3,2,1,0:T(8,128)(2,1)S(1)}, bf16[4,5,128,128]{3,2,1,0:T(8,128)(2,1)}, u32[]{:S(2)}) copy-start(bf16[4,5,128,128]{3,2,1,0:T(8,128)(2,1)} %get-tuple-element.41.right_ref) | copy-start | bytes 1966084
  111.9 7.6 %collective-permute-start.12 = (bf16[4,128,128]{2,1,0:T(8,128)(2,1)S(1)}, bf16[4,128,128]{2,1,0:T(8,128)(2,1)S(1)}, u32[]{:S(2)}, u32[]{:S(2)}) collective-permute-start(bf16[4,128,128]{2,1,0:T(8,128)(2,1)S(1)} %get-tuple-element.57), channel_id=1, source_target_pairs={{0,8},{8,0},{1,9},{9,1},{2,10},{10,2},{3,11},{11,3},{4,12},{12,4},... | collective-permute-start | bytes 393224 | tf_op jit(solution)/shard_map/ppermute | solution.py:333
  112.0 7.7 %collective-permute-start.13 = (bf16[4,128,128]{2,1,0:T(8,128)(2,1)S(1)}, bf16[4,128,128]{2,1,0:T(8,128)(2,1)S(1)}, u32[]{:S(2)}, u32[]{:S(2)}) collective-permute-start(bf16[4,128,128]{2,1,0:T(8,128)(2,1)S(1)} %get-tuple-element.58), channel_id=1, source_target_pairs={{0,8},{8,0},{1,9},{9,1},{2,10},{10,2},{3,11},{11,3},{4,12},{12,4},... | collective-permute-start | bytes 393224 | tf_op jit(solution)/shard_map/ppermute | solution.py:333
  112.5 7.6 %collective-permute-start.14 = (bf16[4,128,128]{2,1,0:T(8,128)(2,1)S(1)}, bf16[4,128,128]{2,1,0:T(8,128)(2,1)S(1)}, u32[]{:S(2)}, u32[]{:S(2)}) collective-permute-start(bf16[4,128,128]{2,1,0:T(8,128)(2,1)S(1)} %get-tuple-element.59), channel_id=1, source_target_pairs={{0,8},{8,0},{1,9},{9,1},{2,10},{10,2},{3,11},{11,3},{4,12},{12,4},... | collective-permute-start | bytes 393224 | tf_op jit(solution)/shard_map/ppermute | solution.py:333
  117.4 2.8 %collective-permute-start.15 = (bf16[4,128,128]{2,1,0:T(8,128)(2,1)S(1)}, bf16[4,128,128]{2,1,0:T(8,128)(2,1)S(1)}, u32[]{:S(2)}, u32[]{:S(2)}) collective-permute-start(bf16[4,128,128]{2,1,0:T(8,128)(2,1)S(1)} %get-tuple-element.60), channel_id=1, source_target_pairs={{0,8},{8,0},{1,9},{9,1},{2,10},{10,2},{3,11},{11,3},{4,12},{12,4},... | collective-permute-start | bytes 393224 | tf_op jit(solution)/shard_map/ppermute | solution.py:333
  119.5 1.4 %collective-permute-start.16 = (bf16[4,128,128]{2,1,0:T(8,128)(2,1)S(1)}, bf16[4,128,128]{2,1,0:T(8,128)(2,1)S(1)}, u32[]{:S(2)}, u32[]{:S(2)}) collective-permute-start(bf16[4,128,128]{2,1,0:T(8,128)(2,1)S(1)} %get-tuple-element.61), channel_id=1, source_target_pairs={{0,8},{8,0},{1,9},{9,1},{2,10},{10,2},{3,11},{11,3},{4,12},{12,4},... | collective-permute-start | bytes 393224 | tf_op jit(solution)/shard_map/ppermute | solution.py:333
  119.7 1.4 %collective-permute-start.17 = (bf16[4,128,128]{2,1,0:T(8,128)(2,1)S(1)}, bf16[4,128,128]{2,1,0:T(8,128)(2,1)S(1)}, u32[]{:S(2)}, u32[]{:S(2)}) collective-permute-start(bf16[4,128,128]{2,1,0:T(8,128)(2,1)S(1)} %get-tuple-element.62), channel_id=1, source_target_pairs={{0,8},{8,0},{1,9},{9,1},{2,10},{10,2},{3,11},{11,3},{4,12},{12,4},... | collective-permute-start | bytes 393224 | tf_op jit(solution)/shard_map/ppermute | solution.py:333
  120.1 1.3 collective-permute-start.18
  133.5 1.4 %collective-permute-start.20 = (bf16[4,128,128]{2,1,0:T(8,128)(2,1)S(1)}, bf16[4,128,128]{2,1,0:T(8,128)(2,1)S(1)}, u32[]{:S(2)}, u32[]{:S(2)}) collective-permute-start(bf16[4,128,128]{2,1,0:T(8,128)(2,1)S(1)} %get-tuple-element.67), channel_id=1, source_target_pairs={{0,8},{8,0},{1,9},{9,1},{2,10},{10,2},{3,11},{11,3},{4,12},{12,4},... | collective-permute-start | bytes 393224 | tf_op jit(solution)/shard_map/ppermute | solution.py:333
  (6 other events, 6.3 us)

commit v4 on v3

--- a/solution.py
+++ b/solution.py
@@ -300,16 +300,16 @@
     everyone = functools.partial(lax.all_to_all, axis_name="rows", split_axis=0, concat_axis=0, tiled=True)
     rows, comps = term_mask.shape
     if plan.by_pairs:
-        pair = jnp.concatenate([term_mask, meet(term_mask, (1,))])
-        quad = jnp.concatenate([pair, meet(pair, (6,))])
+        far = [meet(term_mask, (6,)), meet(term_mask, (7,))]
+        quad = jnp.concatenate([term_mask, meet(term_mask, (1,)), *far])
         near = meet(quad, (2,))
         urgent = [(6,), (7,)]
-        made = dict(zip(urgent, send(plan, urgent, [(0, 2), (0, 3)], code, [quad], right_env, other_r)))
-        code, made[(6,)] = lax.optimization_barrier((code, made[(6,)]))
+        made = dict(zip(urgent, send(plan, urgent, [(0, 0), (1, 0)], code, far, right_env, other_r)))
+        code, left_env, wave, made[(6,)] = lax.optimization_barrier((code, left_env, wave, made[(6,)]))
         others = [(1,), (2,), (4,), (3,), (5,), (0,)]
         where = [(0, 1), (1, 0), (1, 2), (1, 1), (1, 3), (0, 0)]
         made.update(zip(others, send(plan, others, where, code, [quad, near], right_env, other_r)))
-        after = {(5,): (6,)}
+        after = {(5,): (6,), (1,): (7,)}
         arrived = {}
         for g in groups:
             x = made[g]

time: 137 us -> 134 us (0.978)
  waiting for transfers between devices: 42.4 us -> 48.1 us
  starting transfers between devices: 49.3 us -> 43.6 us
  local copies, waits for them, and re-layouts: 8 us -> 4.89 us
    ppermute x10 -> x11, waiting for transfers between devices: 39.8 us -> 45.7 us  [meet(): return lax.ppermute(x, 'rows', [(i, i ^ group[0]) for i in range(devices)])]
    ppermute x10 -> x11, starting transfers between devices: 46.4 us -> 40.7 us  [meet(): return lax.ppermute(x, 'rows', [(i, i ^ group[0]) for i in range(devices)])]
    unnamed x20 -> x21, local copies, waits for them, and re-layouts: 6.5 us -> 2.77 us
  transfers between devices with their start and end apart: 21 -> 22, of which waited for: 7 -> 9; matrix products, arithmetic and copies ran while one was open for 3% -> 3% of each run, Pallas kernels for 24% -> 22%
where the time goes in v4:
time: 134 us; the launch traced here: 133 us
  waiting for transfers between devices  48.1 us (36%)
  starting transfers between devices  43.6 us (33%)
  Pallas kernels  35.1 us (26%)
  local copies, waits for them, and re-layouts  4.89 us (4%)
    ppermute x11, waiting for transfers between devices, meet(): return lax.ppermute(x, 'rows', [(i, i ^ group[0]) for i in range(devices)])  45.7 us
    ppermute x11, starting transfers between devices, meet(): return lax.ppermute(x, 'rows', [(i, i ^ group[0]) for i in range(devices)])  40.7 us
    pallas_call x1, Pallas kernels, products(): pl.pallas_call(functools.partial(product_kernel, plan, late), grid=(slots...  12.7 us
    pallas_call x8, Pallas kernels, contract(): pl.pallas_call(functools.partial(contract_kernel, plan), grid=(count // b...  9.59 us
    pallas_call x2, Pallas kernels, send(): pl.pallas_call(functools.partial(send_kernel, plan, groups, where, len(ma...  9.54 us
    unnamed x21, local copies, waits for them, and re-layouts  2.77 us
  transfers between devices with their start and end apart: 22, of which 9 were waited for; matrix products, arithmetic and copies ran while one was open for 3% of the time, Pallas kernels for 22%

profile of v4, /device:TPU:0, one launch (start us, length us, event | category | flops | bytes accessed | tf_op | source)
XLA Modules:
  0.0 132.9 jit_solution(5245413060268966302)
XLA Ops:
  0.5 4.6 %collective-permute-start = (s32[16,10]{1,0:T(8,128)}, s32[16,10]{1,0:T(8,128)S(1)}, u32[]{:S(2)}, u32[]{:S(2)}) collective-permute-start(s32[16,10]{1,0:T(8,128)} %mask_ref.1), channel_id=1, source_target_pairs={{0,6},{1,7},{2,4},{3,5},{4,2},{5,3},{6,0},{7,1},{8,14},{9,15},{10,... | collective-permute-start | bytes 1928 | tf_op jit(solution)/shard_map/ppermute | solution.py:298
  5.1 1.2 collective-permute-start.1
  6.2 0.8 reshape.245
  8.2 3.4 %collective-permute-done.1.rest_1_ = s32[16,10]{1,0:T(8,128)S(1)} collective-permute-done((s32[16,10]{1,0:T(8,128)}, s32[16,10]{1,0:T(8,128)S(1)}, u32[]{:S(2)}, u32[]{:S(2)}) %collective-permute-start.1) | collective-permute-done | bytes 672 | tf_op jit(solution)/shard_map/ppermute | solution.py:298
  12.2 3.4 %shard_map.55 = (bf16[4,5,128,128]{3,2,1,0:T(8,128)(2,1)}, bf16[4,5,128,128]{3,2,1,0:T(8,128)(2,1)}) custom-call(s32[64]{0:T(128)} %reshape.247.code_ref, s32[16,10]{1,0:T(8,128)} %copy-done.7, s32[16,10]{1,0:T(8,128)} %copy-done.8, bf16[16,5,128,128]{3,2,1,0:T(8,128)(2,1)} %rest_2_.3, bf16[16,5,128,128]{3,2,1,0:T(8,128)(2,1)} %collective-permute-done.2.rest_3_), custom_call_target="tpu_custom_call" | custom-call | bytes 8000000 | tf_op jit(solution)/shard_map/pallas_call | solution.py:125
  16.2 1.2 collective-permute-start.8
  17.4 3.6 %collective-permute-start.7 = (bf16[4,5,128,128]{3,2,1,0:T(8,128)(2,1)}, bf16[4,5,128,128]{3,2,1,0:T(8,128)(2,1)}, u32[]{:S(2)}, u32[]{:S(2)}) collective-permute-start(bf16[4,5,128,128]{3,2,1,0:T(8,128)(2,1)} %get-tuple-element.50), channel_id=1, source_target_pairs={{0,6},{1,7},{2,4},{3,5},{4,2},{5,3},{6,0},{7,1},{8,14},{9,15},{10,... | collective-permute-start | bytes 1966088 | tf_op jit(solution)/shard_map/ppermute | solution.py:298
  21.5 7.4 %collective-permute-done.5 = s32[16,10]{1,0:T(8,128)S(1)} collective-permute-done((s32[16,10]{1,0:T(8,128)S(1)}, s32[16,10]{1,0:T(8,128)S(1)}, u32[]{:S(2)}, u32[]{:S(2)}) %collective-permute-start.5) | collective-permute-done | bytes 672 | tf_op jit(solution)/shard_map/ppermute | solution.py:298
  28.9 0.7 constant_dynamic-update-slice_fusion.1
  30.3 20.5 %collective-permute-done.6.rest_1_ = s32[64,10]{1,0:T(8,128)S(1)} collective-permute-done((s32[64,10]{1,0:T(8,128)S(1)}, s32[64,10]{1,0:T(8,128)S(1)}, u32[]{:S(2)}, u32[]{:S(2)}) %collective-permute-start.6) | collective-permute-done | bytes 2592 | tf_op jit(solution)/shard_map/ppermute | solution.py:298
  51.4 6.1 %shard_map.57 = (bf16[4,5,128,128]{3,2,1,0:T(8,128)(2,1)}, bf16[4,5,128,128]{3,2,1,0:T(8,128)(2,1)}, bf16[4,5,128,128]{3,2,1,0:T(8,128)(2,1)}, bf16[4,5,128,128]...) custom-call(s32[64]{0:T(128)} %reshape.247.code_ref, s32[64,10]{1,0:T(8,128)} %copy-done.5, ...), custom_call_target="tpu_custom_call" | custom-call | bytes 8000000 | tf_op jit(solution)/shard_map/pallas_call | solution.py:125
  57.6 0.9 copy-done.1
  58.5 3.1 %collective-permute-start.11 = (bf16[4,5,128,128]{3,2,1,0:T(8,128)(2,1)}, bf16[4,5,128,128]{3,2,1,0:T(8,128)(2,1)}, u32[]{:S(2)}, u32[]{:S(2)}) collective-permute-start(bf16[4,5,128,128]{3,2,1,0:T(8,128)(2,1)} %get-tuple-element.61), channel_id=1, source_target_pairs={{0,4},{1,5},{2,6},{3,7},{4,0},{5,1},{6,2},{7,3},{8,12},{9,13},{10,... | collective-permute-start | bytes 1966088 | tf_op jit(solution)/shard_map/ppermute | solution.py:298
  61.5 26.4 %collective-permute-start.10 = (bf16[4,5,128,128]{3,2,1,0:T(8,128)(2,1)}, bf16[4,5,128,128]{3,2,1,0:T(8,128)(2,1)}, u32[]{:S(2)}, u32[]{:S(2)}) collective-permute-start(bf16[4,5,128,128]{3,2,1,0:T(8,128)(2,1)} %get-tuple-element.59), channel_id=1, source_target_pairs={{0,2},{1,3},{2,0},{3,1},{4,6},{5,7},{6,4},{7,5},{8,10},{9,11},{10,... | collective-permute-start | bytes 1966088 | tf_op jit(solution)/shard_map/ppermute | solution.py:298
  88.4 12.7 %shard_map.56 = (bf16[32,256,640]{2,1,0:T(8,128)(2,1)S(1)}, bf16[4,256,640]{2,1,0:T(8,128)(2,1)S(1)}) custom-call(s32[64]{0:T(128)S(1)} %reshape.246.order_ref, s32[16,10]{1,0:T(8,128)S(1)} %copy-done.4, bf16[16,5,128,128]{3,2,1,0:T(8,128)(2,1)S(1)} %copy-done, bf16[16,5,128,128]{3,2,1,0:T(8,128)(2,1)} %collective-permute-done.3.other_l, ...), custom_call_target="tpu_custom_call" | custom-call | flops 1000 | bytes 1000 | tf_op jit(solution)/shard_map/pallas_call | solution.py:180
  101.1 1.6 %shard_map.64 = (bf16[4,128,128]{2,1,0:T(8,128)(2,1)S(1)}, bf16[4,128,128]{2,1,0:T(8,128)(2,1)S(1)}) custom-call(bf16[32,256,640]{2,1,0:T(8,128)(2,1)S(1)} %get-tuple-element.45.terms_ref, bf16[4,5,128,128]{3,2,1,0:T(8,128)(2,1)} %collective-permute-done.12.right_ref), custom_call_target="tpu_custom_call" | custom-call | flops 1000 | bytes 1000 | tf_op jit(solution)/shard_map/pallas_call | solution.py:215
  102.8 13.8 %collective-permute-done.11.right_ref = bf16[4,5,128,128]{3,2,1,0:T(8,128)(2,1)} collective-permute-done((bf16[4,5,128,128]{3,2,1,0:T(8,128)(2,1)}, bf16[4,5,128,128]{3,2,1,0:T(8,128)(2,1)}, u32[]{:S(2)}, u32[]{:S(2)}) %collective-permute-start.11) | collective-permute-done | bytes 655392 | tf_op jit(solution)/shard_map/ppermute | solution.py:298
  116.6 1.6 %shard_map.63 = (bf16[4,128,128]{2,1,0:T(8,128)(2,1)S(1)}, bf16[4,128,128]{2,1,0:T(8,128)(2,1)S(1)}) custom-call(bf16[32,256,640]{2,1,0:T(8,128)(2,1)S(1)} %get-tuple-element.45.terms_ref, bf16[4,5,128,128]{3,2,1,0:T(8,128)(2,1)} %collective-permute-done.11.right_ref), custom_call_target="tpu_custom_call" | custom-call | flops 1000 | bytes 1000 | tf_op jit(solution)/shard_map/pallas_call | solution.py:215
  118.3 1.6 %shard_map.62 = (bf16[4,128,128]{2,1,0:T(8,128)(2,1)S(1)}, bf16[4,128,128]{2,1,0:T(8,128)(2,1)S(1)}) custom-call(bf16[32,256,640]{2,1,0:T(8,128)(2,1)S(1)} %get-tuple-element.45.terms_ref, bf16[4,5,128,128]{3,2,1,0:T(8,128)(2,1)} %collective-permute-done.10.right_ref), custom_call_target="tpu_custom_call" | custom-call | flops 1000 | bytes 1000 | tf_op jit(solution)/shard_map/pallas_call | solution.py:215
  120.5 1.6 %shard_map.61 = (bf16[4,128,128]{2,1,0:T(8,128)(2,1)S(1)}, bf16[4,128,128]{2,1,0:T(8,128)(2,1)S(1)}) custom-call(bf16[32,256,640]{2,1,0:T(8,128)(2,1)S(1)} %get-tuple-element.45.terms_ref, bf16[4,5,128,128]{3,2,1,0:T(8,128)(2,1)} %collective-permute-done.9.right_ref), custom_call_target="tpu_custom_call" | custom-call | flops 1000 | bytes 1000 | tf_op jit(solution)/shard_map/pallas_call | solution.py:215
  122.8 1.7 %shard_map.59 = (bf16[4,128,128]{2,1,0:T(8,128)(2,1)S(1)}, bf16[4,128,128]{2,1,0:T(8,128)(2,1)S(1)}) custom-call(bf16[32,256,640]{2,1,0:T(8,128)(2,1)S(1)} %get-tuple-element.45.terms_ref, bf16[4,5,128,128]{3,2,1,0:T(8,128)(2,1)} %collective-permute-done.7.right_ref), custom_call_target="tpu_custom_call" | custom-call | flops 1000 | bytes 1000 | tf_op jit(solution)/shard_map/pallas_call | solution.py:215
  127.0 2.0 %shard_map.65.rest_2_ = bf16[64,128,128]{2,1,0:T(8,128)(2,1)} custom-call(s32[64]{0:T(128)S(1)} %reshape.246.order_ref, bf16[4,128,128]{2,1,0:T(8,128)(2,1)S(1)} %get-tuple-element.48.rest_0_, bf16[4,128,128]{2,1,0:T(8,128)(2,1)S(1)} %get-tuple-element.52.rest_1_, bf16[4,128,128]{2,1,0:T(8,128)(2,1)S(1)} %get-tuple-element.56.rest_2_, ...), custom_call_target="tpu_custom_call" | custom-call | flops 1000 | bytes 1000 | tf_op jit(solution)/shard_map/pallas_call | solution.py:248
  130.2 1.3 %collective-permute-done.21.rest_1_ = bf16[4,128,128]{2,1,0:T(8,128)(2,1)S(1)} collective-permute-done((bf16[4,128,128]{2,1,0:T(8,128)(2,1)S(1)}, bf16[4,128,128]{2,1,0:T(8,128)(2,1)S(1)}, u32[]{:S(2)}, u32[]{:S(2)}) %collective-permute-start.21) | collective-permute-done | bytes 131104 | tf_op jit(solution)/shard_map/ppermute | solution.py:333
  131.6 1.3 shard_map.67
  (69 shorter events, 10.3 us)
Async XLA Ops:
  0.0 11.6 %collective-permute-start.2 = (bf16[16,5,128,128]{3,2,1,0:T(8,128)(2,1)}, bf16[16,5,128,128]{3,2,1,0:T(8,128)(2,1)}, u32[]{:S(2)}, u32[]{:S(2)}) collective-permute-start(bf16[16,5,128,128]{3,2,1,0:T(8,128)(2,1)} %rest_2_.3), channel_id=1, source_target_pairs={{0,8},{8,0},{1,9},{9,1},{2,10},{10,2},{3,11},{11,3},{4,12},{12,4},... | collective-permute-start | bytes 7864328 | tf_op jit(solution)/shard_map/ppermute | solution.py:291
  0.5 7.8 %collective-permute-start = (s32[16,10]{1,0:T(8,128)}, s32[16,10]{1,0:T(8,128)S(1)}, u32[]{:S(2)}, u32[]{:S(2)}) collective-permute-start(s32[16,10]{1,0:T(8,128)} %mask_ref.1), channel_id=1, source_target_pairs={{0,6},{1,7},{2,4},{3,5},{4,2},{5,3},{6,0},{7,1},{8,14},{9,15},{10,... | collective-permute-start | bytes 1928 | tf_op jit(solution)/shard_map/ppermute | solution.py:298
  5.1 6.6 %collective-permute-start.1 = (s32[16,10]{1,0:T(8,128)}, s32[16,10]{1,0:T(8,128)S(1)}, u32[]{:S(2)}, u32[]{:S(2)}) collective-permute-start(s32[16,10]{1,0:T(8,128)} %mask_ref.1), channel_id=1, source_target_pairs={{0,7},{1,6},{2,5},{3,4},{4,3},{5,2},{6,1},{7,0},{8,15},{9,14},{10,... | collective-permute-start | bytes 1928 | tf_op jit(solution)/shard_map/ppermute | solution.py:298
  8.2 12.8 %copy-start.4 = (s32[16,10]{1,0:T(8,128)S(1)}, s32[16,10]{1,0:T(8,128)}, u32[]{:S(2)}) copy-start(s32[16,10]{1,0:T(8,128)} %mask_ref.1) | copy-start | bytes 1924
  15.7 72.4 %collective-permute-start.3 = (bf16[16,5,128,128]{3,2,1,0:T(8,128)(2,1)S(1)}, bf16[16,5,128,128]{3,2,1,0:T(8,128)(2,1)}, u32[]{:S(2)}, u32[]{:S(2)}) collective-permute-start(bf16[16,5,128,128]{3,2,1,0:T(8,128)(2,1)S(1)} %copy-done), channel_id=1, source_target_pairs={{0,8},{8,0},{1,9},{9,1},{2,10},{10,2},{3,11},{11,3},{4,12},{12,4},... | collective-permute-start | bytes 7864328 | tf_op jit(solution)/shard_map/ppermute | solution.py:325
  15.7 72.2 %collective-permute-start.4 = (bf16[64,128,128]{2,1,0:T(8,128)(2,1)}, bf16[64,128,128]{2,1,0:T(8,128)(2,1)}, u32[]{:S(2)}, u32[]{:S(2)}) collective-permute-start(bf16[64,128,128]{2,1,0:T(8,128)(2,1)} %bitcast.2.rest_0_), channel_id=1, source_target_pairs={{0,8},{8,0},{1,9},{9,1},{2,10},{10,2},{3,11},{11,3},{4,12},{12,4},... | collective-permute-start | bytes 6291464 | tf_op jit(solution)/shard_map/ppermute | solution.py:326
  16.2 41.4 %collective-permute-start.8 = (bf16[4,5,128,128]{3,2,1,0:T(8,128)(2,1)}, bf16[4,5,128,128]{3,2,1,0:T(8,128)(2,1)S(1)}, u32[]{:S(2)}, u32[]{:S(2)}) collective-permute-start(bf16[4,5,128,128]{3,2,1,0:T(8,128)(2,1)} %get-tuple-element.54), channel_id=1, source_target_pairs={{0,7},{1,6},{2,5},{3,4},{4,3},{5,2},{6,1},{7,0},{8,15},{9,14},{10,... | collective-permute-start | bytes 1966088 | tf_op jit(solution)/shard_map/ppermute | solution.py:298
  17.4 44.1 %collective-permute-start.7 = (bf16[4,5,128,128]{3,2,1,0:T(8,128)(2,1)}, bf16[4,5,128,128]{3,2,1,0:T(8,128)(2,1)}, u32[]{:S(2)}, u32[]{:S(2)}) collective-permute-start(bf16[4,5,128,128]{3,2,1,0:T(8,128)(2,1)} %get-tuple-element.50), channel_id=1, source_target_pairs={{0,6},{1,7},{2,4},{3,5},{4,2},{5,3},{6,0},{7,1},{8,14},{9,15},{10,... | collective-permute-start | bytes 1966088 | tf_op jit(solution)/shard_map/ppermute | solution.py:298
  21.0 7.9 %collective-permute-start.5 = (s32[16,10]{1,0:T(8,128)S(1)}, s32[16,10]{1,0:T(8,128)S(1)}, u32[]{:S(2)}, u32[]{:S(2)}) collective-permute-start(s32[16,10]{1,0:T(8,128)S(1)} %copy-done.4), channel_id=1, source_target_pairs={{0,1},{1,0},{2,3},{3,2},{4,5},{5,4},{6,7},{7,6},{8,9},{9,8},{10,11... | collective-permute-start | bytes 1928 | tf_op jit(solution)/shard_map/ppermute | solution.py:298
  30.3 20.5 %copy-start.5 = (s32[64,10]{1,0:T(8,128)}, s32[64,10]{1,0:T(8,128)S(1)}, u32[]{:S(2)}) copy-start(s32[64,10]{1,0:T(8,128)S(1)} %constant_dynamic-update-slice_fusion.rest_0_) | copy-start | bytes 7684
  30.3 20.5 %collective-permute-start.6 = (s32[64,10]{1,0:T(8,128)S(1)}, s32[64,10]{1,0:T(8,128)S(1)}, u32[]{:S(2)}, u32[]{:S(2)}) collective-permute-start(s32[64,10]{1,0:T(8,128)S(1)} %constant_dynamic-update-slice_fusion.rest_0_), channel_id=1, source_target_pairs={{0,2},{1,3},{2,0},{3,1},{4,6},{5,7},{6,4},{7,5},{8,10},{9,11},{10,... | collective-permute-start | bytes 7688 | tf_op jit(solution)/shard_map/ppermute | solution.py:298
  57.5 43.6 %collective-permute-start.12 = (bf16[4,5,128,128]{3,2,1,0:T(8,128)(2,1)}, bf16[4,5,128,128]{3,2,1,0:T(8,128)(2,1)}, u32[]{:S(2)}, u32[]{:S(2)}) collective-permute-start(bf16[4,5,128,128]{3,2,1,0:T(8,128)(2,1)} %get-tuple-element.63), channel_id=1, source_target_pairs={{0,3},{1,2},{2,1},{3,0},{4,7},{5,6},{6,5},{7,4},{8,11},{9,10},{10,... | collective-permute-start | bytes 1966088 | tf_op jit(solution)/shard_map/ppermute | solution.py:298
  58.5 58.1 %collective-permute-start.11 = (bf16[4,5,128,128]{3,2,1,0:T(8,128)(2,1)}, bf16[4,5,128,128]{3,2,1,0:T(8,128)(2,1)}, u32[]{:S(2)}, u32[]{:S(2)}) collective-permute-start(bf16[4,5,128,128]{3,2,1,0:T(8,128)(2,1)} %get-tuple-element.61), channel_id=1, source_target_pairs={{0,4},{1,5},{2,6},{3,7},{4,0},{5,1},{6,2},{7,3},{8,12},{9,13},{10,... | collective-permute-start | bytes 1966088 | tf_op jit(solution)/shard_map/ppermute | solution.py:298
  61.5 56.8 %collective-permute-start.10 = (bf16[4,5,128,128]{3,2,1,0:T(8,128)(2,1)}, bf16[4,5,128,128]{3,2,1,0:T(8,128)(2,1)}, u32[]{:S(2)}, u32[]{:S(2)}) collective-permute-start(bf16[4,5,128,128]{3,2,1,0:T(8,128)(2,1)} %get-tuple-element.59), channel_id=1, source_target_pairs={{0,2},{1,3},{2,0},{3,1},{4,6},{5,7},{6,4},{7,5},{8,10},{9,11},{10,... | collective-permute-start | bytes 1966088 | tf_op jit(solution)/shard_map/ppermute | solution.py:298
  87.9 32.6 %collective-permute-start.9 = (bf16[4,5,128,128]{3,2,1,0:T(8,128)(2,1)}, bf16[4,5,128,128]{3,2,1,0:T(8,128)(2,1)}, u32[]{:S(2)}, u32[]{:S(2)}) collective-permute-start(bf16[4,5,128,128]{3,2,1,0:T(8,128)(2,1)} %get-tuple-element.57), channel_id=1, source_target_pairs={{0,1},{1,0},{2,3},{3,2},{4,5},{5,4},{6,7},{7,6},{8,9},{9,8},{10,11... | collective-permute-start | bytes 1966088 | tf_op jit(solution)/shard_map/ppermute | solution.py:298
  88.0 41.6 %collective-permute-start.20 = (bf16[4,5,128,128]{3,2,1,0:T(8,128)(2,1)}, bf16[4,5,128,128]{3,2,1,0:T(8,128)(2,1)S(1)}, u32[]{:S(2)}, u32[]{:S(2)}) collective-permute-start(bf16[4,5,128,128]{3,2,1,0:T(8,128)(2,1)} %get-tuple-element.72), channel_id=1, source_target_pairs={{0,5},{1,4},{2,7},{3,6},{4,1},{5,0},{6,3},{7,2},{8,13},{9,12},{10,... | collective-permute-start | bytes 1966088 | tf_op jit(solution)/shard_map/ppermute | solution.py:298
  102.7 22.3 %collective-permute-start.19 = (bf16[4,128,128]{2,1,0:T(8,128)(2,1)S(1)}, bf16[4,128,128]{2,1,0:T(8,128)(2,1)S(1)}, u32[]{:S(2)}, u32[]{:S(2)}) collective-permute-start(bf16[4,128,128]{2,1,0:T(8,128)(2,1)S(1)} %get-tuple-element.71), channel_id=1, source_target_pairs={{0,8},{8,0},{1,9},{9,1},{2,10},{10,2},{3,11},{11,3},{4,12},{12,4},... | collective-permute-start | bytes 393224 | tf_op jit(solution)/shard_map/ppermute | solution.py:333
  118.2 7.2 %collective-permute-start.18 = (bf16[4,128,128]{2,1,0:T(8,128)(2,1)S(1)}, bf16[4,128,128]{2,1,0:T(8,128)(2,1)S(1)}, u32[]{:S(2)}, u32[]{:S(2)}) collective-permute-start(bf16[4,128,128]{2,1,0:T(8,128)(2,1)S(1)} %get-tuple-element.70), channel_id=1, source_target_pairs={{0,8},{8,0},{1,9},{9,1},{2,10},{10,2},{3,11},{11,3},{4,12},{12,4},... | collective-permute-start | bytes 393224 | tf_op jit(solution)/shard_map/ppermute | solution.py:333
  119.9 5.6 %collective-permute-start.17 = (bf16[4,128,128]{2,1,0:T(8,128)(2,1)S(1)}, bf16[4,128,128]{2,1,0:T(8,128)(2,1)S(1)}, u32[]{:S(2)}, u32[]{:S(2)}) collective-permute-start(bf16[4,128,128]{2,1,0:T(8,128)(2,1)S(1)} %get-tuple-element.69), channel_id=1, source_target_pairs={{0,8},{8,0},{1,9},{9,1},{2,10},{10,2},{3,11},{11,3},{4,12},{12,4},... | collective-permute-start | bytes 393224 | tf_op jit(solution)/shard_map/ppermute | solution.py:333
  122.1 3.9 %collective-permute-start.16 = (bf16[4,128,128]{2,1,0:T(8,128)(2,1)S(1)}, bf16[4,128,128]{2,1,0:T(8,128)(2,1)S(1)}, u32[]{:S(2)}, u32[]{:S(2)}) collective-permute-start(bf16[4,128,128]{2,1,0:T(8,128)(2,1)S(1)} %get-tuple-element.68), channel_id=1, source_target_pairs={{0,8},{8,0},{1,9},{9,1},{2,10},{10,2},{3,11},{11,3},{4,12},{12,4},... | collective-permute-start | bytes 393224 | tf_op jit(solution)/shard_map/ppermute | solution.py:333
  125.0 1.5 %collective-permute-start.15 = (bf16[4,128,128]{2,1,0:T(8,128)(2,1)S(1)}, bf16[4,128,128]{2,1,0:T(8,128)(2,1)S(1)}, u32[]{:S(2)}, u32[]{:S(2)}) collective-permute-start(bf16[4,128,128]{2,1,0:T(8,128)(2,1)S(1)} %get-tuple-element.67), channel_id=1, source_target_pairs={{0,8},{8,0},{1,9},{9,1},{2,10},{10,2},{3,11},{11,3},{4,12},{12,4},... | collective-permute-start | bytes 393224 | tf_op jit(solution)/shard_map/ppermute | solution.py:333
  125.5 1.3 %collective-permute-start.14 = (bf16[4,128,128]{2,1,0:T(8,128)(2,1)S(1)}, bf16[4,128,128]{2,1,0:T(8,128)(2,1)S(1)}, u32[]{:S(2)}, u32[]{:S(2)}) collective-permute-start(bf16[4,128,128]{2,1,0:T(8,128)(2,1)S(1)} %get-tuple-element.66), channel_id=1, source_target_pairs={{0,8},{8,0},{1,9},{9,1},{2,10},{10,2},{3,11},{11,3},{4,12},{12,4},... | collective-permute-start | bytes 393224 | tf_op jit(solution)/shard_map/ppermute | solution.py:333
  125.6 1.4 %collective-permute-start.13 = (bf16[4,128,128]{2,1,0:T(8,128)(2,1)S(1)}, bf16[4,128,128]{2,1,0:T(8,128)(2,1)S(1)}, u32[]{:S(2)}, u32[]{:S(2)}) collective-permute-start(bf16[4,128,128]{2,1,0:T(8,128)(2,1)S(1)} %get-tuple-element.65), channel_id=1, source_target_pairs={{0,8},{8,0},{1,9},{9,1},{2,10},{10,2},{3,11},{11,3},{4,12},{12,4},... | collective-permute-start | bytes 393224 | tf_op jit(solution)/shard_map/ppermute | solution.py:333
  130.2 1.4 %collective-permute-start.21 = (bf16[4,128,128]{2,1,0:T(8,128)(2,1)S(1)}, bf16[4,128,128]{2,1,0:T(8,128)(2,1)S(1)}, u32[]{:S(2)}, u32[]{:S(2)}) collective-permute-start(bf16[4,128,128]{2,1,0:T(8,128)(2,1)S(1)} %get-tuple-element.75), channel_id=1, source_target_pairs={{0,8},{8,0},{1,9},{9,1},{2,10},{10,2},{3,11},{11,3},{4,12},{12,4},... | collective-permute-start | bytes 393224 | tf_op jit(solution)/shard_map/ppermute | solution.py:333
  (7 other events, 16.8 us)

commit v5 on v4

--- a/solution.py
+++ b/solution.py
@@ -91,10 +91,11 @@
 
 def send_kernel(plan, groups, where, masks, code_ref, *rest):
     mask_refs, (own_ref, other_ref) = rest[:masks], rest[masks : masks + 2]
-    outs, (found, sem) = rest[masks + 2 : -2], rest[-2:]
+    n = len(groups)
+    outs, held, (found, sem) = rest[masks + 2 : masks + 2 + n], rest[masks + 2 + n : -2], rest[-2:]
     core = lax.axis_index("blk")
-    for n, (group, (held, first), out) in enumerate(zip(groups, where, outs)):
-        mask_ref = mask_refs[held]
+    for n, (group, (which, first), out) in enumerate(zip(groups, where, held)):
+        mask_ref = mask_refs[which]
 
         def step(s):
             p, q = slot(plan, group, s)
@@ -116,8 +117,13 @@
                     pltpu.make_async_copy(other_ref.at[sector, at], out.at[s, j], sem.at[n]).start()
 
         each(len(group) * plan.capc, step)
-    for n, out in enumerate(outs):
-        pltpu.make_async_copy(out, out, sem.at[n]).wait()
+    copies = []
+    for n, (out, mine) in enumerate(zip(outs, held)):
+        pltpu.make_async_copy(mine, mine, sem.at[n]).wait()
+        copies.append(pltpu.make_async_copy(mine, out, sem.at[len(groups) + n]))
+        copies[-1].start()
+    for copy in copies:
+        copy.wait()
 
 
 def send(plan, groups, where, code, masks, own, other):
@@ -126,9 +132,10 @@
         functools.partial(send_kernel, plan, groups, where, len(masks)),
         out_shape=[jax.ShapeDtypeStruct((len(g) * plan.capc, WACT, w, w), own.dtype) for g in groups],
         in_specs=[smem()] + [smem() for _ in masks] + [hbm(), hbm()],
-        out_specs=[vmem() for _ in groups],
-        scratch_shapes=[pltpu.SMEM((left_comps + 1,), jnp.int32), pltpu.SemaphoreType.DMA((len(groups),))],
-        compiler_params=pltpu.CompilerParams(vmem_limit_bytes=58 * MIB),
+        out_specs=[hbm() for _ in groups],
+        scratch_shapes=[pltpu.VMEM((len(g) * plan.capc, WACT, w, w), own.dtype) for g in groups]
+        + [pltpu.SMEM((left_comps + 1,), jnp.int32), pltpu.SemaphoreType.DMA((2 * len(groups),))],
+        compiler_params=pltpu.CompilerParams(vmem_limit_bytes=(52 if len(groups) == 2 else 58) * MIB),
         cost_estimate=pl.CostEstimate(flops=0, bytes_accessed=8_000_000, transcendentals=0),
     )(code, *masks, own, other)
 

time: 134 us -> 133 us (level)
  local copies, waits for them, and re-layouts: 4.89 us -> 2.41 us
  waiting for transfers between devices: 48.1 us -> 49.5 us
    ppermute x11, waiting for transfers between devices: 45.7 us -> 47.1 us  [meet(): return lax.ppermute(x, 'rows', [(i, i ^ group[0]) for i in range(devices)])]
    unnamed x21 -> x19, local copies, waits for them, and re-layouts: 2.77 us -> 1.49 us
  transfers between devices with their start and end apart: 22 -> 22, of which waited for: 9 -> 9; matrix products, arithmetic and copies ran while one was open for 3% -> 1% of each run, Pallas kernels for 22% -> 22%
where the time goes in v5:
time: 133 us; the launch traced here: 132 us
  waiting for transfers between devices  49.5 us (37%)
  starting transfers between devices  44.9 us (34%)
  Pallas kernels  34 us (26%)
  local copies, waits for them, and re-layouts  2.41 us (2%)
    ppermute x11, waiting for transfers between devices, meet(): return lax.ppermute(x, 'rows', [(i, i ^ group[0]) for i in range(devices)])  47.1 us
    ppermute x11, starting transfers between devices, meet(): return lax.ppermute(x, 'rows', [(i, i ^ group[0]) for i in range(devices)])  42 us
    pallas_call x1, Pallas kernels, products(): pl.pallas_call(functools.partial(product_kernel, plan, late), grid=(slots...  12.7 us
    pallas_call x8, Pallas kernels, contract(): pl.pallas_call(functools.partial(contract_kernel, plan), grid=(count // b...  9.56 us
    pallas_call x2, Pallas kernels, send(): pl.pallas_call(functools.partial(send_kernel, plan, groups, where, len(ma...  8.42 us
  transfers between devices with their start and end apart: 22, of which 9 were waited for; matrix products, arithmetic and copies ran while one was open for 1% of the time, Pallas kernels for 22%

profile of v5, /device:TPU:0, one launch (start us, length us, event | category | flops | bytes accessed | tf_op | source)
XLA Modules:
  0.0 132.0 jit_solution(13164882977380909494)
XLA Ops:
  0.5 4.6 %collective-permute-start = (s32[16,10]{1,0:T(8,128)}, s32[16,10]{1,0:T(8,128)S(1)}, u32[]{:S(2)}, u32[]{:S(2)}) collective-permute-start(s32[16,10]{1,0:T(8,128)} %mask_ref.1), channel_id=1, source_target_pairs={{0,6},{1,7},{2,4},{3,5},{4,2},{5,3},{6,0},{7,1},{8,14},{9,15},{10,... | collective-permute-start | bytes 1928 | tf_op jit(solution)/shard_map/ppermute | solution.py:305
  5.1 1.2 collective-permute-start.1
  6.2 0.8 reshape.245
  7.8 3.9 %collective-permute-done.1.rest_1_ = s32[16,10]{1,0:T(8,128)S(1)} collective-permute-done((s32[16,10]{1,0:T(8,128)}, s32[16,10]{1,0:T(8,128)S(1)}, u32[]{:S(2)}, u32[]{:S(2)}) %collective-permute-start.1) | collective-permute-done | bytes 672 | tf_op jit(solution)/shard_map/ppermute | solution.py:305
  11.6 3.1 %shard_map.55 = (bf16[4,5,128,128]{3,2,1,0:T(8,128)(2,1)}, bf16[4,5,128,128]{3,2,1,0:T(8,128)(2,1)}) custom-call(s32[64]{0:T(128)S(1)} %reshape.247.code_ref, s32[16,10]{1,0:T(8,128)S(1)} %collective-permute-done.rest_0_, s32[16,10]{1,0:T(8,128)S(1)} %collective-permute-done.1.rest_1_, bf16[16,5,128,128]{3,2,1,0:T(8,128)(2,1)} %rest_2_.3, ...), custom_call_target="tpu_custom_call" | custom-call | bytes 8000000 | tf_op jit(solution)/shard_map/pallas_call | solution.py:131
  15.3 1.2 collective-permute-start.8
  16.5 3.6 %collective-permute-start.7 = (bf16[4,5,128,128]{3,2,1,0:T(8,128)(2,1)}, bf16[4,5,128,128]{3,2,1,0:T(8,128)(2,1)}, u32[]{:S(2)}, u32[]{:S(2)}) collective-permute-start(bf16[4,5,128,128]{3,2,1,0:T(8,128)(2,1)} %get-tuple-element.50), channel_id=1, source_target_pairs={{0,6},{1,7},{2,4},{3,5},{4,2},{5,3},{6,0},{7,1},{8,14},{9,15},{10,... | collective-permute-start | bytes 1966088 | tf_op jit(solution)/shard_map/ppermute | solution.py:305
  20.6 6.1 %collective-permute-done.5 = s32[16,10]{1,0:T(8,128)S(1)} collective-permute-done((s32[16,10]{1,0:T(8,128)S(1)}, s32[16,10]{1,0:T(8,128)S(1)}, u32[]{:S(2)}, u32[]{:S(2)}) %collective-permute-start.5) | collective-permute-done | bytes 672 | tf_op jit(solution)/shard_map/ppermute | solution.py:305
  26.8 23.1 %collective-permute-done.6.rest_1_ = s32[64,10]{1,0:T(8,128)S(1)} collective-permute-done((s32[64,10]{1,0:T(8,128)S(1)}, s32[64,10]{1,0:T(8,128)S(1)}, u32[]{:S(2)}, u32[]{:S(2)}) %collective-permute-start.6) | collective-permute-done | bytes 2592 | tf_op jit(solution)/shard_map/ppermute | solution.py:305
  50.5 5.3 %shard_map.57 = (bf16[4,5,128,128]{3,2,1,0:T(8,128)(2,1)}, bf16[4,5,128,128]{3,2,1,0:T(8,128)(2,1)}, bf16[4,5,128,128]{3,2,1,0:T(8,128)(2,1)}, bf16[4,5,128,128]...) custom-call(s32[64]{0:T(128)} %copy-done.5, s32[64,10]{1,0:T(8,128)} %copy-done.6, ...), custom_call_target="tpu_custom_call" | custom-call | bytes 8000000 | tf_op jit(solution)/shard_map/pallas_call | solution.py:131
  55.9 0.8 copy-done.1
  56.8 4.1 %collective-permute-start.11 = (bf16[4,5,128,128]{3,2,1,0:T(8,128)(2,1)}, bf16[4,5,128,128]{3,2,1,0:T(8,128)(2,1)}, u32[]{:S(2)}, u32[]{:S(2)}) collective-permute-start(bf16[4,5,128,128]{3,2,1,0:T(8,128)(2,1)} %get-tuple-element.61), channel_id=1, source_target_pairs={{0,4},{1,5},{2,6},{3,7},{4,0},{5,1},{6,2},{7,3},{8,12},{9,13},{10,... | collective-permute-start | bytes 1966088 | tf_op jit(solution)/shard_map/ppermute | solution.py:305
  60.8 26.6 %collective-permute-start.10 = (bf16[4,5,128,128]{3,2,1,0:T(8,128)(2,1)}, bf16[4,5,128,128]{3,2,1,0:T(8,128)(2,1)}, u32[]{:S(2)}, u32[]{:S(2)}) collective-permute-start(bf16[4,5,128,128]{3,2,1,0:T(8,128)(2,1)} %get-tuple-element.59), channel_id=1, source_target_pairs={{0,2},{1,3},{2,0},{3,1},{4,6},{5,7},{6,4},{7,5},{8,10},{9,11},{10,... | collective-permute-start | bytes 1966088 | tf_op jit(solution)/shard_map/ppermute | solution.py:305
  87.9 12.7 %shard_map.56 = (bf16[32,256,640]{2,1,0:T(8,128)(2,1)S(1)}, bf16[4,256,640]{2,1,0:T(8,128)(2,1)S(1)}) custom-call(s32[64]{0:T(128)S(1)} %reshape.246.order_ref, s32[16,10]{1,0:T(8,128)S(1)} %copy-done.4, bf16[16,5,128,128]{3,2,1,0:T(8,128)(2,1)S(1)} %copy-done, bf16[16,5,128,128]{3,2,1,0:T(8,128)(2,1)} %collective-permute-done.3.other_l, ...), custom_call_target="tpu_custom_call" | custom-call | flops 1000 | bytes 1000 | tf_op jit(solution)/shard_map/pallas_call | solution.py:187
  100.6 1.6 %shard_map.64 = (bf16[4,128,128]{2,1,0:T(8,128)(2,1)S(1)}, bf16[4,128,128]{2,1,0:T(8,128)(2,1)S(1)}) custom-call(bf16[32,256,640]{2,1,0:T(8,128)(2,1)S(1)} %get-tuple-element.45.terms_ref, bf16[4,5,128,128]{3,2,1,0:T(8,128)(2,1)} %collective-permute-done.12.right_ref), custom_call_target="tpu_custom_call" | custom-call | flops 1000 | bytes 1000 | tf_op jit(solution)/shard_map/pallas_call | solution.py:222
  102.3 13.4 %collective-permute-done.11.right_ref = bf16[4,5,128,128]{3,2,1,0:T(8,128)(2,1)} collective-permute-done((bf16[4,5,128,128]{3,2,1,0:T(8,128)(2,1)}, bf16[4,5,128,128]{3,2,1,0:T(8,128)(2,1)}, u32[]{:S(2)}, u32[]{:S(2)}) %collective-permute-start.11) | collective-permute-done | bytes 655392 | tf_op jit(solution)/shard_map/ppermute | solution.py:305
  115.7 1.6 %shard_map.63 = (bf16[4,128,128]{2,1,0:T(8,128)(2,1)S(1)}, bf16[4,128,128]{2,1,0:T(8,128)(2,1)S(1)}) custom-call(bf16[32,256,640]{2,1,0:T(8,128)(2,1)S(1)} %get-tuple-element.45.terms_ref, bf16[4,5,128,128]{3,2,1,0:T(8,128)(2,1)} %collective-permute-done.11.right_ref), custom_call_target="tpu_custom_call" | custom-call | flops 1000 | bytes 1000 | tf_op jit(solution)/shard_map/pallas_call | solution.py:222
  117.4 1.6 %shard_map.62 = (bf16[4,128,128]{2,1,0:T(8,128)(2,1)S(1)}, bf16[4,128,128]{2,1,0:T(8,128)(2,1)S(1)}) custom-call(bf16[32,256,640]{2,1,0:T(8,128)(2,1)S(1)} %get-tuple-element.45.terms_ref, bf16[4,5,128,128]{3,2,1,0:T(8,128)(2,1)} %collective-permute-done.10.right_ref), custom_call_target="tpu_custom_call" | custom-call | flops 1000 | bytes 1000 | tf_op jit(solution)/shard_map/pallas_call | solution.py:222
  119.6 1.6 %shard_map.61 = (bf16[4,128,128]{2,1,0:T(8,128)(2,1)S(1)}, bf16[4,128,128]{2,1,0:T(8,128)(2,1)S(1)}) custom-call(bf16[32,256,640]{2,1,0:T(8,128)(2,1)S(1)} %get-tuple-element.45.terms_ref, bf16[4,5,128,128]{3,2,1,0:T(8,128)(2,1)} %collective-permute-done.9.right_ref), custom_call_target="tpu_custom_call" | custom-call | flops 1000 | bytes 1000 | tf_op jit(solution)/shard_map/pallas_call | solution.py:222
  121.9 1.7 %shard_map.59 = (bf16[4,128,128]{2,1,0:T(8,128)(2,1)S(1)}, bf16[4,128,128]{2,1,0:T(8,128)(2,1)S(1)}) custom-call(bf16[32,256,640]{2,1,0:T(8,128)(2,1)S(1)} %get-tuple-element.45.terms_ref, bf16[4,5,128,128]{3,2,1,0:T(8,128)(2,1)} %collective-permute-done.7.right_ref), custom_call_target="tpu_custom_call" | custom-call | flops 1000 | bytes 1000 | tf_op jit(solution)/shard_map/pallas_call | solution.py:222
  126.1 2.0 %shard_map.65.rest_2_ = bf16[64,128,128]{2,1,0:T(8,128)(2,1)} custom-call(s32[64]{0:T(128)S(1)} %reshape.246.order_ref, bf16[4,128,128]{2,1,0:T(8,128)(2,1)S(1)} %get-tuple-element.48.rest_0_, bf16[4,128,128]{2,1,0:T(8,128)(2,1)S(1)} %get-tuple-element.52.rest_1_, bf16[4,128,128]{2,1,0:T(8,128)(2,1)S(1)} %get-tuple-element.56.rest_2_, ...), custom_call_target="tpu_custom_call" | custom-call | flops 1000 | bytes 1000 | tf_op jit(solution)/shard_map/pallas_call | solution.py:255
  128.1 0.6 collective-permute-done.20.right_ref
  129.3 1.3 %collective-permute-done.21.rest_1_ = bf16[4,128,128]{2,1,0:T(8,128)(2,1)S(1)} collective-permute-done((bf16[4,128,128]{2,1,0:T(8,128)(2,1)S(1)}, bf16[4,128,128]{2,1,0:T(8,128)(2,1)S(1)}, u32[]{:S(2)}, u32[]{:S(2)}) %collective-permute-start.21) | collective-permute-done | bytes 131104 | tf_op jit(solution)/shard_map/ppermute | solution.py:340
  130.7 1.3 shard_map.67
  (67 shorter events, 8.0 us)
Async XLA Ops:
  0.0 11.6 %collective-permute-start.2 = (bf16[16,5,128,128]{3,2,1,0:T(8,128)(2,1)}, bf16[16,5,128,128]{3,2,1,0:T(8,128)(2,1)}, u32[]{:S(2)}, u32[]{:S(2)}) collective-permute-start(bf16[16,5,128,128]{3,2,1,0:T(8,128)(2,1)} %rest_2_.3), channel_id=1, source_target_pairs={{0,8},{8,0},{1,9},{9,1},{2,10},{10,2},{3,11},{11,3},{4,12},{12,4},... | collective-permute-start | bytes 7864328 | tf_op jit(solution)/shard_map/ppermute | solution.py:298
  0.5 7.3 %collective-permute-start = (s32[16,10]{1,0:T(8,128)}, s32[16,10]{1,0:T(8,128)S(1)}, u32[]{:S(2)}, u32[]{:S(2)}) collective-permute-start(s32[16,10]{1,0:T(8,128)} %mask_ref.1), channel_id=1, source_target_pairs={{0,6},{1,7},{2,4},{3,5},{4,2},{5,3},{6,0},{7,1},{8,14},{9,15},{10,... | collective-permute-start | bytes 1928 | tf_op jit(solution)/shard_map/ppermute | solution.py:305
  5.1 6.6 %collective-permute-start.1 = (s32[16,10]{1,0:T(8,128)}, s32[16,10]{1,0:T(8,128)S(1)}, u32[]{:S(2)}, u32[]{:S(2)}) collective-permute-start(s32[16,10]{1,0:T(8,128)} %mask_ref.1), channel_id=1, source_target_pairs={{0,7},{1,6},{2,5},{3,4},{4,3},{5,2},{6,1},{7,0},{8,15},{9,14},{10,... | collective-permute-start | bytes 1928 | tf_op jit(solution)/shard_map/ppermute | solution.py:305
  7.7 12.4 %copy-start.4 = (s32[16,10]{1,0:T(8,128)S(1)}, s32[16,10]{1,0:T(8,128)}, u32[]{:S(2)}) copy-start(s32[16,10]{1,0:T(8,128)} %mask_ref.1) | copy-start | bytes 1924
  14.8 72.8 %collective-permute-start.3 = (bf16[16,5,128,128]{3,2,1,0:T(8,128)(2,1)S(1)}, bf16[16,5,128,128]{3,2,1,0:T(8,128)(2,1)}, u32[]{:S(2)}, u32[]{:S(2)}) collective-permute-start(bf16[16,5,128,128]{3,2,1,0:T(8,128)(2,1)S(1)} %copy-done), channel_id=1, source_target_pairs={{0,8},{8,0},{1,9},{9,1},{2,10},{10,2},{3,11},{11,3},{4,12},{12,4},... | collective-permute-start | bytes 7864328 | tf_op jit(solution)/shard_map/ppermute | solution.py:332
  14.8 72.6 %collective-permute-start.4 = (bf16[64,128,128]{2,1,0:T(8,128)(2,1)}, bf16[64,128,128]{2,1,0:T(8,128)(2,1)}, u32[]{:S(2)}, u32[]{:S(2)}) collective-permute-start(bf16[64,128,128]{2,1,0:T(8,128)(2,1)} %bitcast.2.rest_0_), channel_id=1, source_target_pairs={{0,8},{8,0},{1,9},{9,1},{2,10},{10,2},{3,11},{11,3},{4,12},{12,4},... | collective-permute-start | bytes 6291464 | tf_op jit(solution)/shard_map/ppermute | solution.py:333
  15.3 40.6 %collective-permute-start.8 = (bf16[4,5,128,128]{3,2,1,0:T(8,128)(2,1)}, bf16[4,5,128,128]{3,2,1,0:T(8,128)(2,1)S(1)}, u32[]{:S(2)}, u32[]{:S(2)}) collective-permute-start(bf16[4,5,128,128]{3,2,1,0:T(8,128)(2,1)} %get-tuple-element.54), channel_id=1, source_target_pairs={{0,7},{1,6},{2,5},{3,4},{4,3},{5,2},{6,1},{7,0},{8,15},{9,14},{10,... | collective-permute-start | bytes 1966088 | tf_op jit(solution)/shard_map/ppermute | solution.py:305
  16.5 44.3 %collective-permute-start.7 = (bf16[4,5,128,128]{3,2,1,0:T(8,128)(2,1)}, bf16[4,5,128,128]{3,2,1,0:T(8,128)(2,1)}, u32[]{:S(2)}, u32[]{:S(2)}) collective-permute-start(bf16[4,5,128,128]{3,2,1,0:T(8,128)(2,1)} %get-tuple-element.50), channel_id=1, source_target_pairs={{0,6},{1,7},{2,4},{3,5},{4,2},{5,3},{6,0},{7,1},{8,14},{9,15},{10,... | collective-permute-start | bytes 1966088 | tf_op jit(solution)/shard_map/ppermute | solution.py:305
  20.1 6.6 %collective-permute-start.5 = (s32[16,10]{1,0:T(8,128)S(1)}, s32[16,10]{1,0:T(8,128)S(1)}, u32[]{:S(2)}, u32[]{:S(2)}) collective-permute-start(s32[16,10]{1,0:T(8,128)S(1)} %copy-done.4), channel_id=1, source_target_pairs={{0,1},{1,0},{2,3},{3,2},{4,5},{5,4},{6,7},{7,6},{8,9},{9,8},{10,11... | collective-permute-start | bytes 1928 | tf_op jit(solution)/shard_map/ppermute | solution.py:305
  26.7 23.2 %copy-start.6 = (s32[64,10]{1,0:T(8,128)}, s32[64,10]{1,0:T(8,128)S(1)}, u32[]{:S(2)}) copy-start(s32[64,10]{1,0:T(8,128)S(1)} %constant_dynamic-update-slice_fusion.rest_0_) | copy-start | bytes 7684
  26.7 23.2 %collective-permute-start.6 = (s32[64,10]{1,0:T(8,128)S(1)}, s32[64,10]{1,0:T(8,128)S(1)}, u32[]{:S(2)}, u32[]{:S(2)}) collective-permute-start(s32[64,10]{1,0:T(8,128)S(1)} %constant_dynamic-update-slice_fusion.rest_0_), channel_id=1, source_target_pairs={{0,2},{1,3},{2,0},{3,1},{4,6},{5,7},{6,4},{7,5},{8,10},{9,11},{10,... | collective-permute-start | bytes 7688 | tf_op jit(solution)/shard_map/ppermute | solution.py:305
  55.8 44.8 %collective-permute-start.12 = (bf16[4,5,128,128]{3,2,1,0:T(8,128)(2,1)}, bf16[4,5,128,128]{3,2,1,0:T(8,128)(2,1)}, u32[]{:S(2)}, u32[]{:S(2)}) collective-permute-start(bf16[4,5,128,128]{3,2,1,0:T(8,128)(2,1)} %get-tuple-element.63), channel_id=1, source_target_pairs={{0,3},{1,2},{2,1},{3,0},{4,7},{5,6},{6,5},{7,4},{8,11},{9,10},{10,... | collective-permute-start | bytes 1966088 | tf_op jit(solution)/shard_map/ppermute | solution.py:305
  56.8 59.0 %collective-permute-start.11 = (bf16[4,5,128,128]{3,2,1,0:T(8,128)(2,1)}, bf16[4,5,128,128]{3,2,1,0:T(8,128)(2,1)}, u32[]{:S(2)}, u32[]{:S(2)}) collective-permute-start(bf16[4,5,128,128]{3,2,1,0:T(8,128)(2,1)} %get-tuple-element.61), channel_id=1, source_target_pairs={{0,4},{1,5},{2,6},{3,7},{4,0},{5,1},{6,2},{7,3},{8,12},{9,13},{10,... | collective-permute-start | bytes 1966088 | tf_op jit(solution)/shard_map/ppermute | solution.py:305
  60.8 56.6 %collective-permute-start.10 = (bf16[4,5,128,128]{3,2,1,0:T(8,128)(2,1)}, bf16[4,5,128,128]{3,2,1,0:T(8,128)(2,1)}, u32[]{:S(2)}, u32[]{:S(2)}) collective-permute-start(bf16[4,5,128,128]{3,2,1,0:T(8,128)(2,1)} %get-tuple-element.59), channel_id=1, source_target_pairs={{0,2},{1,3},{2,0},{3,1},{4,6},{5,7},{6,4},{7,5},{8,10},{9,11},{10,... | collective-permute-start | bytes 1966088 | tf_op jit(solution)/shard_map/ppermute | solution.py:305
  87.4 32.2 %collective-permute-start.9 = (bf16[4,5,128,128]{3,2,1,0:T(8,128)(2,1)}, bf16[4,5,128,128]{3,2,1,0:T(8,128)(2,1)}, u32[]{:S(2)}, u32[]{:S(2)}) collective-permute-start(bf16[4,5,128,128]{3,2,1,0:T(8,128)(2,1)} %get-tuple-element.57), channel_id=1, source_target_pairs={{0,1},{1,0},{2,3},{3,2},{4,5},{5,4},{6,7},{7,6},{8,9},{9,8},{10,11... | collective-permute-start | bytes 1966088 | tf_op jit(solution)/shard_map/ppermute | solution.py:305
  87.5 41.2 %collective-permute-start.20 = (bf16[4,5,128,128]{3,2,1,0:T(8,128)(2,1)}, bf16[4,5,128,128]{3,2,1,0:T(8,128)(2,1)S(1)}, u32[]{:S(2)}, u32[]{:S(2)}) collective-permute-start(bf16[4,5,128,128]{3,2,1,0:T(8,128)(2,1)} %get-tuple-element.72), channel_id=1, source_target_pairs={{0,5},{1,4},{2,7},{3,6},{4,1},{5,0},{6,3},{7,2},{8,13},{9,12},{10,... | collective-permute-start | bytes 1966088 | tf_op jit(solution)/shard_map/ppermute | solution.py:305
  102.2 21.8 %collective-permute-start.19 = (bf16[4,128,128]{2,1,0:T(8,128)(2,1)S(1)}, bf16[4,128,128]{2,1,0:T(8,128)(2,1)S(1)}, u32[]{:S(2)}, u32[]{:S(2)}) collective-permute-start(bf16[4,128,128]{2,1,0:T(8,128)(2,1)S(1)} %get-tuple-element.71), channel_id=1, source_target_pairs={{0,8},{8,0},{1,9},{9,1},{2,10},{10,2},{3,11},{11,3},{4,12},{12,4},... | collective-permute-start | bytes 393224 | tf_op jit(solution)/shard_map/ppermute | solution.py:340
  117.3 7.2 %collective-permute-start.18 = (bf16[4,128,128]{2,1,0:T(8,128)(2,1)S(1)}, bf16[4,128,128]{2,1,0:T(8,128)(2,1)S(1)}, u32[]{:S(2)}, u32[]{:S(2)}) collective-permute-start(bf16[4,128,128]{2,1,0:T(8,128)(2,1)S(1)} %get-tuple-element.70), channel_id=1, source_target_pairs={{0,8},{8,0},{1,9},{9,1},{2,10},{10,2},{3,11},{11,3},{4,12},{12,4},... | collective-permute-start | bytes 393224 | tf_op jit(solution)/shard_map/ppermute | solution.py:340
  119.0 5.6 %collective-permute-start.17 = (bf16[4,128,128]{2,1,0:T(8,128)(2,1)S(1)}, bf16[4,128,128]{2,1,0:T(8,128)(2,1)S(1)}, u32[]{:S(2)}, u32[]{:S(2)}) collective-permute-start(bf16[4,128,128]{2,1,0:T(8,128)(2,1)S(1)} %get-tuple-element.69), channel_id=1, source_target_pairs={{0,8},{8,0},{1,9},{9,1},{2,10},{10,2},{3,11},{11,3},{4,12},{12,4},... | collective-permute-start | bytes 393224 | tf_op jit(solution)/shard_map/ppermute | solution.py:340
  121.2 3.9 %collective-permute-start.16 = (bf16[4,128,128]{2,1,0:T(8,128)(2,1)S(1)}, bf16[4,128,128]{2,1,0:T(8,128)(2,1)S(1)}, u32[]{:S(2)}, u32[]{:S(2)}) collective-permute-start(bf16[4,128,128]{2,1,0:T(8,128)(2,1)S(1)} %get-tuple-element.68), channel_id=1, source_target_pairs={{0,8},{8,0},{1,9},{9,1},{2,10},{10,2},{3,11},{11,3},{4,12},{12,4},... | collective-permute-start | bytes 393224 | tf_op jit(solution)/shard_map/ppermute | solution.py:340
  124.1 1.5 %collective-permute-start.15 = (bf16[4,128,128]{2,1,0:T(8,128)(2,1)S(1)}, bf16[4,128,128]{2,1,0:T(8,128)(2,1)S(1)}, u32[]{:S(2)}, u32[]{:S(2)}) collective-permute-start(bf16[4,128,128]{2,1,0:T(8,128)(2,1)S(1)} %get-tuple-element.67), channel_id=1, source_target_pairs={{0,8},{8,0},{1,9},{9,1},{2,10},{10,2},{3,11},{11,3},{4,12},{12,4},... | collective-permute-start | bytes 393224 | tf_op jit(solution)/shard_map/ppermute | solution.py:340
  124.6 1.3 %collective-permute-start.14 = (bf16[4,128,128]{2,1,0:T(8,128)(2,1)S(1)}, bf16[4,128,128]{2,1,0:T(8,128)(2,1)S(1)}, u32[]{:S(2)}, u32[]{:S(2)}) collective-permute-start(bf16[4,128,128]{2,1,0:T(8,128)(2,1)S(1)} %get-tuple-element.66), channel_id=1, source_target_pairs={{0,8},{8,0},{1,9},{9,1},{2,10},{10,2},{3,11},{11,3},{4,12},{12,4},... | collective-permute-start | bytes 393224 | tf_op jit(solution)/shard_map/ppermute | solution.py:340
  124.7 1.4 %collective-permute-start.13 = (bf16[4,128,128]{2,1,0:T(8,128)(2,1)S(1)}, bf16[4,128,128]{2,1,0:T(8,128)(2,1)S(1)}, u32[]{:S(2)}, u32[]{:S(2)}) collective-permute-start(bf16[4,128,128]{2,1,0:T(8,128)(2,1)S(1)} %get-tuple-element.65), channel_id=1, source_target_pairs={{0,8},{8,0},{1,9},{9,1},{2,10},{10,2},{3,11},{11,3},{4,12},{12,4},... | collective-permute-start | bytes 393224 | tf_op jit(solution)/shard_map/ppermute | solution.py:340
  129.3 1.4 %collective-permute-start.21 = (bf16[4,128,128]{2,1,0:T(8,128)(2,1)S(1)}, bf16[4,128,128]{2,1,0:T(8,128)(2,1)S(1)}, u32[]{:S(2)}, u32[]{:S(2)}) collective-permute-start(bf16[4,128,128]{2,1,0:T(8,128)(2,1)S(1)} %get-tuple-element.75), channel_id=1, source_target_pairs={{0,8},{8,0},{1,9},{9,1},{2,10},{10,2},{3,11},{11,3},{4,12},{12,4},... | collective-permute-start | bytes 393224 | tf_op jit(solution)/shard_map/ppermute | solution.py:340
  (6 other events, 19.5 us)

commit v6 on v5

--- a/solution.py
+++ b/solution.py
@@ -217,7 +217,7 @@
 
 def contract(plan, group, terms, right):
     w, count = plan.width, len(group) * plan.capc
-    block = min(count, 4)
+    block = min(count, 4 if terms.shape[0] == count else 2)
     first = 0 if terms.shape[0] == count else group[0] * plan.capc // block
     return pl.pallas_call(
         functools.partial(contract_kernel, plan),

time: 133 us -> 133 us (level)
  transfers between devices with their start and end apart: 22 -> 22, of which waited for: 9 -> 8; matrix products, arithmetic and copies ran while one was open for 1% -> 1% of each run, Pallas kernels for 22% -> 23%
where the time goes in v6:
time: 133 us; the launch traced here: 132 us
  waiting for transfers between devices  48.5 us (36%)
  starting transfers between devices  45.2 us (34%)
  Pallas kernels  34.8 us (26%)
  local copies, waits for them, and re-layouts  2.41 us (2%)
    ppermute x11, waiting for transfers between devices, meet(): return lax.ppermute(x, 'rows', [(i, i ^ group[0]) for i in range(devices)])  46.4 us
    ppermute x11, starting transfers between devices, meet(): return lax.ppermute(x, 'rows', [(i, i ^ group[0]) for i in range(devices)])  42 us
    pallas_call x1, Pallas kernels, products(): pl.pallas_call(functools.partial(product_kernel, plan, late), grid=(slots...  12.7 us
    pallas_call x8, Pallas kernels, contract(): pl.pallas_call(functools.partial(contract_kernel, plan), grid=(count // b...  10.4 us
    pallas_call x2, Pallas kernels, send(): pl.pallas_call(functools.partial(send_kernel, plan, groups, where, len(ma...  8.42 us
  transfers between devices with their start and end apart: 22, of which 8 were waited for; matrix products, arithmetic and copies ran while one was open for 1% of the time, Pallas kernels for 23%

profile of v6, /device:TPU:0, one launch (start us, length us, event | category | flops | bytes accessed | tf_op | source)
XLA Modules:
  0.0 132.1 jit_solution(10998515013853619708)
XLA Ops:
  0.5 4.6 %collective-permute-start = (s32[16,10]{1,0:T(8,128)}, s32[16,10]{1,0:T(8,128)S(1)}, u32[]{:S(2)}, u32[]{:S(2)}) collective-permute-start(s32[16,10]{1,0:T(8,128)} %mask_ref.1), channel_id=1, source_target_pairs={{0,6},{1,7},{2,4},{3,5},{4,2},{5,3},{6,0},{7,1},{8,14},{9,15},{10,... | collective-permute-start | bytes 1928 | tf_op jit(solution)/shard_map/ppermute | solution.py:305
  5.1 1.2 collective-permute-start.1
  6.2 0.8 reshape.245
  7.8 3.9 %collective-permute-done.1.rest_1_ = s32[16,10]{1,0:T(8,128)S(1)} collective-permute-done((s32[16,10]{1,0:T(8,128)}, s32[16,10]{1,0:T(8,128)S(1)}, u32[]{:S(2)}, u32[]{:S(2)}) %collective-permute-start.1) | collective-permute-done | bytes 672 | tf_op jit(solution)/shard_map/ppermute | solution.py:305
  11.6 3.1 %shard_map.55 = (bf16[4,5,128,128]{3,2,1,0:T(8,128)(2,1)}, bf16[4,5,128,128]{3,2,1,0:T(8,128)(2,1)}) custom-call(s32[64]{0:T(128)S(1)} %reshape.247.code_ref, s32[16,10]{1,0:T(8,128)S(1)} %collective-permute-done.rest_0_, s32[16,10]{1,0:T(8,128)S(1)} %collective-permute-done.1.rest_1_, bf16[16,5,128,128]{3,2,1,0:T(8,128)(2,1)} %rest_2_.3, ...), custom_call_target="tpu_custom_call" | custom-call | bytes 8000000 | tf_op jit(solution)/shard_map/pallas_call | solution.py:131
  15.3 1.2 collective-permute-start.8
  16.5 3.6 %collective-permute-start.7 = (bf16[4,5,128,128]{3,2,1,0:T(8,128)(2,1)}, bf16[4,5,128,128]{3,2,1,0:T(8,128)(2,1)}, u32[]{:S(2)}, u32[]{:S(2)}) collective-permute-start(bf16[4,5,128,128]{3,2,1,0:T(8,128)(2,1)} %get-tuple-element.50), channel_id=1, source_target_pairs={{0,6},{1,7},{2,4},{3,5},{4,2},{5,3},{6,0},{7,1},{8,14},{9,15},{10,... | collective-permute-start | bytes 1966088 | tf_op jit(solution)/shard_map/ppermute | solution.py:305
  20.6 6.1 %collective-permute-done.5 = s32[16,10]{1,0:T(8,128)S(1)} collective-permute-done((s32[16,10]{1,0:T(8,128)S(1)}, s32[16,10]{1,0:T(8,128)S(1)}, u32[]{:S(2)}, u32[]{:S(2)}) %collective-permute-start.5) | collective-permute-done | bytes 672 | tf_op jit(solution)/shard_map/ppermute | solution.py:305
  26.8 23.1 %collective-permute-done.6.rest_1_ = s32[64,10]{1,0:T(8,128)S(1)} collective-permute-done((s32[64,10]{1,0:T(8,128)S(1)}, s32[64,10]{1,0:T(8,128)S(1)}, u32[]{:S(2)}, u32[]{:S(2)}) %collective-permute-start.6) | collective-permute-done | bytes 2592 | tf_op jit(solution)/shard_map/ppermute | solution.py:305
  50.5 5.3 %shard_map.57 = (bf16[4,5,128,128]{3,2,1,0:T(8,128)(2,1)}, bf16[4,5,128,128]{3,2,1,0:T(8,128)(2,1)}, bf16[4,5,128,128]{3,2,1,0:T(8,128)(2,1)}, bf16[4,5,128,128]...) custom-call(s32[64]{0:T(128)} %copy-done.5, s32[64,10]{1,0:T(8,128)} %copy-done.6, ...), custom_call_target="tpu_custom_call" | custom-call | bytes 8000000 | tf_op jit(solution)/shard_map/pallas_call | solution.py:131
  55.9 0.8 copy-done.1
  56.8 4.1 %collective-permute-start.11 = (bf16[4,5,128,128]{3,2,1,0:T(8,128)(2,1)}, bf16[4,5,128,128]{3,2,1,0:T(8,128)(2,1)}, u32[]{:S(2)}, u32[]{:S(2)}) collective-permute-start(bf16[4,5,128,128]{3,2,1,0:T(8,128)(2,1)} %get-tuple-element.61), channel_id=1, source_target_pairs={{0,4},{1,5},{2,6},{3,7},{4,0},{5,1},{6,2},{7,3},{8,12},{9,13},{10,... | collective-permute-start | bytes 1966088 | tf_op jit(solution)/shard_map/ppermute | solution.py:305
  60.8 26.6 %collective-permute-start.10 = (bf16[4,5,128,128]{3,2,1,0:T(8,128)(2,1)}, bf16[4,5,128,128]{3,2,1,0:T(8,128)(2,1)}, u32[]{:S(2)}, u32[]{:S(2)}) collective-permute-start(bf16[4,5,128,128]{3,2,1,0:T(8,128)(2,1)} %get-tuple-element.59), channel_id=1, source_target_pairs={{0,2},{1,3},{2,0},{3,1},{4,6},{5,7},{6,4},{7,5},{8,10},{9,11},{10,... | collective-permute-start | bytes 1966088 | tf_op jit(solution)/shard_map/ppermute | solution.py:305
  87.9 12.7 %shard_map.56 = (bf16[32,256,640]{2,1,0:T(8,128)(2,1)S(1)}, bf16[4,256,640]{2,1,0:T(8,128)(2,1)S(1)}) custom-call(s32[64]{0:T(128)S(1)} %reshape.246.order_ref, s32[16,10]{1,0:T(8,128)S(1)} %copy-done.4, bf16[16,5,128,128]{3,2,1,0:T(8,128)(2,1)S(1)} %copy-done, bf16[16,5,128,128]{3,2,1,0:T(8,128)(2,1)} %collective-permute-done.3.other_l, ...), custom_call_target="tpu_custom_call" | custom-call | flops 1000 | bytes 1000 | tf_op jit(solution)/shard_map/pallas_call | solution.py:187
  100.6 1.7 %shard_map.64 = (bf16[4,128,128]{2,1,0:T(8,128)(2,1)S(1)}, bf16[4,128,128]{2,1,0:T(8,128)(2,1)S(1)}) custom-call(bf16[32,256,640]{2,1,0:T(8,128)(2,1)S(1)} %get-tuple-element.45.terms_ref, bf16[4,5,128,128]{3,2,1,0:T(8,128)(2,1)} %collective-permute-done.12.right_ref), custom_call_target="tpu_custom_call" | custom-call | flops 1000 | bytes 1000 | tf_op jit(solution)/shard_map/pallas_call | solution.py:222
  102.4 13.3 %collective-permute-done.11.right_ref = bf16[4,5,128,128]{3,2,1,0:T(8,128)(2,1)} collective-permute-done((bf16[4,5,128,128]{3,2,1,0:T(8,128)(2,1)}, bf16[4,5,128,128]{3,2,1,0:T(8,128)(2,1)}, u32[]{:S(2)}, u32[]{:S(2)}) %collective-permute-start.11) | collective-permute-done | bytes 655392 | tf_op jit(solution)/shard_map/ppermute | solution.py:305
  115.7 1.7 %shard_map.63 = (bf16[4,128,128]{2,1,0:T(8,128)(2,1)S(1)}, bf16[4,128,128]{2,1,0:T(8,128)(2,1)S(1)}) custom-call(bf16[32,256,640]{2,1,0:T(8,128)(2,1)S(1)} %get-tuple-element.45.terms_ref, bf16[4,5,128,128]{3,2,1,0:T(8,128)(2,1)} %collective-permute-done.11.right_ref), custom_call_target="tpu_custom_call" | custom-call | flops 1000 | bytes 1000 | tf_op jit(solution)/shard_map/pallas_call | solution.py:222
  117.5 1.7 %shard_map.62 = (bf16[4,128,128]{2,1,0:T(8,128)(2,1)S(1)}, bf16[4,128,128]{2,1,0:T(8,128)(2,1)S(1)}) custom-call(bf16[32,256,640]{2,1,0:T(8,128)(2,1)S(1)} %get-tuple-element.45.terms_ref, bf16[4,5,128,128]{3,2,1,0:T(8,128)(2,1)} %collective-permute-done.10.right_ref), custom_call_target="tpu_custom_call" | custom-call | flops 1000 | bytes 1000 | tf_op jit(solution)/shard_map/pallas_call | solution.py:222
  119.8 1.7 %shard_map.61 = (bf16[4,128,128]{2,1,0:T(8,128)(2,1)S(1)}, bf16[4,128,128]{2,1,0:T(8,128)(2,1)S(1)}) custom-call(bf16[32,256,640]{2,1,0:T(8,128)(2,1)S(1)} %get-tuple-element.45.terms_ref, bf16[4,5,128,128]{3,2,1,0:T(8,128)(2,1)} %collective-permute-done.9.right_ref), custom_call_target="tpu_custom_call" | custom-call | flops 1000 | bytes 1000 | tf_op jit(solution)/shard_map/pallas_call | solution.py:222
  122.3 1.8 %shard_map.59 = (bf16[4,128,128]{2,1,0:T(8,128)(2,1)S(1)}, bf16[4,128,128]{2,1,0:T(8,128)(2,1)S(1)}) custom-call(bf16[32,256,640]{2,1,0:T(8,128)(2,1)S(1)} %get-tuple-element.45.terms_ref, bf16[4,5,128,128]{3,2,1,0:T(8,128)(2,1)} %collective-permute-done.7.right_ref), custom_call_target="tpu_custom_call" | custom-call | flops 1000 | bytes 1000 | tf_op jit(solution)/shard_map/pallas_call | solution.py:222
  124.1 0.7 shard_map.58
  126.9 2.0 %shard_map.65.rest_2_ = bf16[64,128,128]{2,1,0:T(8,128)(2,1)} custom-call(s32[64]{0:T(128)S(1)} %reshape.246.order_ref, bf16[4,128,128]{2,1,0:T(8,128)(2,1)S(1)} %get-tuple-element.48.rest_0_, bf16[4,128,128]{2,1,0:T(8,128)(2,1)S(1)} %get-tuple-element.52.rest_1_, bf16[4,128,128]{2,1,0:T(8,128)(2,1)S(1)} %get-tuple-element.56.rest_2_, ...), custom_call_target="tpu_custom_call" | custom-call | flops 1000 | bytes 1000 | tf_op jit(solution)/shard_map/pallas_call | solution.py:255
  129.8 1.0 collective-permute-done.21.rest_1_
  130.8 1.3 shard_map.67
  (67 shorter events, 8.0 us)
Async XLA Ops:
  0.0 11.6 %collective-permute-start.2 = (bf16[16,5,128,128]{3,2,1,0:T(8,128)(2,1)}, bf16[16,5,128,128]{3,2,1,0:T(8,128)(2,1)}, u32[]{:S(2)}, u32[]{:S(2)}) collective-permute-start(bf16[16,5,128,128]{3,2,1,0:T(8,128)(2,1)} %rest_2_.3), channel_id=1, source_target_pairs={{0,8},{8,0},{1,9},{9,1},{2,10},{10,2},{3,11},{11,3},{4,12},{12,4},... | collective-permute-start | bytes 7864328 | tf_op jit(solution)/shard_map/ppermute | solution.py:298
  0.5 7.3 %collective-permute-start = (s32[16,10]{1,0:T(8,128)}, s32[16,10]{1,0:T(8,128)S(1)}, u32[]{:S(2)}, u32[]{:S(2)}) collective-permute-start(s32[16,10]{1,0:T(8,128)} %mask_ref.1), channel_id=1, source_target_pairs={{0,6},{1,7},{2,4},{3,5},{4,2},{5,3},{6,0},{7,1},{8,14},{9,15},{10,... | collective-permute-start | bytes 1928 | tf_op jit(solution)/shard_map/ppermute | solution.py:305
  5.1 6.6 %collective-permute-start.1 = (s32[16,10]{1,0:T(8,128)}, s32[16,10]{1,0:T(8,128)S(1)}, u32[]{:S(2)}, u32[]{:S(2)}) collective-permute-start(s32[16,10]{1,0:T(8,128)} %mask_ref.1), channel_id=1, source_target_pairs={{0,7},{1,6},{2,5},{3,4},{4,3},{5,2},{6,1},{7,0},{8,15},{9,14},{10,... | collective-permute-start | bytes 1928 | tf_op jit(solution)/shard_map/ppermute | solution.py:305
  7.7 12.4 %copy-start.4 = (s32[16,10]{1,0:T(8,128)S(1)}, s32[16,10]{1,0:T(8,128)}, u32[]{:S(2)}) copy-start(s32[16,10]{1,0:T(8,128)} %mask_ref.1) | copy-start | bytes 1924
  14.8 72.8 %collective-permute-start.3 = (bf16[16,5,128,128]{3,2,1,0:T(8,128)(2,1)S(1)}, bf16[16,5,128,128]{3,2,1,0:T(8,128)(2,1)}, u32[]{:S(2)}, u32[]{:S(2)}) collective-permute-start(bf16[16,5,128,128]{3,2,1,0:T(8,128)(2,1)S(1)} %copy-done), channel_id=1, source_target_pairs={{0,8},{8,0},{1,9},{9,1},{2,10},{10,2},{3,11},{11,3},{4,12},{12,4},... | collective-permute-start | bytes 7864328 | tf_op jit(solution)/shard_map/ppermute | solution.py:332
  14.8 72.6 %collective-permute-start.4 = (bf16[64,128,128]{2,1,0:T(8,128)(2,1)}, bf16[64,128,128]{2,1,0:T(8,128)(2,1)}, u32[]{:S(2)}, u32[]{:S(2)}) collective-permute-start(bf16[64,128,128]{2,1,0:T(8,128)(2,1)} %bitcast.2.rest_0_), channel_id=1, source_target_pairs={{0,8},{8,0},{1,9},{9,1},{2,10},{10,2},{3,11},{11,3},{4,12},{12,4},... | collective-permute-start | bytes 6291464 | tf_op jit(solution)/shard_map/ppermute | solution.py:333
  15.3 40.6 %collective-permute-start.8 = (bf16[4,5,128,128]{3,2,1,0:T(8,128)(2,1)}, bf16[4,5,128,128]{3,2,1,0:T(8,128)(2,1)S(1)}, u32[]{:S(2)}, u32[]{:S(2)}) collective-permute-start(bf16[4,5,128,128]{3,2,1,0:T(8,128)(2,1)} %get-tuple-element.54), channel_id=1, source_target_pairs={{0,7},{1,6},{2,5},{3,4},{4,3},{5,2},{6,1},{7,0},{8,15},{9,14},{10,... | collective-permute-start | bytes 1966088 | tf_op jit(solution)/shard_map/ppermute | solution.py:305
  16.5 44.3 %collective-permute-start.7 = (bf16[4,5,128,128]{3,2,1,0:T(8,128)(2,1)}, bf16[4,5,128,128]{3,2,1,0:T(8,128)(2,1)}, u32[]{:S(2)}, u32[]{:S(2)}) collective-permute-start(bf16[4,5,128,128]{3,2,1,0:T(8,128)(2,1)} %get-tuple-element.50), channel_id=1, source_target_pairs={{0,6},{1,7},{2,4},{3,5},{4,2},{5,3},{6,0},{7,1},{8,14},{9,15},{10,... | collective-permute-start | bytes 1966088 | tf_op jit(solution)/shard_map/ppermute | solution.py:305
  20.1 6.6 %collective-permute-start.5 = (s32[16,10]{1,0:T(8,128)S(1)}, s32[16,10]{1,0:T(8,128)S(1)}, u32[]{:S(2)}, u32[]{:S(2)}) collective-permute-start(s32[16,10]{1,0:T(8,128)S(1)} %copy-done.4), channel_id=1, source_target_pairs={{0,1},{1,0},{2,3},{3,2},{4,5},{5,4},{6,7},{7,6},{8,9},{9,8},{10,11... | collective-permute-start | bytes 1928 | tf_op jit(solution)/shard_map/ppermute | solution.py:305
  26.7 23.2 %copy-start.6 = (s32[64,10]{1,0:T(8,128)}, s32[64,10]{1,0:T(8,128)S(1)}, u32[]{:S(2)}) copy-start(s32[64,10]{1,0:T(8,128)S(1)} %constant_dynamic-update-slice_fusion.rest_0_) | copy-start | bytes 7684
  26.7 23.2 %collective-permute-start.6 = (s32[64,10]{1,0:T(8,128)S(1)}, s32[64,10]{1,0:T(8,128)S(1)}, u32[]{:S(2)}, u32[]{:S(2)}) collective-permute-start(s32[64,10]{1,0:T(8,128)S(1)} %constant_dynamic-update-slice_fusion.rest_0_), channel_id=1, source_target_pairs={{0,2},{1,3},{2,0},{3,1},{4,6},{5,7},{6,4},{7,5},{8,10},{9,11},{10,... | collective-permute-start | bytes 7688 | tf_op jit(solution)/shard_map/ppermute | solution.py:305
  55.8 44.8 %collective-permute-start.12 = (bf16[4,5,128,128]{3,2,1,0:T(8,128)(2,1)}, bf16[4,5,128,128]{3,2,1,0:T(8,128)(2,1)}, u32[]{:S(2)}, u32[]{:S(2)}) collective-permute-start(bf16[4,5,128,128]{3,2,1,0:T(8,128)(2,1)} %get-tuple-element.63), channel_id=1, source_target_pairs={{0,3},{1,2},{2,1},{3,0},{4,7},{5,6},{6,5},{7,4},{8,11},{9,10},{10,... | collective-permute-start | bytes 1966088 | tf_op jit(solution)/shard_map/ppermute | solution.py:305
  56.8 59.0 %collective-permute-start.11 = (bf16[4,5,128,128]{3,2,1,0:T(8,128)(2,1)}, bf16[4,5,128,128]{3,2,1,0:T(8,128)(2,1)}, u32[]{:S(2)}, u32[]{:S(2)}) collective-permute-start(bf16[4,5,128,128]{3,2,1,0:T(8,128)(2,1)} %get-tuple-element.61), channel_id=1, source_target_pairs={{0,4},{1,5},{2,6},{3,7},{4,0},{5,1},{6,2},{7,3},{8,12},{9,13},{10,... | collective-permute-start | bytes 1966088 | tf_op jit(solution)/shard_map/ppermute | solution.py:305
  60.8 56.7 %collective-permute-start.10 = (bf16[4,5,128,128]{3,2,1,0:T(8,128)(2,1)}, bf16[4,5,128,128]{3,2,1,0:T(8,128)(2,1)}, u32[]{:S(2)}, u32[]{:S(2)}) collective-permute-start(bf16[4,5,128,128]{3,2,1,0:T(8,128)(2,1)} %get-tuple-element.59), channel_id=1, source_target_pairs={{0,2},{1,3},{2,0},{3,1},{4,6},{5,7},{6,4},{7,5},{8,10},{9,11},{10,... | collective-permute-start | bytes 1966088 | tf_op jit(solution)/shard_map/ppermute | solution.py:305
  87.4 32.3 %collective-permute-start.9 = (bf16[4,5,128,128]{3,2,1,0:T(8,128)(2,1)}, bf16[4,5,128,128]{3,2,1,0:T(8,128)(2,1)}, u32[]{:S(2)}, u32[]{:S(2)}) collective-permute-start(bf16[4,5,128,128]{3,2,1,0:T(8,128)(2,1)} %get-tuple-element.57), channel_id=1, source_target_pairs={{0,1},{1,0},{2,3},{3,2},{4,5},{5,4},{6,7},{7,6},{8,9},{9,8},{10,11... | collective-permute-start | bytes 1966088 | tf_op jit(solution)/shard_map/ppermute | solution.py:305
  87.5 41.4 %collective-permute-start.20 = (bf16[4,5,128,128]{3,2,1,0:T(8,128)(2,1)}, bf16[4,5,128,128]{3,2,1,0:T(8,128)(2,1)S(1)}, u32[]{:S(2)}, u32[]{:S(2)}) collective-permute-start(bf16[4,5,128,128]{3,2,1,0:T(8,128)(2,1)} %get-tuple-element.72), channel_id=1, source_target_pairs={{0,5},{1,4},{2,7},{3,6},{4,1},{5,0},{6,3},{7,2},{8,13},{9,12},{10,... | collective-permute-start | bytes 1966088 | tf_op jit(solution)/shard_map/ppermute | solution.py:305
  102.3 22.5 %collective-permute-start.19 = (bf16[4,128,128]{2,1,0:T(8,128)(2,1)S(1)}, bf16[4,128,128]{2,1,0:T(8,128)(2,1)S(1)}, u32[]{:S(2)}, u32[]{:S(2)}) collective-permute-start(bf16[4,128,128]{2,1,0:T(8,128)(2,1)S(1)} %get-tuple-element.71), channel_id=1, source_target_pairs={{0,8},{8,0},{1,9},{9,1},{2,10},{10,2},{3,11},{11,3},{4,12},{12,4},... | collective-permute-start | bytes 393224 | tf_op jit(solution)/shard_map/ppermute | solution.py:340
  117.4 7.9 %collective-permute-start.18 = (bf16[4,128,128]{2,1,0:T(8,128)(2,1)S(1)}, bf16[4,128,128]{2,1,0:T(8,128)(2,1)S(1)}, u32[]{:S(2)}, u32[]{:S(2)}) collective-permute-start(bf16[4,128,128]{2,1,0:T(8,128)(2,1)S(1)} %get-tuple-element.70), channel_id=1, source_target_pairs={{0,8},{8,0},{1,9},{9,1},{2,10},{10,2},{3,11},{11,3},{4,12},{12,4},... | collective-permute-start | bytes 393224 | tf_op jit(solution)/shard_map/ppermute | solution.py:340
  119.2 6.2 %collective-permute-start.17 = (bf16[4,128,128]{2,1,0:T(8,128)(2,1)S(1)}, bf16[4,128,128]{2,1,0:T(8,128)(2,1)S(1)}, u32[]{:S(2)}, u32[]{:S(2)}) collective-permute-start(bf16[4,128,128]{2,1,0:T(8,128)(2,1)S(1)} %get-tuple-element.69), channel_id=1, source_target_pairs={{0,8},{8,0},{1,9},{9,1},{2,10},{10,2},{3,11},{11,3},{4,12},{12,4},... | collective-permute-start | bytes 393224 | tf_op jit(solution)/shard_map/ppermute | solution.py:340
  121.5 4.4 %collective-permute-start.16 = (bf16[4,128,128]{2,1,0:T(8,128)(2,1)S(1)}, bf16[4,128,128]{2,1,0:T(8,128)(2,1)S(1)}, u32[]{:S(2)}, u32[]{:S(2)}) collective-permute-start(bf16[4,128,128]{2,1,0:T(8,128)(2,1)S(1)} %get-tuple-element.68), channel_id=1, source_target_pairs={{0,8},{8,0},{1,9},{9,1},{2,10},{10,2},{3,11},{11,3},{4,12},{12,4},... | collective-permute-start | bytes 393224 | tf_op jit(solution)/shard_map/ppermute | solution.py:340
  124.8 1.5 %collective-permute-start.15 = (bf16[4,128,128]{2,1,0:T(8,128)(2,1)S(1)}, bf16[4,128,128]{2,1,0:T(8,128)(2,1)S(1)}, u32[]{:S(2)}, u32[]{:S(2)}) collective-permute-start(bf16[4,128,128]{2,1,0:T(8,128)(2,1)S(1)} %get-tuple-element.67), channel_id=1, source_target_pairs={{0,8},{8,0},{1,9},{9,1},{2,10},{10,2},{3,11},{11,3},{4,12},{12,4},... | collective-permute-start | bytes 393224 | tf_op jit(solution)/shard_map/ppermute | solution.py:340
  125.3 1.3 %collective-permute-start.14 = (bf16[4,128,128]{2,1,0:T(8,128)(2,1)S(1)}, bf16[4,128,128]{2,1,0:T(8,128)(2,1)S(1)}, u32[]{:S(2)}, u32[]{:S(2)}) collective-permute-start(bf16[4,128,128]{2,1,0:T(8,128)(2,1)S(1)} %get-tuple-element.66), channel_id=1, source_target_pairs={{0,8},{8,0},{1,9},{9,1},{2,10},{10,2},{3,11},{11,3},{4,12},{12,4},... | collective-permute-start | bytes 393224 | tf_op jit(solution)/shard_map/ppermute | solution.py:340
  125.4 1.4 %collective-permute-start.13 = (bf16[4,128,128]{2,1,0:T(8,128)(2,1)S(1)}, bf16[4,128,128]{2,1,0:T(8,128)(2,1)S(1)}, u32[]{:S(2)}, u32[]{:S(2)}) collective-permute-start(bf16[4,128,128]{2,1,0:T(8,128)(2,1)S(1)} %get-tuple-element.65), channel_id=1, source_target_pairs={{0,8},{8,0},{1,9},{9,1},{2,10},{10,2},{3,11},{11,3},{4,12},{12,4},... | collective-permute-start | bytes 393224 | tf_op jit(solution)/shard_map/ppermute | solution.py:340
  129.4 1.4 %collective-permute-start.21 = (bf16[4,128,128]{2,1,0:T(8,128)(2,1)S(1)}, bf16[4,128,128]{2,1,0:T(8,128)(2,1)S(1)}, u32[]{:S(2)}, u32[]{:S(2)}) collective-permute-start(bf16[4,128,128]{2,1,0:T(8,128)(2,1)S(1)} %get-tuple-element.75), channel_id=1, source_target_pairs={{0,8},{8,0},{1,9},{9,1},{2,10},{10,2},{3,11},{11,3},{4,12},{12,4},... | collective-permute-start | bytes 393224 | tf_op jit(solution)/shard_map/ppermute | solution.py:340
  (6 other events, 19.7 us)
